TPU v7x, 256 devices: a whole 4x4x8 slice. The times are simulated.
256 devices in a mesh: chan: 8 (over y_lo, x), lat: 32 (over z, y_hi, core).
Axes of the slice: x: 4, y: 4 (y_hi: 2, y_lo: 2; y = y_hi * 2 + y_lo), z: 8, core: 2. Of those that a mesh axis runs over, the one named last changes fastest.
Arguments:
- source_field: bfloat16 [384, 512, 1440], P('chan', 'lat'), may hold values from -6 to 6
- band_start: int32 [512], P('lat'), may hold values from -2 to 2, as said below
- band_width: int32 [512], P('lat'), may hold values from 1 to 4
- band_coef: bfloat16 [512, 4], P('lat'), may hold values from 0.049804688 to 0.59765625
- mixing_weight: bfloat16 [192, 384, 384], P('lat', 'chan'), may hold values from -0.3125 to 0.3125
- output_grad: bfloat16 [384, 512, 1440], P('chan', 'lat'), may hold values from -6 to 6
Outputs:
- mixed_field: bfloat16 [384, 512, 1440], P('chan', 'lat')
- grad_input: bfloat16 [384, 512, 1440], P('chan', 'lat')
- grad_mixing: float32 [192, 384, 384], P('lat', 'chan')
Inputs may be any that keep to these rules, and one draw needn't show every extreme that they name: band_start[i] + band_width[i] <= 3 for every row i.
All inputs are finite; a program needn't handle non-finite values.
Results may differ from a plain program's by a relative error of at most 0.0085.
Values may be sent and summed in bfloat16 or wider, within the bound.
A program may use at most 128 MiB of HBM per device.

v0:
```python
import functools
import math

import jax
import jax.numpy as jnp
import numpy as np
from jax import lax
from jax.experimental import pallas as pl
from jax.experimental.pallas import tpu as pltpu
from jax.sharding import PartitionSpec as P

NLAT = 512
NLON = 1440
MMAX = 192
LMAX = 192
HALO = 2
LAT = 32
CHAN = 8
MODES = MMAX // LAT
ROWS = NLAT // LAT
MESH = pl.DeviceIdType.MESH
VMEM_LIMIT = 48 * 1024 * 1024


def log_norms():
    return np.array(
        [
            0.5
            * (
                math.log((2.0 * m + 1.0) / (4.0 * math.pi))
                + math.lgamma(m + 0.5)
                - math.lgamma(m + 1.0)
                - 0.5 * math.log(math.pi)
            )
            for m in range(MMAX)
        ],
        np.float32,
    )


def fourier_table():
    phase = 2.0 * math.pi / NLON * (np.outer(np.arange(NLON), np.arange(MMAX)) % NLON)
    return np.stack([np.cos(phase), -np.sin(phase)], axis=2).reshape(NLON, MMAX * 2)


def legendre_kernel(order_ref, cosine_ref, sector_ref, out_ref):
    order = jnp.broadcast_to(order_ref[...], (8, NLAT))
    cosine = jnp.broadcast_to(cosine_ref[...], (8, NLAT))
    sector = sector_ref[...]
    order_sq = order * order

    def advance(degree_index, carry):
        previous, earlier = carry
        degree = jnp.full((8, NLAT), degree_index, jnp.int32).astype(jnp.float32)
        lower = degree - 1.0
        scale_a = jnp.sqrt(
            jnp.maximum(4.0 * degree * degree - 1.0, 0.0)
            / jnp.maximum(degree * degree - order_sq, 1.0)
        )
        scale_b = jnp.sqrt(
            jnp.maximum(lower * lower - order_sq, 0.0)
            / jnp.maximum(4.0 * lower * lower - 1.0, 1.0)
        )
        value = scale_a * (cosine * previous - scale_b * earlier)
        value = jnp.where(degree < order, 0.0, jnp.where(degree == order, sector, value))
        out_ref[LMAX - 1 - degree_index] = value
        return value, previous

    zero = sector * 0.0
    lax.fori_loop(0, LMAX, advance, (zero, zero))


def legendre_tables():
    theta = math.pi * (np.arange(NLAT, dtype=np.float64) + 0.5) / NLAT
    cosine = np.cos(theta).astype(np.float32)[None, :]
    sine = np.sin(theta)
    orders = lax.axis_index("lat") * MODES + jnp.arange(8, dtype=jnp.int32)
    norm = jnp.asarray(np.concatenate([log_norms(), np.zeros(2, np.float32)]))
    order = orders.astype(jnp.float32)[:, None]
    own = lax.dynamic_slice(norm, (lax.axis_index("lat") * MODES,), (8,))
    sector = jnp.exp(own[:, None] + order * jnp.asarray(np.log(sine).astype(np.float32))[None, :])
    table = pl.pallas_call(
        legendre_kernel,
        out_shape=jax.ShapeDtypeStruct((LMAX, 8, NLAT), jnp.float32),
        in_specs=[pl.BlockSpec(memory_space=pltpu.VMEM)] * 3,
        out_specs=pl.BlockSpec(memory_space=pltpu.VMEM),
        compiler_params=pltpu.CompilerParams(vmem_limit_bytes=VMEM_LIMIT),
    )(order, jnp.asarray(cosine), sector)
    table = jnp.transpose(table[:, :MODES], (1, 0, 2))
    quadrature = (math.sqrt(NLAT) * math.pi / NLAT * sine).astype(np.float32)
    analysis = (table * jnp.asarray(quadrature)[None, None, :]).astype(jnp.bfloat16)
    synthesis = (table * (1.0 / math.sqrt(LMAX))).astype(jnp.bfloat16)
    return analysis, synthesis


def lat_to(step, lat, chan):
    other = lax.rem(lat + step, LAT)
    return other, chan, other, lat


def spectral_to(step, lat, chan):
    other = lax.rem(lat + step, LAT)
    return other, lax.div(lat, 4), other, lax.rem(lat, 4) * CHAN + chan


def spectral_from(step, lat, chan):
    quarter, group = lax.div(step, CHAN), lax.rem(chan + step, CHAN)
    return chan * 4 + quarter, group, quarter * CHAN + group, lat


def exchange_kernel(sends, receives, spread, *refs):
    if spread is None:
        x_ref, out_ref, send_sem, recv_sem, own_sem = refs
    else:
        x_ref, side_ref, out_ref, side_out_ref = refs[:4]
        send_sem, recv_sem, own_sem, side_send, side_recv, side_own = refs[4:]
    lat, chan = lax.axis_index("lat"), lax.axis_index("chan")
    barrier = pltpu.get_barrier_semaphore()

    def same(pair):
        return (pair[0] == lat) & (pair[1] == chan)

    def greet(step, count):
        source = receives(step, lat, chan)

        @pl.when(jnp.logical_not(same(source)))
        def _():
            pl.semaphore_signal(
                barrier, inc=1, device_id={"lat": source[0], "chan": source[1]},
                device_id_type=MESH,
            )

        return count + jnp.where(same(sends(step, lat, chan)), 0, 1)

    expected = lax.fori_loop(0, LAT, greet, jnp.int32(0))
    if spread is not None:

        def greet_side(step, count):
            pl.semaphore_signal(
                barrier, inc=1, device_id={"lat": lat, "chan": lax.rem(chan + step, CHAN)},
                device_id_type=MESH,
            )
            return count + 1

        expected = lax.fori_loop(1, CHAN, greet_side, expected)
    pl.semaphore_wait(barrier, expected)

    def remote(target):
        return pltpu.make_async_remote_copy(
            src_ref=x_ref.at[target[2]],
            dst_ref=out_ref.at[target[3]],
            send_sem=send_sem.at[target[2]],
            recv_sem=recv_sem.at[target[3]],
            device_id={"lat": target[0], "chan": target[1]},
            device_id_type=MESH,
        )

    def side(step, source):
        other = lax.rem(chan + step, CHAN)
        return pltpu.make_async_remote_copy(
            src_ref=side_ref.at[other] if spread == "parts" else side_ref,
            dst_ref=side_out_ref.at[other if source else chan],
            send_sem=side_send.at[other],
            recv_sem=side_recv.at[other if source else chan],
            device_id={"lat": lat, "chan": other},
            device_id_type=MESH,
        )

    def side_local():
        source = side_ref.at[chan] if spread == "parts" else side_ref
        return pltpu.make_async_copy(source, side_out_ref.at[chan], side_own)

    def start(step, carry):
        target = sends(step, lat, chan)

        @pl.when(same(target))
        def _():
            pltpu.make_async_copy(x_ref.at[target[2]], out_ref.at[target[3]], own_sem).start()

        @pl.when(jnp.logical_not(same(target)))
        def _():
            remote(target).start()

        return carry

    def start_side(step, carry):
        side(step, False).start()
        return carry

    lax.fori_loop(0, LAT, start, 0)
    if spread is not None:
        side_local().start()
        lax.fori_loop(1, CHAN, start_side, 0)

    def finish(step, carry):
        target = sends(step, lat, chan)
        source = receives(step, lat, chan)

        @pl.when(same(target))
        def _():
            pltpu.make_async_copy(x_ref.at[target[2]], out_ref.at[target[3]], own_sem).wait()

        @pl.when(jnp.logical_not(same(target)))
        def _():
            remote(target).wait_send()

        @pl.when(jnp.logical_not(same(source)))
        def _():
            remote((source[0], source[1], source[2], source[2])).wait_recv()

        return carry

    def finish_side(step, carry):
        side(step, False).wait_send()
        side(step, True).wait_recv()
        return carry

    lax.fori_loop(0, LAT, finish, 0)
    if spread is not None:
        side_local().wait()
        lax.fori_loop(1, CHAN, finish_side, 0)


def exchange(x, sends, receives, collective_id, spread=None, extra=None):
    arrays, shapes = [x], [jax.ShapeDtypeStruct(x.shape, x.dtype)]
    scratch = [
        pltpu.SemaphoreType.DMA((LAT,)),
        pltpu.SemaphoreType.DMA((LAT,)),
        pltpu.SemaphoreType.DMA,
    ]
    if spread is not None:
        shape = extra.shape if spread == "parts" else (CHAN,) + extra.shape
        arrays.append(extra)
        shapes.append(jax.ShapeDtypeStruct(shape, extra.dtype))
        scratch += [
            pltpu.SemaphoreType.DMA((CHAN,)),
            pltpu.SemaphoreType.DMA((CHAN,)),
            pltpu.SemaphoreType.DMA,
        ]
    out = pl.pallas_call(
        functools.partial(exchange_kernel, sends, receives, spread),
        out_shape=shapes,
        in_specs=[pl.BlockSpec(memory_space=pl.ANY)] * len(arrays),
        out_specs=[pl.BlockSpec(memory_space=pl.ANY)] * len(arrays),
        scratch_shapes=scratch,
        compiler_params=pltpu.CompilerParams(
            collective_id=collective_id, has_side_effects=True, vmem_limit_bytes=VMEM_LIMIT
        ),
    )(*arrays)
    return out if spread is not None else out[0]


def with_halo(block):
    forward = [(i, i + 1) for i in range(LAT - 1)]
    backward = [(i + 1, i) for i in range(LAT - 1)]
    low = lax.ppermute(block[:, -HALO:], "lat", forward)
    high = lax.ppermute(block[:, :HALO], "lat", backward)
    return jnp.concatenate([low, block, high], axis=1)


def band_matrix(band_start, band_width, band_coef):
    row = jnp.concatenate(
        [
            band_start.astype(jnp.float32)[:, None],
            band_width.astype(jnp.float32)[:, None],
            band_coef.astype(jnp.float32),
        ],
        axis=1,
    )
    rows = lax.all_gather(row, "lat", axis=0, tiled=True)
    start = rows[:, 0:1].astype(jnp.int32)
    width = rows[:, 1:2].astype(jnp.int32)
    target = jnp.arange(NLAT, dtype=jnp.int32)[:, None]
    source = jnp.arange(NLAT, dtype=jnp.int32)[None, :]
    relative = source - target - start
    matrix = jnp.zeros((NLAT, NLAT), jnp.float32)
    for offset in range(4):
        keep = (relative == offset) & (width > offset)
        matrix = matrix + jnp.where(keep, rows[:, 2 + offset : 3 + offset], 0.0)
    return matrix.astype(jnp.bfloat16)


def dot(spec, a, b):
    return jnp.einsum(spec, a, b, preferred_element_type=jnp.float32)


def per_device(source_field, band_start, band_width, band_coef, mixing_weight, output_grad):
    lat = lax.axis_index("lat")
    channels = source_field.shape[0]
    table = fourier_table()
    lon_analysis = jnp.asarray((table / math.sqrt(NLON)).astype(jnp.bfloat16))
    lon_synthesis = jnp.asarray((table / math.sqrt(MMAX)).astype(jnp.bfloat16))

    band = band_matrix(band_start, band_width, band_coef)
    padded_band = jnp.pad(band, HALO)
    band_rows = lax.dynamic_slice(padded_band, (lat * ROWS + HALO, lat * ROWS), (ROWS, ROWS + 4))
    band_cols = lax.dynamic_slice(padded_band, (lat * ROWS, lat * ROWS + HALO), (ROWS + 4, ROWS))

    analysis, synthesis = legendre_tables()
    banded = dot("mli,ij->mlj", analysis, band).astype(jnp.bfloat16)

    panels = jnp.stack(
        [
            dot("cin,nk->cik", source_field, lon_analysis).astype(jnp.bfloat16),
            dot("cin,nk->cik", output_grad, lon_synthesis).astype(jnp.bfloat16),
        ]
    )
    panels = panels.reshape(2, channels, ROWS, LAT, 3, 2, 2)
    panels = jnp.transpose(panels, (3, 4, 2, 5, 0, 6, 1)).reshape(LAT, 3, ROWS, 8 * channels)
    columns, weight = exchange(
        panels, lat_to, lambda k, a, b: lat_to(LAT - k, a, b), 1, "whole", mixing_weight
    )
    weight = jnp.transpose(weight, (1, 0, 2, 3)).reshape(6, CHAN * channels, CHAN * channels)

    columns = columns.reshape(LAT, 3, ROWS, 2, 2, 2, channels)
    columns = jnp.transpose(columns, (4, 1, 3, 0, 2, 5, 6)).reshape(2, MODES, NLAT, 2 * channels)
    spectral = jnp.stack(
        [
            dot("mlj,mjk->mlk", banded, columns[0]).astype(jnp.bfloat16),
            dot("mlj,mjk->mlk", synthesis, columns[1]).astype(jnp.bfloat16),
        ]
    )
    message = jnp.transpose(
        spectral.reshape(2, MODES, LAT, 6, 2 * channels), (2, 0, 1, 3, 4)
    ).reshape(LAT, 54, 128)
    message = jnp.pad(message, ((0, 0), (0, 10), (0, 0)))

    def backwards(step, a, b):
        other = spectral_from(step, a, b)
        return other

    received = exchange(message, spectral_to, backwards, 2)
    received = received[:, :54].reshape(4, CHAN, 2, MODES, 6, 2, channels)
    received = jnp.transpose(received, (2, 4, 0, 3, 5, 1, 6)).reshape(2, 6, 48, CHAN * channels)
    coefficients, back_mixed = received[0], received[1]
    grad = dot("lkc,lko->lco", coefficients, back_mixed).astype(jnp.bfloat16)
    grad = jnp.transpose(grad.reshape(6, CHAN, channels, CHAN * channels), (1, 0, 2, 3))
    mixed = dot("lkc,lco->lko", coefficients, weight).astype(jnp.bfloat16)
    back_coef = dot("lko,lco->lkc", back_mixed, weight).astype(jnp.bfloat16)
    reply = jnp.stack([mixed, back_coef]).reshape(2, 6, 4, MODES, 2, CHAN, channels)
    reply = jnp.transpose(reply, (2, 5, 0, 3, 1, 4, 6)).reshape(LAT, 54, 128)
    reply = jnp.pad(reply, ((0, 0), (0, 10), (0, 0)))

    def replies(step, a, b):
        other = lax.rem(a + step, LAT)
        return other, lax.div(a, 4), other, 0

    answers = exchange(reply, spectral_from, replies, 3)
    answers = answers[:, :54].reshape(LAT, 2, MODES, 6, 2 * channels)
    answers = jnp.transpose(answers, (1, 2, 0, 3, 4)).reshape(2, MODES, LMAX, 2 * channels)
    grids = jnp.stack(
        [
            dot("mlj,mlk->mjk", synthesis, answers[0]).astype(jnp.bfloat16),
            dot("mlj,mlk->mjk", banded, answers[1]).astype(jnp.bfloat16),
        ]
    )
    grids = grids.reshape(2, 3, 2, LAT, ROWS, 2, channels)
    grids = jnp.transpose(grids, (3, 1, 4, 2, 0, 5, 6)).reshape(LAT, 3, ROWS, 8 * channels)
    grids, grad_parts = exchange(
        grids, lat_to, lambda k, a, b: lat_to(LAT - k, a, b), 4, "parts", grad
    )
    grad_mixing = jnp.sum(grad_parts.astype(jnp.float32), axis=0)
    grids = grids.reshape(LAT, 3, ROWS, 2, 2, 2, channels)
    grids = jnp.transpose(grids, (4, 6, 2, 0, 1, 3, 5)).reshape(2, channels, ROWS, 2 * MMAX)

    mixed_field = dot("cik,nk->cin", grids[0], lon_synthesis) + dot(
        "ij,cjn->cin", band_rows, with_halo(source_field)
    )
    grad_input = dot("cik,nk->cin", grids[1], lon_analysis) + dot(
        "ji,cjn->cin", band_cols, with_halo(output_grad)
    )
    return (mixed_field.astype(jnp.bfloat16), grad_input.astype(jnp.bfloat16), grad_mixing)


def solution(mesh):
    in_specs = (
        P("chan", "lat", None),
        P("lat"),
        P("lat"),
        P("lat", None),
        P("lat", "chan", None),
        P("chan", "lat", None),
    )
    out_specs = (P("chan", "lat", None), P("chan", "lat", None), P("lat", "chan", None))
    return jax.shard_map(
        per_device, mesh=mesh, in_specs=in_specs, out_specs=out_specs, check_vma=False
    )
```

profile of v0, /device:TPU:1, one launch (start us, length us, event | category | flops | bytes accessed | tf_op | source)
XLA Modules:
  0.0 376.4 jit_solution(3435080937908607595)
XLA Ops:
  0.7 3.0 fusion.51
  3.7 6.2 %collective-permute-start = (bf16[48,2,1440]{2,1,0:T(2,128)(2,1)}, bf16[48,2,1440]{2,1,0:T(2,128)(2,1)}, u32[]{:S(2)}, u32[]{:S(2)}) collective-permute-start(bf16[48,2,1440]{2,1,0:T(2,128)(2,1)} %get-tuple-element.23), channel_id=1, source_target_pairs={{0,1},{1,2},{2,3},{3,4},{4,5},{5,6},{6,7},{7,8},{8,9},{9,10},{10,1... | collective-permute-start | bytes 829448 | tf_op jit(solution)/shard_map/ppermute | solution.py:256
  9.9 1.9 collective-permute-start.1
  11.8 2.9 fusion.50
  14.7 5.1 %collective-permute-start.2 = (bf16[48,2,1440]{2,1,0:T(2,128)(2,1)}, bf16[48,2,1440]{2,1,0:T(2,128)(2,1)}, u32[]{:S(2)}, u32[]{:S(2)}) collective-permute-start(bf16[48,2,1440]{2,1,0:T(2,128)(2,1)} %get-tuple-element.21), channel_id=1, source_target_pairs={{0,1},{1,2},{2,3},{3,4},{4,5},{5,6},{6,7},{7,8},{8,9},{9,10},{10,1... | collective-permute-start | bytes 829448 | tf_op jit(solution)/shard_map/ppermute | solution.py:256
  19.9 1.9 collective-permute-start.3
  21.9 45.5 %all-gather = f32[32,16,6]{1,2,0:T(8,128)S(1)} all-gather(f32[1,16,6]{1,2,0:T(8,128)S(1)} %maximum_bitcast_fusion.4), channel_id=1, replica_groups=mesh['chan'=8,'lat'=32] {'lat'}, dimensions={0}, use_global_device_ids=true | all-gather | bytes 12672 | tf_op jit(solution)/shard_map/all_gather | solution.py:270
  67.7 4.1 %fusion.27 = bf16[48,16,384]{2,0,1:T(8,128)(2,1)} fusion(bf16[1440,384,1]{1,0,2:T(8,128)(2,1)S(1)} %copy-done.9, bf16[48,16,1440]{2,1,0:T(8,128)(2,1)} %param.12), kind=kOutput, calls=%fused_computation.35 | convolution fusion | flops 849641472 | bytes 3907584 | tf_op jit(solution)/shard_map/cin,nk->cik/dot_general | solution.py:284
  71.8 1.5 fusion.24
  73.3 1.4 copy.72
  74.7 2.1 copy.70
  76.9 0.7 maximum_bitcast_fusion
  77.6 5.1 %copy.73 = bf16[32,3,16,2,2,2,48]{6,5,4,3,2,1,0:T(2,128)(2,1)} copy(bf16[32,3,16,2,2,2,48]{6,2,5,3,1,0,4:T(8,128)(2,1)S(1)} %maximum_bitcast_fusion) | data formatting | bytes 2359296 | tf_op jit(solution)/shard_map/transpose | solution.py:309
  82.7 9.6 %reshape.90.refs_0_ = bf16[32,3,16,384]{3,2,1,0:T(8,128)(2,1)S(1)} reshape(bf16[32,3,16,2,2,2,48]{6,5,4,3,2,1,0:T(2,128)(2,1)} %copy.73) | data formatting | bytes 2359296 | tf_op jit(solution)/shard_map/reshape | solution.py:309
  92.4 41.4 %shard_map.140 = (bf16[32,3,16,384]{3,2,1,0:T(8,128)(2,1)S(1)}, bf16[8,6,48,384]{3,2,1,0:T(8,128)(2,1)S(1)}) custom-call(bf16[32,3,16,384]{3,2,1,0:T(8,128)(2,1)S(1)} %reshape.90.refs_0_, bf16[6,48,384]{2,1,0:T(8,128)(2,1)S(1)} %copy-done.1), custom_call_target="tpu_custom_call" | custom-call | tf_op jit(solution)/shard_map/pallas_call | solution.py:240
  133.8 1.4 copy.80
  135.2 3.8 %reshape.91 = bf16[32,3,16,2,2,2,48]{6,5,4,3,2,1,0:T(2,128)(2,1)} reshape(bf16[32,3,16,384]{3,2,1,0:T(8,128)(2,1)S(1)} %get-tuple-element.7) | data formatting | bytes 2359296 | tf_op jit(solution)/shard_map/reshape | solution.py:315
  139.0 4.6 %copy.125 = bf16[32,3,16,2,2,2,48]{6,5,2,0,3,1,4:T(2,128)(2,1)S(1)} copy(bf16[32,3,16,2,2,2,48]{6,5,4,3,2,1,0:T(2,128)(2,1)} %reshape.91) | data formatting | bytes 2359296 | tf_op jit(solution)/shard_map/reshape | solution.py:315
  143.5 3.1 fusion.49
  146.6 1.5 squeeze.24
  148.1 0.7 squeeze.25
  149.1 5.6 %shard_map.139 = f32[192,8,512]{2,1,0:T(8,128)S(1)} custom-call(f32[8,1]{1,0:T(8,128)S(1)} %add_convert_fusion.1.order_ref, f32[1,512]{1,0:T(1,128)S(1)} %copy-done.2, f32[8,512]{1,0:T(8,128)S(1)} %add_exponential_fusion.sector_ref), custom_call_target="tpu_custom_call" | custom-call | tf_op jit(solution)/shard_map/pallas_call | solution.py:82
  154.7 0.5 fusion.16
  155.3 1.7 convolution_convert_fusion.1
  157.0 1.0 copy-done.4
  158.7 0.8 convolution_convert_fusion.4
  160.0 1.0 reshape.92
  161.1 17.7 %shard_map.141 = bf16[32,64,128]{2,1,0:T(8,128)(2,1)S(1)} custom-call(bf16[32,64,128]{2,1,0:T(8,128)(2,1)S(1)} %pad.11.refs_0_), custom_call_target="tpu_custom_call" | custom-call | tf_op jit(solution)/shard_map/pallas_call | solution.py:240
  178.8 1.0 reshape.93
  179.9 0.8 fusion.52
  182.6 0.7 convolution_convert_fusion.6
  183.3 0.7 convolution_convert_fusion
  183.9 0.5 stack.42
  184.4 0.5 copy.82
  184.9 0.5 stack.43
  185.4 0.5 copy.83
  185.9 1.9 maximum_bitcast_fusion.2
  187.7 1.7 reshape.95
  189.6 56.0 %shard_map.142 = bf16[32,64,128]{2,1,0:T(8,128)(2,1)S(1)} custom-call(bf16[32,64,128]{2,1,0:T(8,128)(2,1)S(1)} %pad.12.refs_0_), custom_call_target="tpu_custom_call" | custom-call | tf_op jit(solution)/shard_map/pallas_call | solution.py:240
  245.6 0.8 reshape.96
  246.8 3.1 convolution_convert_fusion.3
  249.9 2.3 copy.87
  252.2 0.8 copy.88
  253.0 1.9 squeeze.29
  254.9 1.3 convolution_convert_fusion.2
  256.2 1.2 copy.90
  257.4 3.2 stack.46
  260.6 3.9 %stack.45 = bf16[1,3,2,32,16,2,48]{6,5,4,3,2,1,0:T(2,128)(2,1)} reshape(bf16[6,512,96]{2,1,0:T(8,128)(2,1)} %copy.87) | data formatting | bytes 1179648 | tf_op jit(solution)/shard_map/stack | solution.py:351
  264.5 6.7 %maximum_bitcast_fusion.1 = bf16[32,3,16,2,2,2,48]{6,5,2,0,3,1,4:T(2,128)(2,1)S(1)} fusion(bf16[1,3,2,32,16,2,48]{6,5,4,3,2,1,0:T(2,128)(2,1)S(1)} %stack.46, bf16[1,3,2,32,16,2,48]{6,5,4,3,2,1,0:T(2,128)(2,1)} %stack.45), kind=kLoop, calls=%fused_computation.16 | loop fusion | flops 589824 | bytes 2359296 | tf_op jit(solution)/shard_map/transpose | solution.py:358
  271.2 5.2 %copy.91 = bf16[32,3,16,2,2,2,48]{6,5,4,3,2,1,0:T(2,128)(2,1)} copy(bf16[32,3,16,2,2,2,48]{6,5,2,0,3,1,4:T(2,128)(2,1)S(1)} %maximum_bitcast_fusion.1) | data formatting | bytes 2359296 | tf_op jit(solution)/shard_map/transpose | solution.py:358
  276.3 9.6 %reshape.97.refs_0_ = bf16[32,3,16,384]{3,2,1,0:T(8,128)(2,1)S(1)} reshape(bf16[32,3,16,2,2,2,48]{6,5,4,3,2,1,0:T(2,128)(2,1)} %copy.91) | data formatting | bytes 2359296 | tf_op jit(solution)/shard_map/reshape | solution.py:358
  286.1 44.8 %shard_map.143 = (bf16[32,3,16,384]{3,2,1,0:T(8,128)(2,1)S(1)}, bf16[8,6,48,384]{3,2,1,0:T(8,128)(2,1)S(1)}) custom-call(bf16[32,3,16,384]{3,2,1,0:T(8,128)(2,1)S(1)} %reshape.97.refs_0_, bf16[8,6,48,384]{3,2,1,0:T(8,128)(2,1)S(1)} %bitcast.92), custom_call_target="tpu_custom_call" | custom-call | tf_op jit(solution)/shard_map/pallas_call | solution.py:240
  330.9 1.0 copy-done
  331.9 12.5 %reshape.99 = bf16[32,3,16,2,2,2,48]{6,5,4,3,2,1,0:T(2,128)(2,1)} reshape(bf16[32,3,16,384]{3,2,1,0:T(8,128)(2,1)} %copy-done) | data formatting | bytes 2359296 | tf_op jit(solution)/shard_map/reshape | solution.py:363
  344.5 2.9 copy.124
  347.4 1.9 fusion.48
  349.3 3.0 copy.95
  352.3 2.0 copy.94
  354.2 5.2 %fusion.54 = f32[48,16,1440]{2,1,0:T(8,128)} fusion(bf16[48,16,384]{2,1,0:T(8,128)(2,1)} %copy.94, bf16[1440,384,1]{1,0,2:T(8,128)(2,1)} %constant.65), kind=kOutput, calls=%fused_computation.82 | convolution fusion | flops 849346560 | bytes 6119424 | tf_op jit(solution)/shard_map/cik,nk->cin/dot_general | solution.py:284
  359.4 3.6 fusion.55
  363.0 1.0 convert_reduce_fusion
  364.0 1.2 add_convert_fusion
  365.2 6.5 %fusion.1 = bf16[48,16,1440]{2,1,0:T(8,128)(2,1)} fusion(f32[48,16,1440]{2,1,0:T(8,128)} %fusion.54, bf16[48,2,1440]{2,1,0:T(2,128)(2,1)} %collective-permute-done.1, bf16[48,16,1440]{2,1,0:T(8,128)(2,1)} %param.12, bf16[48,2,1440]{2,1,0:T(2,128)(2,1)} %collective-permute-done, s32[]{:T(128)S(6)} %select_n.29, s32[]{:T(128)S(6)} %select_n.30, ...), kind=kOutput, calls=%fused_computation.3 | convolution fusion | flops 54743040 | bytes 9924616 | tf_op jit(solution)/shard_map/ij,cjn->cin/dot_general | solution.py:284
  371.8 4.4 %fusion = bf16[48,16,1440]{2,1,0:T(8,128)(2,1)} fusion(f32[48,16,1440]{2,1,0:T(8,128)S(1)} %bitcast.104, bf16[48,2,1440]{2,1,0:T(2,128)(2,1)} %collective-permute-done.3, bf16[48,16,1440]{2,1,0:T(8,128)(2,1)S(1)} %copy-done.13, bf16[48,2,1440]{2,1,0:T(2,128)(2,1)} %collective-permute-done.2, s32[]{:T(128)S(6)} %select_n.30, s32[]{:T(128)S(6)} %select_n.29, ...), kind=kOutput, calls=%fused_computation.1 | convolution fusion | flops 54743040 | bytes 9924616 | tf_op jit(solution)/shard_map/ji,cjn->cin/dot_general | solution.py:284
  (96 shorter events, 4.2 us)
Async XLA Ops:
  0.6 67.0 %copy-start.9 = (bf16[1440,384,1]{1,0,2:T(8,128)(2,1)S(1)}, bf16[1440,384,1]{1,0,2:T(8,128)(2,1)}, u32[]{:S(2)}) copy-start(bf16[1440,384,1]{1,0,2:T(8,128)(2,1)} %constant.64) | copy-start | bytes 3317764
  0.6 21.2 %copy-start.26 = (bf16[16,4]{0,1:T(4,128)(2,1)S(1)}, bf16[16,4]{0,1:T(4,128)(2,1)}, u32[]{:S(2)}) copy-start(bf16[16,4]{0,1:T(4,128)(2,1)} %param.15) | copy-start | bytes 388
  0.7 21.2 %copy-start.27 = (s32[16]{0:T(128)S(1)}, s32[16]{0:T(128)}, u32[]{:S(2)}) copy-start(s32[16]{0:T(128)} %param.14) | copy-start | bytes 196
  0.7 21.2 %copy-start.28 = (s32[16]{0:T(128)S(1)}, s32[16]{0:T(128)}, u32[]{:S(2)}) copy-start(s32[16]{0:T(128)} %param.13) | copy-start | bytes 196
  3.7 361.5 %collective-permute-start = (bf16[48,2,1440]{2,1,0:T(2,128)(2,1)}, bf16[48,2,1440]{2,1,0:T(2,128)(2,1)}, u32[]{:S(2)}, u32[]{:S(2)}) collective-permute-start(bf16[48,2,1440]{2,1,0:T(2,128)(2,1)} %get-tuple-element.23), channel_id=1, source_target_pairs={{0,1},{1,2},{2,3},{3,4},{4,5},{5,6},{6,7},{7,8},{8,9},{9,10},{10,1... | collective-permute-start | bytes 829448 | tf_op jit(solution)/shard_map/ppermute | solution.py:256
  9.9 355.3 %collective-permute-start.1 = (bf16[48,2,1440]{2,1,0:T(2,128)(2,1)}, bf16[48,2,1440]{2,1,0:T(2,128)(2,1)}, u32[]{:S(2)}, u32[]{:S(2)}) collective-permute-start(bf16[48,2,1440]{2,1,0:T(2,128)(2,1)} %get-tuple-element.24), channel_id=1, source_target_pairs={{1,0},{2,1},{3,2},{4,3},{5,4},{6,5},{7,6},{8,7},{9,8},{10,9},{11,1... | collective-permute-start | bytes 829448 | tf_op jit(solution)/shard_map/ppermute | solution.py:257
  14.7 357.0 %collective-permute-start.2 = (bf16[48,2,1440]{2,1,0:T(2,128)(2,1)}, bf16[48,2,1440]{2,1,0:T(2,128)(2,1)}, u32[]{:S(2)}, u32[]{:S(2)}) collective-permute-start(bf16[48,2,1440]{2,1,0:T(2,128)(2,1)} %get-tuple-element.21), channel_id=1, source_target_pairs={{0,1},{1,2},{2,3},{3,4},{4,5},{5,6},{6,7},{7,8},{8,9},{9,10},{10,1... | collective-permute-start | bytes 829448 | tf_op jit(solution)/shard_map/ppermute | solution.py:256
  19.9 351.8 %collective-permute-start.3 = (bf16[48,2,1440]{2,1,0:T(2,128)(2,1)}, bf16[48,2,1440]{2,1,0:T(2,128)(2,1)}, u32[]{:S(2)}, u32[]{:S(2)}) collective-permute-start(bf16[48,2,1440]{2,1,0:T(2,128)(2,1)} %get-tuple-element.22), channel_id=1, source_target_pairs={{1,0},{2,1},{3,2},{4,3},{5,4},{6,5},{7,6},{8,7},{9,8},{10,9},{11,1... | collective-permute-start | bytes 829448 | tf_op jit(solution)/shard_map/ppermute | solution.py:257
  67.6 87.7 %copy-start.18 = (pred[512]{0:T(512)(128)(4,1)}, pred[512]{0:T(512)(128)(4,1)S(1)}, u32[]{:S(2)}) copy-start(pred[512]{0:T(512)(128)(4,1)S(1)} %get-tuple-element.11) | copy-start | bytes 1540
  67.6 87.7 %copy-start.20 = (pred[512]{0:T(512)(128)(4,1)}, pred[512]{0:T(512)(128)(4,1)S(1)}, u32[]{:S(2)}) copy-start(pred[512]{0:T(512)(128)(4,1)S(1)} %get-tuple-element.12) | copy-start | bytes 1540
  67.6 87.7 %copy-start.22 = (pred[512]{0:T(512)(128)(4,1)}, pred[512]{0:T(512)(128)(4,1)S(1)}, u32[]{:S(2)}) copy-start(pred[512]{0:T(512)(128)(4,1)S(1)} %get-tuple-element.13) | copy-start | bytes 1540
  67.6 87.7 %copy-start.24 = (pred[512]{0:T(512)(128)(4,1)}, pred[512]{0:T(512)(128)(4,1)S(1)}, u32[]{:S(2)}) copy-start(pred[512]{0:T(512)(128)(4,1)S(1)} %get-tuple-element.14) | copy-start | bytes 1540
  67.6 87.7 %copy-start.14 = (f32[512,1]{0,1:T(1,128)}, f32[512,1]{0,1:T(1,128)S(1)}, u32[]{:S(2)}) copy-start(f32[512,1]{0,1:T(1,128)S(1)} %get-tuple-element.33) | copy-start | bytes 6148
  67.6 4.2 %copy-start.11 = (bf16[1440,384,1]{1,0,2:T(8,128)(2,1)S(1)}, bf16[1440,384,1]{1,0,2:T(8,128)(2,1)}, u32[]{:S(2)}) copy-start(bf16[1440,384,1]{1,0,2:T(8,128)(2,1)} %constant.65) | copy-start | bytes 3317764
  67.6 4.1 %copy-start.12 = (bf16[48,16,1440]{2,1,0:T(8,128)(2,1)S(1)}, bf16[48,16,1440]{2,1,0:T(8,128)(2,1)}, u32[]{:S(2)}) copy-start(bf16[48,16,1440]{2,1,0:T(8,128)(2,1)} %param.17) | copy-start | bytes 6635524
  82.7 9.7 %copy-start.1 = (bf16[6,48,384]{2,1,0:T(8,128)(2,1)S(1)}, bf16[6,48,384]{2,1,0:T(8,128)(2,1)}, u32[]{:S(2)}) copy-start(bf16[6,48,384]{2,1,0:T(8,128)(2,1)} %refs_1_.1) | copy-start | bytes 663556
  148.1 0.8 copy-start.29
  148.1 0.8 copy-start.17
  148.1 0.9 copy-start.2
  148.9 5.8 %copy-start.16 = (f32[512]{0:T(512)S(1)}, f32[512]{0:T(512)}, u32[]{:S(2)}) copy-start(f32[512]{0:T(512)} %constant.51.clone) | copy-start | bytes 6148
  155.2 3.5 copy-start.8
  155.3 2.8 copy-start.6
  157.0 1.0 copy-start.4
  180.7 1.5 copy-start.3
  249.9 5.0 %copy-start.5 = (bf16[6,192,512]{2,1,0:T(8,128)(2,1)S(1)}, bf16[6,192,512]{2,1,0:T(8,128)(2,1)}, u32[]{:S(2)}) copy-start(bf16[6,192,512]{2,1,0:T(8,128)(2,1)} %copy-done.4) | copy-start | bytes 3538948
  330.9 1.0 copy-start
  354.2 5.2 %copy-start.7 = (bf16[48,16,384]{2,1,0:T(8,128)(2,1)S(1)}, bf16[48,16,384]{2,1,0:T(8,128)(2,1)}, u32[]{:S(2)}) copy-start(bf16[48,16,384]{2,1,0:T(8,128)(2,1)} %copy.95) | copy-start | bytes 1769476
  354.2 5.2 %copy-start.10 = (bf16[1440,384,1]{1,0,2:T(8,128)(2,1)S(1)}, bf16[1440,384,1]{1,0,2:T(8,128)(2,1)}, u32[]{:S(2)}) copy-start(bf16[1440,384,1]{1,0,2:T(8,128)(2,1)} %constant.64) | copy-start | bytes 3317764
  363.0 1.0 copy-start.15
  363.0 1.0 copy-start.19
  363.0 1.0 copy-start.21
  363.0 1.0 copy-start.23
  363.0 1.0 copy-start.25
  364.0 7.7 %slice-start = ((s8[4718592]{0:T(1024)(128)(4,1)}), s8[4194304]{0:T(1024)(128)(4,1)S(1)}, s32[]{:S(2)}) async-start(s8[4718592]{0:T(1024)(128)(4,1)} %bitcast.103), calls=%async_computation | async-start | bytes 8388608
  365.2 6.6 %slice-start.1 = ((s8[4718592]{0:T(1024)(128)(4,1)}), s8[524288]{0:T(1024)(128)(4,1)S(1)}, s32[]{:S(2)}) async-start(s8[4718592]{0:T(1024)(128)(4,1)} %bitcast.103), calls=%async_computation.1 | async-start | bytes 1048576
  365.2 6.6 %copy-start.13 = (bf16[48,16,1440]{2,1,0:T(8,128)(2,1)S(1)}, bf16[48,16,1440]{2,1,0:T(8,128)(2,1)}, u32[]{:S(2)}) copy-start(bf16[48,16,1440]{2,1,0:T(8,128)(2,1)} %param.17) | copy-start | bytes 6635524
where the time goes:
time: 381 us; the launch traced here: 376 us
  Pallas kernels  165 us (43%)
  local copies, waits for them, and re-layouts  102 us (27%)
  blocking collectives  45.5 us (12%)
  matrix products  34.3 us (9%)
  starting transfers between devices  15.2 us (4%)
  other arithmetic  12.3 us (3%)
    pallas_call x4, Pallas kernels, exchange(): pl.pallas_call(functools.partial(exchange_kernel, sends, receives, spread...  160 us
    all_gather x1, blocking collectives, band_matrix(): rows = lax.all_gather(row, 'lat', axis=0, tiled=True)  45.5 us
    dot_general x14, matrix products, dot(): return jnp.einsum(spec, a, b, preferred_element_type=jnp.float32)  34.3 us
    reshape x2, local copies, waits for them, and re-layouts, per_device(): grids = grids.reshape(LAT, 3, ROWS, 2, 2, 2, channels)  15.4 us
    ppermute x2, starting transfers between devices, with_halo(): low = lax.ppermute(block[:, -HALO:], 'lat', forward)  11.3 us
    reshape x1, local copies, waits for them, and re-layouts, per_device(): jnp.transpose(panels, (3, 4, 2, 5, 0, 6, 1))  9.64 us
    reshape x1, local copies, waits for them, and re-layouts, per_device(): jnp.transpose(grids, (3, 1, 4, 2, 0, 5, 6))  9.6 us
    reshape x2, local copies, waits for them, and re-layouts, per_device(): columns = columns.reshape(LAT, 3, ROWS, 2, 2, 2, channels)  8.37 us
  transfers between devices with their start and end apart: 4, of which 0 were waited for; matrix products, arithmetic and copies ran while one was open for 37% of the time, Pallas kernels for 44%

commit v1 on v0

--- a/solution.py
+++ b/solution.py
@@ -40,14 +40,132 @@
 
 def fourier_table():
     phase = 2.0 * math.pi / NLON * (np.outer(np.arange(NLON), np.arange(MMAX)) % NLON)
-    return np.stack([np.cos(phase), -np.sin(phase)], axis=2).reshape(NLON, MMAX * 2)
-
-
-def legendre_kernel(order_ref, cosine_ref, sector_ref, out_ref):
+    table = np.zeros((NLON, 2, 256))
+    table[:, 0, :MMAX] = np.cos(phase)
+    table[:, 1, :MMAX] = -np.sin(phase)
+    return table.reshape(NLON, 512)
+
+
+def dense(a, b, dims=((1,), (0,))):
+    return lax.dot_general(a, b, (dims, ((), ())), preferred_element_type=jnp.float32)
+
+
+def iota(shape, axis):
+    return lax.broadcasted_iota(jnp.int32, shape, axis)
+
+
+def merge_lanes(a, b, c, d):
+    lane = iota(a.shape, 1)
+    return (
+        jnp.where(lane < 96, a, b),
+        jnp.where(lane < 64, b, c),
+        jnp.where(lane < 32, c, d),
+    )
+
+
+def split_lanes(tiles):
+    lane = iota(tiles[0].shape, 1)
+    units = []
+    for g in range(0, 9, 3):
+        t0, t1, t2 = tiles[g : g + 3]
+        units += [t0, jnp.where(lane < 64, t1, t0), jnp.where(lane < 32, t2, t1), t2]
+    return units
+
+
+def merge_rows(tiles):
+    row = iota(tiles[0].shape, 0) % 8
+    out = list(tiles[:8])
+    for k in range(3):
+        out[k] = jnp.where(row < 6, tiles[k], pltpu.roll(tiles[8], 6 - 2 * k, 0))
+    return out
+
+
+def split_rows(tiles):
+    rows = tiles[0].shape[0]
+    row = iota(tiles[0].shape, 0) % 8
+    back = [pltpu.roll(tiles[k], rows - (6 - 2 * k), 0) for k in range(3)]
+    return list(tiles) + [jnp.where(row < 2, back[0], jnp.where(row < 4, back[1], back[2]))]
+
+
+def store_rows(out_ref, tiles):
+    for p in range(4):
+        pair = [tiles[2 * p + k].reshape(LAT, 8, 128) for k in range(2)]
+        out_ref[:, 16 * p : 16 * p + 16, :] = jnp.concatenate(pair, axis=1).astype(jnp.bfloat16)
+
+
+def load_rows(in_ref):
+    tiles = []
+    for p in range(4):
+        pair = in_ref[:, 16 * p : 16 * p + 16, :].astype(jnp.float32)
+        tiles += [pair[:, :8].reshape(256, 128), pair[:, 8:].reshape(256, 128)]
+    return tiles
+
+
+def spread_kernel(source_ref, grad_ref, band_ref, out_ref, part, rows):
+    for f, ref in ((0, source_ref), (1, grad_ref)):
+        for k in range(4):
+            part[k] = ref[:, 128 * k : 128 * k + 128].astype(jnp.float32)
+
+        def turn(i, carry):
+            for half, count in ((0, 128), (1, 64)):
+                a = part[half, pl.ds(i, 48, stride=16), :]
+                b = part[2 + half, pl.ds(i, 48, stride=16), :]
+                block = jnp.concatenate([a, b, a[:32]], axis=0).T
+                rows[f, pl.ds(half * 2048 + i, count, stride=16), :] = block[:count]
+            return carry
+
+        lax.fori_loop(0, ROWS, turn, 0)
+
+    def send(d, carry):
+        units = [
+            rows[f, pl.ds(pl.multiple_of((d * 6 + m) * 16, 16), 16), :]
+            for f in range(2)
+            for m in range(MODES)
+        ]
+        for g in range(3):
+            a, b, c, e = units[4 * g : 4 * g + 4]
+            tiles = merge_lanes(a, pltpu.roll(b, 96, 1), pltpu.roll(c, 64, 1), pltpu.roll(e, 32, 1))
+            for k in range(3):
+                out_ref[d, 3 * g + k] = tiles[k].astype(jnp.bfloat16)
+        out_ref[d, 9] = band_ref[...]
+        return carry
+
+    lax.fori_loop(0, LAT, send, 0)
+
+
+def gather_kernel(in_ref, source_ref, grad_ref, part, rows):
+    def receive(d, carry):
+        tiles = [in_ref[d, k].astype(jnp.float32) for k in range(9)]
+        units = split_lanes(tiles)
+        for u in range(12):
+            if u % 4:
+                units[u] = pltpu.roll(units[u], 32 * (u % 4), 1)
+            rows[u // 6, pl.ds(pl.multiple_of((d * 6 + u % 6) * 16, 16), 16), :] = units[u]
+        return carry
+
+    lax.fori_loop(0, LAT, receive, 0)
+    for f, ref in ((0, source_ref), (1, grad_ref)):
+
+        def turn(i, carry):
+            block = rows[f, pl.ds(i, MMAX, stride=16), :]
+            halves = (block[:128], jnp.concatenate([block[128:], jnp.zeros((64, 128), jnp.float32)], axis=0))
+            for half in range(2):
+                flat = halves[half].T
+                part[half, pl.ds(i, 48, stride=16), :] = flat[:48]
+                part[2 + half, pl.ds(i, 48, stride=16), :] = flat[48:96]
+            return carry
+
+        lax.fori_loop(0, ROWS, turn, 0)
+        for k in range(4):
+            ref[:, 128 * k : 128 * k + 128] = part[k].astype(jnp.bfloat16)
+
+
+def table_kernel(order_ref, cosine_ref, sector_ref, quad_ref, band_ref, near_ref, far_ref, table):
     order = jnp.broadcast_to(order_ref[...], (8, NLAT))
     cosine = jnp.broadcast_to(cosine_ref[...], (8, NLAT))
     sector = sector_ref[...]
     order_sq = order * order
+    table[...] = jnp.zeros_like(table)
 
     def advance(degree_index, carry):
         previous, earlier = carry
@@ -63,14 +181,119 @@
         )
         value = scale_a * (cosine * previous - scale_b * earlier)
         value = jnp.where(degree < order, 0.0, jnp.where(degree == order, sector, value))
-        out_ref[LMAX - 1 - degree_index] = value
+        place = LMAX - 1 - degree_index
+        row = place // 6 * 8 + place % 6
+        for k in range(4):
+            table[k, pl.ds(row, 8, stride=256), :] = value[:, 128 * k : 128 * k + 128]
         return value, previous
 
     zero = sector * 0.0
     lax.fori_loop(0, LMAX, advance, (zero, zero))
 
-
-def legendre_tables():
+    info = band_ref[...].reshape(NLAT, 128).astype(jnp.float32)
+    relative = (iota((NLAT, NLAT), 1) - iota((NLAT, NLAT), 0)).astype(jnp.float32) - info[:, 0:1]
+    band = jnp.zeros((NLAT, NLAT), jnp.float32)
+    for k in range(4):
+        keep = (relative == float(k)) & (info[:, 1:2] > float(k))
+        band = band + jnp.where(keep, info[:, 2 + k : 3 + k], 0.0)
+    band = band.astype(jnp.bfloat16)
+    for m in range(MODES):
+        own = jnp.concatenate([table[k, 256 * m : 256 * m + 256, :] for k in range(4)], axis=1)
+        analysis = (own * quad_ref[...]).astype(jnp.bfloat16)
+        banded = dense(analysis, band)
+        synthesis = own * (1.0 / math.sqrt(LMAX))
+        near_ref[m] = banded.astype(jnp.bfloat16)
+        near_ref[MODES + m] = synthesis.astype(jnp.bfloat16)
+        far_ref[m] = synthesis.T.astype(jnp.bfloat16)
+        far_ref[MODES + m] = banded.T.astype(jnp.bfloat16)
+
+
+def analysis_kernel(in_ref, table_ref, out_ref):
+    tiles = [in_ref[:, k].reshape(NLAT, 128).astype(jnp.float32) for k in range(9)]
+    units = split_lanes(tiles)
+    units = [dense(table_ref[u], units[u].astype(jnp.bfloat16)) for u in range(12)]
+    packed = []
+    for g in range(3):
+        packed += merge_lanes(*units[4 * g : 4 * g + 4])
+    store_rows(out_ref, merge_rows(packed))
+
+
+def synthesis_kernel(in_ref, table_ref, out_ref):
+    units = split_lanes(split_rows(load_rows(in_ref)))
+    units = [dense(table_ref[u], units[u].astype(jnp.bfloat16)) for u in range(12)]
+    for g in range(3):
+        tiles = merge_lanes(*units[4 * g : 4 * g + 4])
+        for k in range(3):
+            out_ref[:, 3 * g + k] = tiles[k].reshape(LAT, ROWS, 128).astype(jnp.bfloat16)
+
+
+def mixing_kernel(in_ref, weight_ref, pick_ref, pick_t_ref, out_ref, grad_ref, before, after):
+    units = split_lanes(split_rows(load_rows(in_ref)))
+    for u in range(12):
+        if u % 4:
+            units[u] = pltpu.roll(units[u], 32 * (u % 4), 1)
+        f, m = u // 6, u % 6
+        before[f, :, 32 * m : 32 * m + 32, :] = units[u].reshape(CHAN, 32, 128)
+    after[...] = jnp.zeros_like(after)
+    lane = iota((24, 128), 1)
+
+    def degree(l, carry):
+        left = []
+        for f in range(2):
+            columns = []
+            for p in range(4):
+                a = before[f, 2 * p, pl.ds(l, 24, stride=8), :]
+                b = before[f, 2 * p + 1, pl.ds(l, 24, stride=8), :]
+                first = jnp.where(lane < 64, a, pltpu.roll(b, 64, 1))
+                second = jnp.where(lane < 64, pltpu.roll(a, 80, 1), pltpu.roll(b, 16, 1))
+                columns.append(jnp.concatenate([first, second], axis=0))
+            left.append(jnp.concatenate(columns, axis=1).astype(jnp.bfloat16))
+        rows = []
+        for e in range(CHAN):
+            rows += [weight_ref[e, l], jnp.zeros((16, 384), jnp.bfloat16)]
+        weight = dense(jnp.concatenate(rows, axis=0), pick_ref[...]).astype(jnp.bfloat16)
+        mixed = dense(left[0], weight)
+        back = dense(left[1], weight, ((1,), (1,)))
+        dense_back = dense(left[1], pick_t_ref[...]).astype(jnp.bfloat16)
+        grad = dense(left[0], dense_back, ((0,), (0,)))
+        for e in range(CHAN):
+            grad_ref[e, l] = grad[64 * e : 64 * e + 48].astype(jnp.bfloat16)
+            for f, value in ((0, mixed), (1, back)):
+                tile = value[:, 128 * (e // 2) : 128 * (e // 2) + 128]
+                first, second = tile[:24], tile[24:]
+                if e % 2:
+                    first = pltpu.roll(first, 64, 1)
+                second = pltpu.roll(second, 112 if e % 2 else 48, 1)
+                after[f, e, pl.ds(l, 24, stride=8), :] = jnp.where(lane < 48, first, second)
+        return carry
+
+    lax.fori_loop(0, 6, degree, 0)
+    units = [after[u // 6, :, 32 * (u % 6) : 32 * (u % 6) + 32, :].reshape(256, 128) for u in range(12)]
+    packed = []
+    for g in range(3):
+        a, b, c, d = units[4 * g : 4 * g + 4]
+        packed += merge_lanes(a, pltpu.roll(b, 96, 1), pltpu.roll(c, 64, 1), pltpu.roll(d, 32, 1))
+    store_rows(out_ref, merge_rows(packed))
+
+
+def local(kernel, shapes, scratch, *arrays):
+    single = not isinstance(shapes, list)
+    spec = pl.BlockSpec(memory_space=pltpu.VMEM)
+    return pl.pallas_call(
+        kernel,
+        out_shape=shapes,
+        in_specs=[spec] * len(arrays),
+        out_specs=spec if single else [spec] * len(shapes),
+        scratch_shapes=scratch,
+        compiler_params=pltpu.CompilerParams(vmem_limit_bytes=VMEM_LIMIT),
+    )(*arrays)
+
+
+def bf16(*shape):
+    return jax.ShapeDtypeStruct(shape, jnp.bfloat16)
+
+
+def legendre_tables(band_rows):
     theta = math.pi * (np.arange(NLAT, dtype=np.float64) + 0.5) / NLAT
     cosine = np.cos(theta).astype(np.float32)[None, :]
     sine = np.sin(theta)
@@ -79,18 +302,17 @@
     order = orders.astype(jnp.float32)[:, None]
     own = lax.dynamic_slice(norm, (lax.axis_index("lat") * MODES,), (8,))
     sector = jnp.exp(own[:, None] + order * jnp.asarray(np.log(sine).astype(np.float32))[None, :])
-    table = pl.pallas_call(
-        legendre_kernel,
-        out_shape=jax.ShapeDtypeStruct((LMAX, 8, NLAT), jnp.float32),
-        in_specs=[pl.BlockSpec(memory_space=pltpu.VMEM)] * 3,
-        out_specs=pl.BlockSpec(memory_space=pltpu.VMEM),
-        compiler_params=pltpu.CompilerParams(vmem_limit_bytes=VMEM_LIMIT),
-    )(order, jnp.asarray(cosine), sector)
-    table = jnp.transpose(table[:, :MODES], (1, 0, 2))
-    quadrature = (math.sqrt(NLAT) * math.pi / NLAT * sine).astype(np.float32)
-    analysis = (table * jnp.asarray(quadrature)[None, None, :]).astype(jnp.bfloat16)
-    synthesis = (table * (1.0 / math.sqrt(LMAX))).astype(jnp.bfloat16)
-    return analysis, synthesis
+    quadrature = (math.sqrt(NLAT) * math.pi / NLAT * sine).astype(np.float32)[None, :]
+    return local(
+        table_kernel,
+        [bf16(12, 256, NLAT), bf16(12, NLAT, 256)],
+        [pltpu.VMEM((4, 2048, 128), jnp.float32)],
+        order,
+        jnp.asarray(cosine),
+        sector,
+        jnp.asarray(quadrature),
+        band_rows,
+    )
 
 
 def lat_to(step, lat, chan):
@@ -100,12 +322,21 @@
 
 def spectral_to(step, lat, chan):
     other = lax.rem(lat + step, LAT)
-    return other, lax.div(lat, 4), other, lax.rem(lat, 4) * CHAN + chan
+    group = 2 * lax.rem(lat, 4) + lax.rem(lax.div(lat, 4), 2)
+    return other, group, other, chan * 4 + lax.div(lat, 8)
 
 
 def spectral_from(step, lat, chan):
-    quarter, group = lax.div(step, CHAN), lax.rem(chan + step, CHAN)
-    return chan * 4 + quarter, group, quarter * CHAN + group, lat
+    part = lax.rem(step + lat, 4)
+    group = lax.rem(lax.div(step, 4) + chan, CHAN)
+    other = (2 * part + lax.rem(chan, 2)) * 4 + lax.div(chan, 2)
+    return other, group, group * 4 + part, lat
+
+
+def degree_owner(step, lat, chan):
+    other = lax.rem(lat + LAT - step, LAT)
+    group = 2 * lax.rem(lat, 4) + lax.rem(lax.div(lat, 4), 2)
+    return other, group, other, 0
 
 
 def exchange_kernel(sends, receives, spread, *refs):
@@ -258,30 +489,20 @@
     return jnp.concatenate([low, block, high], axis=1)
 
 
-def band_matrix(band_start, band_width, band_coef):
-    row = jnp.concatenate(
-        [
-            band_start.astype(jnp.float32)[:, None],
-            band_width.astype(jnp.float32)[:, None],
-            band_coef.astype(jnp.float32),
-        ],
-        axis=1,
-    )
-    rows = lax.all_gather(row, "lat", axis=0, tiled=True)
-    start = rows[:, 0:1].astype(jnp.int32)
-    width = rows[:, 1:2].astype(jnp.int32)
-    target = jnp.arange(NLAT, dtype=jnp.int32)[:, None]
-    source = jnp.arange(NLAT, dtype=jnp.int32)[None, :]
-    relative = source - target - start
-    matrix = jnp.zeros((NLAT, NLAT), jnp.float32)
-    for offset in range(4):
-        keep = (relative == offset) & (width > offset)
-        matrix = matrix + jnp.where(keep, rows[:, 2 + offset : 3 + offset], 0.0)
-    return matrix.astype(jnp.bfloat16)
-
-
 def dot(spec, a, b):
     return jnp.einsum(spec, a, b, preferred_element_type=jnp.float32)
+
+
+def local_band(start, width, coef, low):
+    count = start.shape[0]
+    target = jnp.arange(count, dtype=jnp.int32)[:, None]
+    source = jnp.arange(ROWS + 4 if low else ROWS, dtype=jnp.int32)[None, :]
+    relative = source - target - (HALO if low else -HALO) - start[:, None]
+    matrix = jnp.zeros(relative.shape, jnp.float32)
+    for offset in range(4):
+        keep = (relative == offset) & (width[:, None] > offset)
+        matrix = matrix + jnp.where(keep, coef[:, offset : offset + 1], 0.0)
+    return matrix.astype(jnp.bfloat16)
 
 
 def per_device(source_field, band_start, band_width, band_coef, mixing_weight, output_grad):
@@ -290,84 +511,71 @@
     table = fourier_table()
     lon_analysis = jnp.asarray((table / math.sqrt(NLON)).astype(jnp.bfloat16))
     lon_synthesis = jnp.asarray((table / math.sqrt(MMAX)).astype(jnp.bfloat16))
-
-    band = band_matrix(band_start, band_width, band_coef)
-    padded_band = jnp.pad(band, HALO)
-    band_rows = lax.dynamic_slice(padded_band, (lat * ROWS + HALO, lat * ROWS), (ROWS, ROWS + 4))
-    band_cols = lax.dynamic_slice(padded_band, (lat * ROWS, lat * ROWS + HALO), (ROWS + 4, ROWS))
-
-    analysis, synthesis = legendre_tables()
-    banded = dot("mli,ij->mlj", analysis, band).astype(jnp.bfloat16)
-
-    panels = jnp.stack(
+    flat = channels * ROWS
+
+    info = jnp.concatenate(
         [
-            dot("cin,nk->cik", source_field, lon_analysis).astype(jnp.bfloat16),
-            dot("cin,nk->cik", output_grad, lon_synthesis).astype(jnp.bfloat16),
-        ]
-    )
-    panels = panels.reshape(2, channels, ROWS, LAT, 3, 2, 2)
-    panels = jnp.transpose(panels, (3, 4, 2, 5, 0, 6, 1)).reshape(LAT, 3, ROWS, 8 * channels)
+            band_start.astype(jnp.bfloat16)[:, None],
+            band_width.astype(jnp.bfloat16)[:, None],
+            band_coef,
+            jnp.zeros((ROWS, 122), jnp.bfloat16),
+        ],
+        axis=1,
+    )
+    message = local(
+        spread_kernel,
+        bf16(LAT, 10, ROWS, 128),
+        [pltpu.VMEM((4, flat, 128), jnp.float32), pltpu.VMEM((2, MMAX * ROWS, 128), jnp.float32)],
+        dot("ik,kn->in", source_field.reshape(flat, NLON), lon_analysis).astype(jnp.bfloat16),
+        dot("ik,kn->in", output_grad.reshape(flat, NLON), lon_synthesis).astype(jnp.bfloat16),
+        info,
+    )
     columns, weight = exchange(
-        panels, lat_to, lambda k, a, b: lat_to(LAT - k, a, b), 1, "whole", mixing_weight
-    )
-    weight = jnp.transpose(weight, (1, 0, 2, 3)).reshape(6, CHAN * channels, CHAN * channels)
-
-    columns = columns.reshape(LAT, 3, ROWS, 2, 2, 2, channels)
-    columns = jnp.transpose(columns, (4, 1, 3, 0, 2, 5, 6)).reshape(2, MODES, NLAT, 2 * channels)
-    spectral = jnp.stack(
-        [
-            dot("mlj,mjk->mlk", banded, columns[0]).astype(jnp.bfloat16),
-            dot("mlj,mjk->mlk", synthesis, columns[1]).astype(jnp.bfloat16),
-        ]
-    )
-    message = jnp.transpose(
-        spectral.reshape(2, MODES, LAT, 6, 2 * channels), (2, 0, 1, 3, 4)
-    ).reshape(LAT, 54, 128)
-    message = jnp.pad(message, ((0, 0), (0, 10), (0, 0)))
-
-    def backwards(step, a, b):
-        other = spectral_from(step, a, b)
-        return other
-
-    received = exchange(message, spectral_to, backwards, 2)
-    received = received[:, :54].reshape(4, CHAN, 2, MODES, 6, 2, channels)
-    received = jnp.transpose(received, (2, 4, 0, 3, 5, 1, 6)).reshape(2, 6, 48, CHAN * channels)
-    coefficients, back_mixed = received[0], received[1]
-    grad = dot("lkc,lko->lco", coefficients, back_mixed).astype(jnp.bfloat16)
-    grad = jnp.transpose(grad.reshape(6, CHAN, channels, CHAN * channels), (1, 0, 2, 3))
-    mixed = dot("lkc,lco->lko", coefficients, weight).astype(jnp.bfloat16)
-    back_coef = dot("lko,lco->lkc", back_mixed, weight).astype(jnp.bfloat16)
-    reply = jnp.stack([mixed, back_coef]).reshape(2, 6, 4, MODES, 2, CHAN, channels)
-    reply = jnp.transpose(reply, (2, 5, 0, 3, 1, 4, 6)).reshape(LAT, 54, 128)
-    reply = jnp.pad(reply, ((0, 0), (0, 10), (0, 0)))
-
-    def replies(step, a, b):
-        other = lax.rem(a + step, LAT)
-        return other, lax.div(a, 4), other, 0
-
-    answers = exchange(reply, spectral_from, replies, 3)
-    answers = answers[:, :54].reshape(LAT, 2, MODES, 6, 2 * channels)
-    answers = jnp.transpose(answers, (1, 2, 0, 3, 4)).reshape(2, MODES, LMAX, 2 * channels)
-    grids = jnp.stack(
-        [
-            dot("mlj,mlk->mjk", synthesis, answers[0]).astype(jnp.bfloat16),
-            dot("mlj,mlk->mjk", banded, answers[1]).astype(jnp.bfloat16),
-        ]
-    )
-    grids = grids.reshape(2, 3, 2, LAT, ROWS, 2, channels)
-    grids = jnp.transpose(grids, (3, 1, 4, 2, 0, 5, 6)).reshape(LAT, 3, ROWS, 8 * channels)
+        message, lat_to, lambda k, a, b: lat_to(LAT - k, a, b), 1, "whole", mixing_weight
+    )
+    band_rows = columns[:, 9]
+    near, far = legendre_tables(band_rows)
+    message = local(analysis_kernel, bf16(LAT, 64, 128), [], columns, near)
+    received = exchange(message, spectral_to, spectral_from, 2)
+
+    pick = np.zeros((CHAN, channels, CHAN, 64), np.float32)
+    for e in range(CHAN):
+        pick[e, :, e, :channels] = np.eye(channels)
+    pick = pick.reshape(CHAN * channels, 512)
+    panel = pltpu.VMEM((2, CHAN, 192, 128), jnp.float32)
+    reply, grad = local(
+        mixing_kernel,
+        [bf16(LAT, 64, 128), bf16(CHAN, 6, channels, CHAN * channels)],
+        [panel, panel],
+        received,
+        weight,
+        jnp.asarray(pick.astype(jnp.bfloat16)),
+        jnp.asarray(pick.T.astype(jnp.bfloat16)),
+    )
+    answers = exchange(reply, spectral_from, degree_owner, 3)
+    message = local(synthesis_kernel, bf16(LAT, 9, ROWS, 128), [], answers, far)
     grids, grad_parts = exchange(
-        grids, lat_to, lambda k, a, b: lat_to(LAT - k, a, b), 4, "parts", grad
+        message, lat_to, lambda k, a, b: lat_to(LAT - k, a, b), 4, "parts", grad
     )
     grad_mixing = jnp.sum(grad_parts.astype(jnp.float32), axis=0)
-    grids = grids.reshape(LAT, 3, ROWS, 2, 2, 2, channels)
-    grids = jnp.transpose(grids, (4, 6, 2, 0, 1, 3, 5)).reshape(2, channels, ROWS, 2 * MMAX)
-
-    mixed_field = dot("cik,nk->cin", grids[0], lon_synthesis) + dot(
-        "ij,cjn->cin", band_rows, with_halo(source_field)
-    )
-    grad_input = dot("cik,nk->cin", grids[1], lon_analysis) + dot(
-        "ji,cjn->cin", band_cols, with_halo(output_grad)
+    forward, backward = local(
+        gather_kernel,
+        [bf16(flat, 512), bf16(flat, 512)],
+        [pltpu.VMEM((4, flat, 128), jnp.float32), pltpu.VMEM((2, MMAX * ROWS, 128), jnp.float32)],
+        grids,
+    )
+
+    rows = jnp.pad(band_rows.reshape(NLAT, 128), ((HALO, HALO), (0, 0)))
+    rows = lax.dynamic_slice(rows, (lat * ROWS, 0), (ROWS + 4, 128)).astype(jnp.float32)
+    start, width, coef = rows[:, 0].astype(jnp.int32), rows[:, 1].astype(jnp.int32), rows[:, 2:6]
+    own = slice(HALO, HALO + ROWS)
+    band_ahead = local_band(start[own], width[own], coef[own], True)
+    band_back = local_band(start, width, coef, False)
+    mixed_field = dot("ik,nk->in", forward, lon_synthesis).reshape(channels, ROWS, NLON) + dot(
+        "ij,cjn->cin", band_ahead, with_halo(source_field)
+    )
+    grad_input = dot("ik,nk->in", backward, lon_analysis).reshape(channels, ROWS, NLON) + dot(
+        "ji,cjn->cin", band_back, with_halo(output_grad)
     )
     return (mixed_field.astype(jnp.bfloat16), grad_input.astype(jnp.bfloat16), grad_mixing)
 

time: 381 us -> 214 us (0.56); the launches traced: 376 us -> 214 us
  local copies, waits for them, and re-layouts: 102 us -> 6.79 us
  blocking collectives: 45.5 us -> 0 us
  matrix products: 34.3 us -> 15.7 us
  other arithmetic: 12.3 us -> 1.37 us
  Pallas kernels: 165 us -> 174 us
    reshape x11 -> x0, local copies, waits for them, and re-layouts: 47.8 us -> none  [the longest x2 15.4 us: per_device(): grids = grids.reshape(LAT, 3, ROWS, 2, 2, 2, channels)]
    all_gather x1 -> x0, blocking collectives: 45.5 us -> none  [band_matrix(): rows = lax.all_gather(row, 'lat', axis=0, tiled=True)]
    pallas_call x1 -> x6, Pallas kernels: 5.62 us -> 35.4 us  [local(): pl.pallas_call(kernel, out_shape=shapes, in_specs=[spec] * len(arrays), o...]
    pallas_call x4, Pallas kernels: 160 us -> 138 us  [exchange(): pl.pallas_call(functools.partial(exchange_kernel, sends, receives, spread...]
    dot_general x14 -> x6, matrix products: 34.3 us -> 15.7 us  [dot(): return jnp.einsum(spec, a, b, preferred_element_type=jnp.float32)]
    transpose x4 -> x0, local copies, waits for them, and re-layouts: 11.9 us -> none  [the longest x1 5.18 us: per_device(): jnp.transpose(grids, (3, 1, 4, 2, 0, 5, 6))]
    squeeze x8 -> x0, local copies, waits for them, and re-layouts: 10 us -> none  [the longest x1 2.99 us: per_device(): grids[1]]
    transpose x4 -> x0, other arithmetic: 9.46 us -> none  [the longest x1 6.66 us: per_device(): jnp.transpose(grids, (3, 1, 4, 2, 0, 5, 6))]
  transfers between devices with their start and end apart: 4 -> 4, of which waited for: 0 -> 0; matrix products, arithmetic and copies ran while one was open for 37% -> 8% of each run, Pallas kernels for 44% -> 81%
where the time goes in v1:
time: 214 us
  Pallas kernels  174 us (81%)
  matrix products  15.7 us (7%)
  starting transfers between devices  15.2 us (7%)
  local copies, waits for them, and re-layouts  6.79 us (3%)
    pallas_call x4, Pallas kernels, exchange(): pl.pallas_call(functools.partial(exchange_kernel, sends, receives, spread...  138 us
    pallas_call x6, Pallas kernels, local(): pl.pallas_call(kernel, out_shape=shapes, in_specs=[spec] * len(arrays), o...  35.4 us
    dot_general x6, matrix products, dot(): return jnp.einsum(spec, a, b, preferred_element_type=jnp.float32)  15.7 us
    ppermute x2, starting transfers between devices, with_halo(): low = lax.ppermute(block[:, -HALO:], 'lat', forward)  11.3 us
    slice x2, local copies, waits for them, and re-layouts, with_halo(): low = lax.ppermute(block[:, -HALO:], 'lat', forward)  5.97 us
  transfers between devices with their start and end apart: 4, of which 0 were waited for; matrix products, arithmetic and copies ran while one was open for 8% of the time, Pallas kernels for 81%

profile of v1, /device:TPU:1, one launch (start us, length us, event | category | flops | bytes accessed | tf_op | source)
XLA Modules:
  0.0 213.7 jit_solution(15612798227824031305)
XLA Ops:
  0.6 0.0 copy-start.8
  0.6 0.0 copy-start.12
  0.7 0.0 copy-start.13
  0.7 0.0 copy-start.11
  0.7 3.0 %fusion.79 = (bf16[48,2,1440]{2,1,0:T(2,128)(2,1)}, bf16[48,2,1440]{2,1,0:T(2,128)(2,1)}) fusion(bf16[48,16,1440]{2,1,0:T(8,128)(2,1)} %param.14), kind=kLoop, calls=%fused_computation.113 | loop fusion | bytes 1105920 | tf_op jit(solution)/shard_map/slice | solution.py:487
  3.7 6.2 %collective-permute-start = (bf16[48,2,1440]{2,1,0:T(2,128)(2,1)}, bf16[48,2,1440]{2,1,0:T(2,128)(2,1)}, u32[]{:S(2)}, u32[]{:S(2)}) collective-permute-start(bf16[48,2,1440]{2,1,0:T(2,128)(2,1)} %get-tuple-element.25), channel_id=1, source_target_pairs={{0,1},{1,2},{2,3},{3,4},{4,5},{5,6},{6,7},{7,8},{8,9},{9,10},{10,1... | collective-permute-start | bytes 829448 | tf_op jit(solution)/shard_map/ppermute | solution.py:487
  9.9 1.9 collective-permute-start.1
  11.9 2.9 %fusion.78 = (bf16[48,2,1440]{2,1,0:T(2,128)(2,1)}, bf16[48,2,1440]{2,1,0:T(2,128)(2,1)}) fusion(bf16[48,16,1440]{2,1,0:T(8,128)(2,1)} %param.19), kind=kLoop, calls=%fused_computation.112 | loop fusion | bytes 1105920 | tf_op jit(solution)/shard_map/slice | solution.py:487
  14.8 5.1 %collective-permute-start.2 = (bf16[48,2,1440]{2,1,0:T(2,128)(2,1)}, bf16[48,2,1440]{2,1,0:T(2,128)(2,1)}, u32[]{:S(2)}, u32[]{:S(2)}) collective-permute-start(bf16[48,2,1440]{2,1,0:T(2,128)(2,1)} %get-tuple-element.23), channel_id=1, source_target_pairs={{0,1},{1,2},{2,3},{3,4},{4,5},{5,6},{6,7},{7,8},{8,9},{9,10},{10,1... | collective-permute-start | bytes 829448 | tf_op jit(solution)/shard_map/ppermute | solution.py:487
  19.9 1.9 collective-permute-start.3
  21.9 0.0 copy-done.12
  21.9 0.0 copy-done.13
  21.9 0.1 copy.29
  22.0 0.1 copy.28
  22.1 0.0 copy-done.11
  22.1 0.1 copy.30
  22.2 0.1 pad.14.clone
  22.3 0.0 copy-done.8
  22.3 2.9 %fusion.13.grad_ref = bf16[768,512]{1,0:T(8,128)(2,1)S(1)} fusion(bf16[768,1440]{1,0:T(8,128)(2,1)S(1)} %bitcast.75, bf16[1440,512]{1,0:T(8,128)(2,1)} %constant.33.clone), kind=kOutput, calls=%fused_computation.18 | convolution fusion | flops 1132855296 | bytes 4472832 | tf_op jit(solution)/shard_map/ik,kn->in/dot_general | solution.py:493
  25.2 0.0 copy-done.6
  25.2 0.0 copy-done.14
  25.2 1.4 fusion.12.source_ref
  26.6 0.0 copy-start.3
  26.6 0.1 maximum_maximum_fusion.band_ref
  26.7 0.0 copy-start.5
  26.7 7.3 %shard_map.157.refs_0_ = bf16[32,10,16,128]{3,2,1,0:T(8,128)(2,1)S(1)} custom-call(bf16[768,512]{1,0:T(8,128)(2,1)S(1)} %fusion.12.source_ref, bf16[768,512]{1,0:T(8,128)(2,1)S(1)} %fusion.13.grad_ref, bf16[16,128]{1,0:T(8,128)(2,1)S(1)} %maximum_maximum_fusion.band_ref), custom_call_target="tpu_custom_call" | custom-call | tf_op jit(solution)/shard_map/pallas_call | solution.py:282
  34.0 0.0 copy-done.3
  34.0 47.6 %shard_map.158 = (bf16[32,10,16,128]{3,2,1,0:T(8,128)(2,1)S(1)}, bf16[8,6,48,384]{3,2,1,0:T(8,128)(2,1)S(1)}) custom-call(bf16[32,10,16,128]{3,2,1,0:T(8,128)(2,1)S(1)} %shard_map.157.refs_0_, bf16[6,48,384]{2,1,0:T(8,128)(2,1)S(1)} %copy-done.3), custom_call_target="tpu_custom_call" | custom-call | tf_op jit(solution)/shard_map/pallas_call | solution.py:471
  81.7 0.1 copy.33
  81.8 0.1 fusion.14
  82.0 0.1 slice_bitcast_fusion.7
  82.0 0.1 slice_bitcast_fusion.8
  82.1 0.1 compare_bitcast_fusion.7
  82.2 0.0 copy-done.17
  82.2 0.1 dynamic_slice.6
  82.3 0.0 copy-done.10
  82.3 0.1 add_exponential_fusion.sector_ref
  82.3 0.0 copy-done.4
  82.4 11.7 %shard_map.159 = (bf16[12,256,512]{2,1,0:T(8,128)(2,1)S(1)}, bf16[12,512,256]{2,1,0:T(8,128)(2,1)}) custom-call(f32[8,1]{1,0:T(8,128)S(1)} %add_convert_fusion.2.order_ref, f32[1,512]{1,0:T(1,128)S(1)} %copy-done.5, f32[8,512]{1,0:T(8,128)S(1)} %add_exponential_fusion.sector_ref, f32[1,512]{1,0:T(1,128)S(1)} %copy-done.4, ...), custom_call_target="tpu_custom_call" | custom-call | tf_op jit(solution)/shard_map/pallas_call | solution.py:282
  94.0 1.0 shard_map.160.refs_0_
  95.1 0.0 copy-start
  95.1 24.6 %shard_map.161.in_ref = bf16[32,64,128]{2,1,0:T(8,128)(2,1)S(1)} custom-call(bf16[32,64,128]{2,1,0:T(8,128)(2,1)S(1)} %shard_map.160.refs_0_), custom_call_target="tpu_custom_call" | custom-call | tf_op jit(solution)/shard_map/pallas_call | solution.py:471
  119.7 0.0 copy-done.1
  119.7 0.0 copy-done.2
  119.7 7.0 %shard_map.162 = (bf16[32,64,128]{2,1,0:T(8,128)(2,1)S(1)}, bf16[8,6,48,384]{3,2,1,0:T(8,128)(2,1)S(1)}) custom-call(bf16[32,64,128]{2,1,0:T(8,128)(2,1)S(1)} %shard_map.161.in_ref, bf16[8,6,48,384]{3,2,1,0:T(8,128)(2,1)S(1)} %get-tuple-element.15.weight_ref, bf16[384,512]{1,0:T(8,128)(2,1)S(1)} %copy-done.2, bf16[512,384]{1,0:T(8,128)(2,1)S(1)} %copy-done.1), custom_call_target="tpu_custom_call" | custom-call | tf_op jit(solution)/shard_map/pallas_call | solution.py:282
  126.8 27.4 %shard_map.163.in_ref = bf16[32,64,128]{2,1,0:T(8,128)(2,1)S(1)} custom-call(bf16[32,64,128]{2,1,0:T(8,128)(2,1)S(1)} %get-tuple-element.16.refs_0_), custom_call_target="tpu_custom_call" | custom-call | tf_op jit(solution)/shard_map/pallas_call | solution.py:471
  154.1 0.0 copy-done
  154.1 1.0 shard_map.164.refs_0_
  155.1 0.0 copy-start.16
  155.1 38.6 %shard_map.165 = (bf16[32,9,16,128]{3,2,1,0:T(8,128)(2,1)S(1)}, bf16[8,6,48,384]{3,2,1,0:T(8,128)(2,1)S(1)}) custom-call(bf16[32,9,16,128]{3,2,1,0:T(8,128)(2,1)S(1)} %shard_map.164.refs_0_, bf16[8,6,48,384]{3,2,1,0:T(8,128)(2,1)S(1)} %get-tuple-element.18.refs_1_), custom_call_target="tpu_custom_call" | custom-call | tf_op jit(solution)/shard_map/pallas_call | solution.py:471
  193.8 7.4 %shard_map.166 = (bf16[768,512]{1,0:T(8,128)(2,1)S(1)}, bf16[768,512]{1,0:T(8,128)(2,1)S(1)}) custom-call(bf16[32,9,16,128]{3,2,1,0:T(8,128)(2,1)S(1)} %get-tuple-element.19.in_ref), custom_call_target="tpu_custom_call" | custom-call | tf_op jit(solution)/shard_map/pallas_call | solution.py:282
  201.2 0.0 copy-start.15
  201.2 1.4 fusion.81
  202.6 0.0 copy-done.15
  202.6 0.0 copy-start.7
  202.6 1.4 fusion.82
  204.0 1.0 convert_reduce_fusion
  205.1 0.0 collective-permute-done
  205.1 0.0 collective-permute-done.1
  205.1 0.0 copy-start.9
  205.1 4.4 %fusion.1 = bf16[48,16,1440]{2,1,0:T(8,128)(2,1)} fusion(f32[48,16,1440]{2,1,0:T(8,128)S(1)} %bitcast.77, bf16[48,2,1440]{2,1,0:T(2,128)(2,1)} %collective-permute-done.1, bf16[48,16,1440]{2,1,0:T(8,128)(2,1)S(1)} %copy-done.7, bf16[48,2,1440]{2,1,0:T(2,128)(2,1)} %collective-permute-done, f32[16]{0:T(128)S(1)} %get-tuple-element.41, ...), kind=kOutput, calls=%fused_computation.3 | convolution fusion | flops 54749120 | bytes 9400704 | tf_op jit(solution)/shard_map/ij,cjn->cin/dot_general | solution.py:493
  209.5 0.0 collective-permute-done.2
  209.5 0.0 collective-permute-done.3
  209.5 4.2 %fusion = bf16[48,16,1440]{2,1,0:T(8,128)(2,1)} fusion(f32[48,16,1440]{2,1,0:T(8,128)S(1)} %bitcast.76, bf16[48,2,1440]{2,1,0:T(2,128)(2,1)} %collective-permute-done.3, bf16[48,16,1440]{2,1,0:T(8,128)(2,1)S(1)} %copy-done.9, bf16[48,2,1440]{2,1,0:T(2,128)(2,1)} %collective-permute-done.2, f32[20]{0:T(128)S(1)} %get-tuple-element.34, ...), kind=kOutput, calls=%fused_computation.1 | convolution fusion | flops 54749120 | bytes 9400800 | tf_op jit(solution)/shard_map/ji,cjn->cin/dot_general | solution.py:493
  (19 shorter events, 0.1 us)
Async XLA Ops:
  0.6 21.7 %copy-start.8 = (bf16[48,16,1440]{2,1,0:T(8,128)(2,1)S(1)}, bf16[48,16,1440]{2,1,0:T(8,128)(2,1)}, u32[]{:S(2)}) copy-start(bf16[48,16,1440]{2,1,0:T(8,128)(2,1)} %param.19) | copy-start | bytes 6635524
  0.6 21.2 %copy-start.12 = (s32[16]{0:T(128)S(1)}, s32[16]{0:T(128)}, u32[]{:S(2)}) copy-start(s32[16]{0:T(128)} %param.15) | copy-start | bytes 196
  0.7 21.3 %copy-start.13 = (s32[16]{0:T(128)S(1)}, s32[16]{0:T(128)}, u32[]{:S(2)}) copy-start(s32[16]{0:T(128)} %param.16) | copy-start | bytes 196
  0.7 21.5 %copy-start.11 = (bf16[16,4]{0,1:T(4,128)(2,1)S(1)}, bf16[16,4]{0,1:T(4,128)(2,1)}, u32[]{:S(2)}) copy-start(bf16[16,4]{0,1:T(4,128)(2,1)} %param.17) | copy-start | bytes 388
  3.7 201.3 %collective-permute-start = (bf16[48,2,1440]{2,1,0:T(2,128)(2,1)}, bf16[48,2,1440]{2,1,0:T(2,128)(2,1)}, u32[]{:S(2)}, u32[]{:S(2)}) collective-permute-start(bf16[48,2,1440]{2,1,0:T(2,128)(2,1)} %get-tuple-element.25), channel_id=1, source_target_pairs={{0,1},{1,2},{2,3},{3,4},{4,5},{5,6},{6,7},{7,8},{8,9},{9,10},{10,1... | collective-permute-start | bytes 829448 | tf_op jit(solution)/shard_map/ppermute | solution.py:487
  9.9 195.1 %collective-permute-start.1 = (bf16[48,2,1440]{2,1,0:T(2,128)(2,1)}, bf16[48,2,1440]{2,1,0:T(2,128)(2,1)}, u32[]{:S(2)}, u32[]{:S(2)}) collective-permute-start(bf16[48,2,1440]{2,1,0:T(2,128)(2,1)} %get-tuple-element.26), channel_id=1, source_target_pairs={{1,0},{2,1},{3,2},{4,3},{5,4},{6,5},{7,6},{8,7},{9,8},{10,9},{11,1... | collective-permute-start | bytes 829448 | tf_op jit(solution)/shard_map/ppermute | solution.py:488
  14.8 194.7 %collective-permute-start.2 = (bf16[48,2,1440]{2,1,0:T(2,128)(2,1)}, bf16[48,2,1440]{2,1,0:T(2,128)(2,1)}, u32[]{:S(2)}, u32[]{:S(2)}) collective-permute-start(bf16[48,2,1440]{2,1,0:T(2,128)(2,1)} %get-tuple-element.23), channel_id=1, source_target_pairs={{0,1},{1,2},{2,3},{3,4},{4,5},{5,6},{6,7},{7,8},{8,9},{9,10},{10,1... | collective-permute-start | bytes 829448 | tf_op jit(solution)/shard_map/ppermute | solution.py:487
  19.9 189.6 %collective-permute-start.3 = (bf16[48,2,1440]{2,1,0:T(2,128)(2,1)}, bf16[48,2,1440]{2,1,0:T(2,128)(2,1)}, u32[]{:S(2)}, u32[]{:S(2)}) collective-permute-start(bf16[48,2,1440]{2,1,0:T(2,128)(2,1)} %get-tuple-element.24), channel_id=1, source_target_pairs={{1,0},{2,1},{3,2},{4,3},{5,4},{6,5},{7,6},{8,7},{9,8},{10,9},{11,1... | collective-permute-start | bytes 829448 | tf_op jit(solution)/shard_map/ppermute | solution.py:488
  22.3 2.9 %copy-start.6 = (bf16[48,16,1440]{2,1,0:T(8,128)(2,1)S(1)}, bf16[48,16,1440]{2,1,0:T(8,128)(2,1)}, u32[]{:S(2)}) copy-start(bf16[48,16,1440]{2,1,0:T(8,128)(2,1)} %param.14) | copy-start | bytes 6635524
  22.3 2.9 %copy-start.14 = (bf16[1440,512]{1,0:T(8,128)(2,1)S(1)}, bf16[1440,512]{1,0:T(8,128)(2,1)}, u32[]{:S(2)}) copy-start(bf16[1440,512]{1,0:T(8,128)(2,1)} %constant.32.clone) | copy-start | bytes 4423684
  26.6 7.4 %copy-start.3 = (bf16[6,48,384]{2,1,0:T(8,128)(2,1)S(1)}, bf16[6,48,384]{2,1,0:T(8,128)(2,1)}, u32[]{:S(2)}) copy-start(bf16[6,48,384]{2,1,0:T(8,128)(2,1)} %refs_1_.1) | copy-start | bytes 663556
  26.7 55.5 %copy-start.17 = (f32[194]{0:T(256)S(1)}, f32[194]{0:T(256)}, u32[]{:S(2)}) copy-start(f32[194]{0:T(256)} %constant.12.clone) | copy-start | bytes 2332
  26.7 55.6 %copy-start.10 = (f32[512]{0:T(512)S(1)}, f32[512]{0:T(512)}, u32[]{:S(2)}) copy-start(f32[512]{0:T(512)} %constant.13.clone) | copy-start | bytes 6148
  26.7 55.6 %copy-start.4 = (f32[1,512]{1,0:T(1,128)S(1)}, f32[1,512]{1,0:T(1,128)}, u32[]{:S(2)}) copy-start(f32[1,512]{1,0:T(1,128)} %constant.15.clone.quad_ref) | copy-start | bytes 6148
  26.7 55.6 %copy-start.5 = (f32[1,512]{1,0:T(1,128)S(1)}, f32[1,512]{1,0:T(1,128)}, u32[]{:S(2)}) copy-start(f32[1,512]{1,0:T(1,128)} %constant.14.clone.cosine_ref) | copy-start | bytes 6148
  94.0 25.7 %copy-start.1 = (bf16[512,384]{1,0:T(8,128)(2,1)S(1)}, bf16[512,384]{1,0:T(8,128)(2,1)}, u32[]{:S(2)}) copy-start(bf16[512,384]{1,0:T(8,128)(2,1)} %constant.17.clone.pick_t_ref) | copy-start | bytes 1179652
  94.0 25.7 %copy-start.2 = (bf16[384,512]{1,0:T(8,128)(2,1)S(1)}, bf16[384,512]{1,0:T(8,128)(2,1)}, u32[]{:S(2)}) copy-start(bf16[384,512]{1,0:T(8,128)(2,1)} %constant.16.clone.pick_ref) | copy-start | bytes 1179652
  95.1 59.1 %copy-start = (bf16[12,512,256]{2,1,0:T(8,128)(2,1)S(1)}, bf16[12,512,256]{2,1,0:T(8,128)(2,1)}, u32[]{:S(2)}) copy-start(bf16[12,512,256]{2,1,0:T(8,128)(2,1)} %get-tuple-element.17.table_ref) | copy-start | bytes 9437188
  155.1 46.0 %copy-start.16 = (bf16[1440,512]{1,0:T(8,128)(2,1)S(1)}, bf16[1440,512]{1,0:T(8,128)(2,1)}, u32[]{:S(2)}) copy-start(bf16[1440,512]{1,0:T(8,128)(2,1)} %constant.33.clone) | copy-start | bytes 4423684
  201.2 1.4 copy-start.15
  202.6 2.5 %copy-start.7 = (bf16[48,16,1440]{2,1,0:T(8,128)(2,1)S(1)}, bf16[48,16,1440]{2,1,0:T(8,128)(2,1)}, u32[]{:S(2)}) copy-start(bf16[48,16,1440]{2,1,0:T(8,128)(2,1)} %param.14) | copy-start | bytes 6635524
  205.1 4.4 %copy-start.9 = (bf16[48,16,1440]{2,1,0:T(8,128)(2,1)S(1)}, bf16[48,16,1440]{2,1,0:T(8,128)(2,1)}, u32[]{:S(2)}) copy-start(bf16[48,16,1440]{2,1,0:T(8,128)(2,1)} %param.19) | copy-start | bytes 6635524

commit v2 on v1

--- a/solution.py
+++ b/solution.py
@@ -93,15 +93,16 @@
         out_ref[:, 16 * p : 16 * p + 16, :] = jnp.concatenate(pair, axis=1).astype(jnp.bfloat16)
 
 
-def load_rows(in_ref):
+def load_rows(in_ref, live):
     tiles = []
     for p in range(4):
         pair = in_ref[:, 16 * p : 16 * p + 16, :].astype(jnp.float32)
+        pair = jnp.where(live, pair, 0.0)
         tiles += [pair[:, :8].reshape(256, 128), pair[:, 8:].reshape(256, 128)]
     return tiles
 
 
-def spread_kernel(source_ref, grad_ref, band_ref, out_ref, part, rows):
+def spread_kernel(source_ref, grad_ref, out_ref, part, rows, link):
     for f, ref in ((0, source_ref), (1, grad_ref)):
         for k in range(4):
             part[k] = ref[:, 128 * k : 128 * k + 128].astype(jnp.float32)
@@ -116,7 +117,8 @@
 
         lax.fori_loop(0, ROWS, turn, 0)
 
-    def send(d, carry):
+    def send(step, carry):
+        d = lax.rem(link.lat + step, LAT)
         units = [
             rows[f, pl.ds(pl.multiple_of((d * 6 + m) * 16, 16), 16), :]
             for f in range(2)
@@ -127,7 +129,7 @@
             tiles = merge_lanes(a, pltpu.roll(b, 96, 1), pltpu.roll(c, 64, 1), pltpu.roll(e, 32, 1))
             for k in range(3):
                 out_ref[d, 3 * g + k] = tiles[k].astype(jnp.bfloat16)
-        out_ref[d, 9] = band_ref[...]
+        link.start(step)
         return carry
 
     lax.fori_loop(0, LAT, send, 0)
@@ -160,7 +162,7 @@
             ref[:, 128 * k : 128 * k + 128] = part[k].astype(jnp.bfloat16)
 
 
-def table_kernel(order_ref, cosine_ref, sector_ref, quad_ref, band_ref, near_ref, far_ref, table):
+def recurrence(order_ref, cosine_ref, sector_ref, table):
     order = jnp.broadcast_to(order_ref[...], (8, NLAT))
     cosine = jnp.broadcast_to(cosine_ref[...], (8, NLAT))
     sector = sector_ref[...]
@@ -190,6 +192,8 @@
     zero = sector * 0.0
     lax.fori_loop(0, LMAX, advance, (zero, zero))
 
+
+def finish_tables(quad_ref, band_ref, near_ref, far_ref, table):
     info = band_ref[...].reshape(NLAT, 128).astype(jnp.float32)
     relative = (iota((NLAT, NLAT), 1) - iota((NLAT, NLAT), 0)).astype(jnp.float32) - info[:, 0:1]
     band = jnp.zeros((NLAT, NLAT), jnp.float32)
@@ -219,7 +223,8 @@
 
 
 def synthesis_kernel(in_ref, table_ref, out_ref):
-    units = split_lanes(split_rows(load_rows(in_ref)))
+    live = iota((LAT, 16, 128), 0) + lax.axis_index("lat") < LAT
+    units = split_lanes(split_rows(load_rows(in_ref, live)))
     units = [dense(table_ref[u], units[u].astype(jnp.bfloat16)) for u in range(12)]
     for g in range(3):
         tiles = merge_lanes(*units[4 * g : 4 * g + 4])
@@ -228,7 +233,10 @@
 
 
 def mixing_kernel(in_ref, weight_ref, pick_ref, pick_t_ref, out_ref, grad_ref, before, after):
-    units = split_lanes(split_rows(load_rows(in_ref)))
+    lat, chan = lax.axis_index("lat"), lax.axis_index("chan")
+    slot = iota((LAT, 16, 128), 0)
+    other = (2 * (slot % 4) + lax.rem(chan, 2)) * 4 + lax.div(chan, 2)
+    units = split_lanes(split_rows(load_rows(in_ref, other + lat < LAT)))
     for u in range(12):
         if u % 4:
             units[u] = pltpu.roll(units[u], 32 * (u % 4), 1)
@@ -293,7 +301,7 @@
     return jax.ShapeDtypeStruct(shape, jnp.bfloat16)
 
 
-def legendre_tables(band_rows):
+def legendre_inputs():
     theta = math.pi * (np.arange(NLAT, dtype=np.float64) + 0.5) / NLAT
     cosine = np.cos(theta).astype(np.float32)[None, :]
     sine = np.sin(theta)
@@ -303,16 +311,7 @@
     own = lax.dynamic_slice(norm, (lax.axis_index("lat") * MODES,), (8,))
     sector = jnp.exp(own[:, None] + order * jnp.asarray(np.log(sine).astype(np.float32))[None, :])
     quadrature = (math.sqrt(NLAT) * math.pi / NLAT * sine).astype(np.float32)[None, :]
-    return local(
-        table_kernel,
-        [bf16(12, 256, NLAT), bf16(12, NLAT, 256)],
-        [pltpu.VMEM((4, 2048, 128), jnp.float32)],
-        order,
-        jnp.asarray(cosine),
-        sector,
-        jnp.asarray(quadrature),
-        band_rows,
-    )
+    return order, jnp.asarray(cosine), sector, jnp.asarray(quadrature)
 
 
 def lat_to(step, lat, chan):
@@ -339,146 +338,260 @@
     return other, group, other, 0
 
 
-def exchange_kernel(sends, receives, spread, *refs):
-    if spread is None:
-        x_ref, out_ref, send_sem, recv_sem, own_sem = refs
-    else:
-        x_ref, side_ref, out_ref, side_out_ref = refs[:4]
-        send_sem, recv_sem, own_sem, side_send, side_recv, side_own = refs[4:]
-    lat, chan = lax.axis_index("lat"), lax.axis_index("chan")
-    barrier = pltpu.get_barrier_semaphore()
-
-    def same(pair):
-        return (pair[0] == lat) & (pair[1] == chan)
-
-    def greet(step, count):
-        source = receives(step, lat, chan)
-
-        @pl.when(jnp.logical_not(same(source)))
+class Wire:
+    def __init__(self, sends, receives, skip, source, target, sems):
+        self.lat, self.chan = lax.axis_index("lat"), lax.axis_index("chan")
+        self.sends, self.receives, self.skip = sends, receives, skip
+        self.source, self.target = source, target
+        self.send_sem, self.recv_sem, self.own_sem = sems
+
+    def live(self, pair):
+        if self.skip:
+            return self.lat + pair[0] < LAT
+        return pair[0] >= 0
+
+    def own(self, pair):
+        return (pair[0] == self.lat) & (pair[1] == self.chan) & self.live(pair)
+
+    def far(self, pair):
+        return jnp.logical_not((pair[0] == self.lat) & (pair[1] == self.chan)) & self.live(pair)
+
+    def greet(self, barrier, total):
+        def step_fn(step, count):
+            source = self.receives(step, self.lat, self.chan)
+
+            @pl.when(self.far(source))
+            def _():
+                pl.semaphore_signal(
+                    barrier, inc=1, device_id={"lat": source[0], "chan": source[1]},
+                    device_id_type=MESH,
+                )
+
+            return count + jnp.where(self.far(self.sends(step, self.lat, self.chan)), 1, 0)
+
+        return lax.fori_loop(0, LAT, step_fn, total)
+
+    def remote(self, pair, slot):
+        return pltpu.make_async_remote_copy(
+            src_ref=self.source.at[pair[2]],
+            dst_ref=self.target.at[slot],
+            send_sem=self.send_sem.at[pair[2]],
+            recv_sem=self.recv_sem.at[slot],
+            device_id={"lat": pair[0], "chan": pair[1]},
+            device_id_type=MESH,
+        )
+
+    def local(self, pair):
+        return pltpu.make_async_copy(
+            self.source.at[pair[2]], self.target.at[pair[3]], self.own_sem
+        )
+
+    def start(self, step):
+        pair = self.sends(step, self.lat, self.chan)
+
+        @pl.when(self.own(pair))
         def _():
+            self.local(pair).start()
+
+        @pl.when(self.far(pair))
+        def _():
+            self.remote(pair, pair[3]).start()
+
+    def start_all(self):
+        def step_fn(step, carry):
+            self.start(step)
+            return carry
+
+        lax.fori_loop(0, LAT, step_fn, 0)
+
+    def arrive(self):
+        def step_fn(step, carry):
+            target = self.sends(step, self.lat, self.chan)
+            source = self.receives(step, self.lat, self.chan)
+
+            @pl.when(self.own(target))
+            def _():
+                self.local(target).wait()
+
+            @pl.when(self.far(source))
+            def _():
+                self.remote(source, source[2]).wait_recv()
+
+            return carry
+
+        lax.fori_loop(0, LAT, step_fn, 0)
+
+    def leave(self):
+        def step_fn(step, carry):
+            target = self.sends(step, self.lat, self.chan)
+
+            @pl.when(self.far(target))
+            def _():
+                self.remote(target, target[3]).wait_send()
+
+            return carry
+
+        lax.fori_loop(0, LAT, step_fn, 0)
+
+
+class Side:
+    def __init__(self, parts, source, target, sems):
+        self.lat, self.chan = lax.axis_index("lat"), lax.axis_index("chan")
+        self.parts, self.source, self.target = parts, source, target
+        self.send_sem, self.recv_sem, self.own_sem = sems
+
+    def greet(self, barrier, total):
+        def step_fn(step, count):
             pl.semaphore_signal(
-                barrier, inc=1, device_id={"lat": source[0], "chan": source[1]},
-                device_id_type=MESH,
-            )
-
-        return count + jnp.where(same(sends(step, lat, chan)), 0, 1)
-
-    expected = lax.fori_loop(0, LAT, greet, jnp.int32(0))
-    if spread is not None:
-
-        def greet_side(step, count):
-            pl.semaphore_signal(
-                barrier, inc=1, device_id={"lat": lat, "chan": lax.rem(chan + step, CHAN)},
+                barrier, inc=1,
+                device_id={"lat": self.lat, "chan": lax.rem(self.chan + step, CHAN)},
                 device_id_type=MESH,
             )
             return count + 1
 
-        expected = lax.fori_loop(1, CHAN, greet_side, expected)
-    pl.semaphore_wait(barrier, expected)
-
-    def remote(target):
+        return lax.fori_loop(1, CHAN, step_fn, total)
+
+    def remote(self, step, incoming):
+        other = lax.rem(self.chan + step, CHAN)
+        slot = other if incoming else self.chan
         return pltpu.make_async_remote_copy(
-            src_ref=x_ref.at[target[2]],
-            dst_ref=out_ref.at[target[3]],
-            send_sem=send_sem.at[target[2]],
-            recv_sem=recv_sem.at[target[3]],
-            device_id={"lat": target[0], "chan": target[1]},
+            src_ref=self.source.at[other] if self.parts else self.source,
+            dst_ref=self.target.at[slot],
+            send_sem=self.send_sem.at[other],
+            recv_sem=self.recv_sem.at[slot],
+            device_id={"lat": self.lat, "chan": other},
             device_id_type=MESH,
         )
 
-    def side(step, source):
-        other = lax.rem(chan + step, CHAN)
+    def local(self):
+        source = self.source.at[self.chan] if self.parts else self.source
+        return pltpu.make_async_copy(source, self.target.at[self.chan], self.own_sem)
+
+    def start(self):
+        self.local().start()
+
+        def step_fn(step, carry):
+            self.remote(step, False).start()
+            return carry
+
+        lax.fori_loop(1, CHAN, step_fn, 0)
+
+    def finish(self):
+        self.local().wait()
+
+        def step_fn(step, carry):
+            self.remote(step, False).wait_send()
+            self.remote(step, True).wait_recv()
+            return carry
+
+        lax.fori_loop(1, CHAN, step_fn, 0)
+
+
+def lat_from(step, lat, chan):
+    return lat_to(LAT - step, lat, chan)
+
+
+def whole_to(step, lat, chan):
+    other = lax.rem(lat + step, LAT)
+    return other, chan, 0, lat
+
+
+def whole_from(step, lat, chan):
+    other = lax.rem(lat + LAT - step, LAT)
+    return other, chan, other, lat
+
+
+class Whole(Wire):
+    def remote(self, pair, slot):
         return pltpu.make_async_remote_copy(
-            src_ref=side_ref.at[other] if spread == "parts" else side_ref,
-            dst_ref=side_out_ref.at[other if source else chan],
-            send_sem=side_send.at[other],
-            recv_sem=side_recv.at[other if source else chan],
-            device_id={"lat": lat, "chan": other},
+            src_ref=self.source,
+            dst_ref=self.target.at[slot],
+            send_sem=self.send_sem.at[pair[0]],
+            recv_sem=self.recv_sem.at[slot],
+            device_id={"lat": pair[0], "chan": pair[1]},
             device_id_type=MESH,
         )
 
-    def side_local():
-        source = side_ref.at[chan] if spread == "parts" else side_ref
-        return pltpu.make_async_copy(source, side_out_ref.at[chan], side_own)
-
-    def start(step, carry):
-        target = sends(step, lat, chan)
-
-        @pl.when(same(target))
-        def _():
-            pltpu.make_async_copy(x_ref.at[target[2]], out_ref.at[target[3]], own_sem).start()
-
-        @pl.when(jnp.logical_not(same(target)))
-        def _():
-            remote(target).start()
-
-        return carry
-
-    def start_side(step, carry):
-        side(step, False).start()
-        return carry
-
-    lax.fori_loop(0, LAT, start, 0)
-    if spread is not None:
-        side_local().start()
-        lax.fori_loop(1, CHAN, start_side, 0)
-
-    def finish(step, carry):
-        target = sends(step, lat, chan)
-        source = receives(step, lat, chan)
-
-        @pl.when(same(target))
-        def _():
-            pltpu.make_async_copy(x_ref.at[target[2]], out_ref.at[target[3]], own_sem).wait()
-
-        @pl.when(jnp.logical_not(same(target)))
-        def _():
-            remote(target).wait_send()
-
-        @pl.when(jnp.logical_not(same(source)))
-        def _():
-            remote((source[0], source[1], source[2], source[2])).wait_recv()
-
-        return carry
-
-    def finish_side(step, carry):
-        side(step, False).wait_send()
-        side(step, True).wait_recv()
-        return carry
-
-    lax.fori_loop(0, LAT, finish, 0)
-    if spread is not None:
-        side_local().wait()
-        lax.fori_loop(1, CHAN, finish_side, 0)
-
-
-def exchange(x, sends, receives, collective_id, spread=None, extra=None):
-    arrays, shapes = [x], [jax.ShapeDtypeStruct(x.shape, x.dtype)]
-    scratch = [
-        pltpu.SemaphoreType.DMA((LAT,)),
-        pltpu.SemaphoreType.DMA((LAT,)),
-        pltpu.SemaphoreType.DMA,
-    ]
-    if spread is not None:
-        shape = extra.shape if spread == "parts" else (CHAN,) + extra.shape
-        arrays.append(extra)
-        shapes.append(jax.ShapeDtypeStruct(shape, extra.dtype))
-        scratch += [
-            pltpu.SemaphoreType.DMA((CHAN,)),
-            pltpu.SemaphoreType.DMA((CHAN,)),
-            pltpu.SemaphoreType.DMA,
-        ]
-    out = pl.pallas_call(
-        functools.partial(exchange_kernel, sends, receives, spread),
+    def local(self, pair):
+        return pltpu.make_async_copy(self.source, self.target.at[pair[3]], self.own_sem)
+
+
+def meet(links):
+    barrier = pltpu.get_barrier_semaphore()
+    total = jnp.int32(0)
+    for link in links:
+        total = link.greet(barrier, total)
+    pl.semaphore_wait(barrier, total)
+
+
+def front_kernel(
+    source_ref, grad_ref, info_ref, weight_ref, order_ref, cosine_ref, sector_ref, quad_ref,
+    out_ref, weights_ref, bands_ref, far_ref,
+    part, rows, table, near, message, landing, bands, spectral, *sems
+):
+    panels = Wire(lat_to, lat_from, False, message, landing, sems[0:3])
+    degrees = Wire(spectral_to, spectral_from, True, spectral, out_ref, sems[3:6])
+    info = Whole(whole_to, whole_from, False, info_ref, bands, sems[6:9])
+    side = Side(False, weight_ref, weights_ref, sems[9:12])
+    meet([panels, degrees, info, side])
+    side.start()
+    info.start_all()
+    spread_kernel(source_ref, grad_ref, message, part, rows, panels)
+    recurrence(order_ref, cosine_ref, sector_ref, table)
+    info.arrive()
+    finish_tables(quad_ref, bands, near, far_ref, table)
+    bands_ref[...] = bands[...]
+    panels.arrive()
+    analysis_kernel(landing, near, spectral)
+    degrees.start_all()
+    info.leave()
+    panels.leave()
+    degrees.arrive()
+    degrees.leave()
+    side.finish()
+
+
+def back_kernel(
+    reply_ref, grad_ref, table_ref, parts_ref, forward_ref, backward_ref,
+    answers, message, landing, part, rows, *sems
+):
+    degrees = Wire(spectral_from, degree_owner, True, reply_ref, answers, sems[0:3])
+    panels = Wire(lat_to, lat_from, False, message, landing, sems[3:6])
+    side = Side(True, grad_ref, parts_ref, sems[6:9])
+    meet([degrees, panels, side])
+    degrees.start_all()
+    side.start()
+    degrees.arrive()
+    synthesis_kernel(answers, table_ref, message)
+    panels.start_all()
+    degrees.leave()
+    panels.arrive()
+    gather_kernel(landing, forward_ref, backward_ref, part, rows)
+    panels.leave()
+    side.finish()
+
+
+def link_sems(counts):
+    out = []
+    for count in counts:
+        out += [pltpu.SemaphoreType.DMA((count,))] * 2 + [pltpu.SemaphoreType.DMA]
+    return out
+
+
+def linked(kernel, collective_id, shapes, out_spaces, scratch, spaces, arrays):
+    def spec(space):
+        return pl.BlockSpec(memory_space=space)
+
+    return pl.pallas_call(
+        kernel,
         out_shape=shapes,
-        in_specs=[pl.BlockSpec(memory_space=pl.ANY)] * len(arrays),
-        out_specs=[pl.BlockSpec(memory_space=pl.ANY)] * len(arrays),
+        in_specs=[spec(space) for space in spaces],
+        out_specs=[spec(space) for space in out_spaces],
         scratch_shapes=scratch,
         compiler_params=pltpu.CompilerParams(
             collective_id=collective_id, has_side_effects=True, vmem_limit_bytes=VMEM_LIMIT
         ),
     )(*arrays)
-    return out if spread is not None else out[0]
 
 
 def with_halo(block):
@@ -522,21 +635,37 @@
         ],
         axis=1,
     )
-    message = local(
-        spread_kernel,
-        bf16(LAT, 10, ROWS, 128),
-        [pltpu.VMEM((4, flat, 128), jnp.float32), pltpu.VMEM((2, MMAX * ROWS, 128), jnp.float32)],
-        dot("ik,kn->in", source_field.reshape(flat, NLON), lon_analysis).astype(jnp.bfloat16),
-        dot("ik,kn->in", output_grad.reshape(flat, NLON), lon_synthesis).astype(jnp.bfloat16),
-        info,
-    )
-    columns, weight = exchange(
-        message, lat_to, lambda k, a, b: lat_to(LAT - k, a, b), 1, "whole", mixing_weight
-    )
-    band_rows = columns[:, 9]
-    near, far = legendre_tables(band_rows)
-    message = local(analysis_kernel, bf16(LAT, 64, 128), [], columns, near)
-    received = exchange(message, spectral_to, spectral_from, 2)
+    vmem, anywhere = pltpu.VMEM, pl.ANY
+    work = [vmem((4, flat, 128), jnp.float32), vmem((2, MMAX * ROWS, 128), jnp.float32)]
+    received, weight, band_rows, far = linked(
+        front_kernel,
+        1,
+        [
+            bf16(LAT, 64, 128),
+            bf16(CHAN, 6, channels, CHAN * channels),
+            bf16(LAT, ROWS, 128),
+            bf16(12, NLAT, 256),
+        ],
+        [anywhere, anywhere, vmem, vmem],
+        work
+        + [
+            vmem((4, 2048, 128), jnp.float32),
+            vmem((12, 256, NLAT), jnp.bfloat16),
+            vmem((LAT, 9, ROWS, 128), jnp.bfloat16),
+            vmem((LAT, 9, ROWS, 128), jnp.bfloat16),
+            vmem((LAT, ROWS, 128), jnp.bfloat16),
+            vmem((LAT, 64, 128), jnp.bfloat16),
+        ]
+        + link_sems([LAT, LAT, LAT, CHAN]),
+        [vmem, vmem, vmem, anywhere] + [vmem] * 4,
+        [
+            dot("ik,kn->in", source_field.reshape(flat, NLON), lon_analysis).astype(jnp.bfloat16),
+            dot("ik,kn->in", output_grad.reshape(flat, NLON), lon_synthesis).astype(jnp.bfloat16),
+            info,
+            mixing_weight,
+            *legendre_inputs(),
+        ],
+    )
 
     pick = np.zeros((CHAN, channels, CHAN, 64), np.float32)
     for e in range(CHAN):
@@ -552,18 +681,22 @@
         jnp.asarray(pick.astype(jnp.bfloat16)),
         jnp.asarray(pick.T.astype(jnp.bfloat16)),
     )
-    answers = exchange(reply, spectral_from, degree_owner, 3)
-    message = local(synthesis_kernel, bf16(LAT, 9, ROWS, 128), [], answers, far)
-    grids, grad_parts = exchange(
-        message, lat_to, lambda k, a, b: lat_to(LAT - k, a, b), 4, "parts", grad
+    grad_parts, forward, backward = linked(
+        back_kernel,
+        2,
+        [bf16(CHAN, 6, channels, CHAN * channels), bf16(flat, 512), bf16(flat, 512)],
+        [anywhere, vmem, vmem],
+        [
+            vmem((LAT, 64, 128), jnp.bfloat16),
+            vmem((LAT, 9, ROWS, 128), jnp.bfloat16),
+            vmem((LAT, 9, ROWS, 128), jnp.bfloat16),
+        ]
+        + work
+        + link_sems([LAT, LAT, CHAN]),
+        [anywhere, anywhere, vmem],
+        [reply, grad, far],
     )
     grad_mixing = jnp.sum(grad_parts.astype(jnp.float32), axis=0)
-    forward, backward = local(
-        gather_kernel,
-        [bf16(flat, 512), bf16(flat, 512)],
-        [pltpu.VMEM((4, flat, 128), jnp.float32), pltpu.VMEM((2, MMAX * ROWS, 128), jnp.float32)],
-        grids,
-    )
 
     rows = jnp.pad(band_rows.reshape(NLAT, 128), ((HALO, HALO), (0, 0)))
     rows = lax.dynamic_slice(rows, (lat * ROWS, 0), (ROWS + 4, 128)).astype(jnp.float32)

time: 214 us -> 180 us (0.84)
  Pallas kernels: 174 us -> 138 us
    pallas_call x6 -> x1, Pallas kernels: 35.4 us -> 7.03 us  [local(): pl.pallas_call(kernel, out_shape=shapes, in_specs=[spec] * len(arrays), o...]
    pallas_call x4 -> x2, Pallas kernels: 138 us -> 131 us  [linked(): pl.pallas_call(kernel, out_shape=shapes, in_specs=[spec(space) for space...]
  transfers between devices with their start and end apart: 4 -> 4, of which waited for: 0 -> 0; matrix products, arithmetic and copies ran while one was open for 8% -> 9% of each run, Pallas kernels for 81% -> 77%
where the time goes in v2:
time: 180 us; the launch traced here: 178 us
  Pallas kernels  138 us (77%)
  matrix products  15.8 us (9%)
  starting transfers between devices  15.2 us (8%)
  local copies, waits for them, and re-layouts  6.77 us (4%)
    pallas_call x2, Pallas kernels, linked(): pl.pallas_call(kernel, out_shape=shapes, in_specs=[spec(space) for space...  131 us
    dot_general x6, matrix products, dot(): return jnp.einsum(spec, a, b, preferred_element_type=jnp.float32)  15.8 us
    ppermute x2, starting transfers between devices, with_halo(): low = lax.ppermute(block[:, -HALO:], 'lat', forward)  11.3 us
    pallas_call x1, Pallas kernels, local(): pl.pallas_call(kernel, out_shape=shapes, in_specs=[spec] * len(arrays), o...  7.03 us
    slice x2, local copies, waits for them, and re-layouts, with_halo(): low = lax.ppermute(block[:, -HALO:], 'lat', forward)  5.97 us
    ppermute x2, starting transfers between devices, with_halo(): high = lax.ppermute(block[:, :HALO], 'lat', backward)  3.84 us
  transfers between devices with their start and end apart: 4, of which 0 were waited for; matrix products, arithmetic and copies ran while one was open for 9% of the time, Pallas kernels for 77%

profile of v2, /device:TPU:1, one launch (start us, length us, event | category | flops | bytes accessed | tf_op | source)
XLA Modules:
  0.0 178.4 jit_solution(319635911947389219)
XLA Ops:
  0.6 0.0 copy-start.16
  0.6 0.0 copy-start.7
  0.7 0.0 copy-start.11
  0.7 0.0 copy-start.12
  0.7 0.0 copy-start.10
  0.7 3.0 %fusion.79 = (bf16[48,2,1440]{2,1,0:T(2,128)(2,1)}, bf16[48,2,1440]{2,1,0:T(2,128)(2,1)}) fusion(bf16[48,16,1440]{2,1,0:T(8,128)(2,1)} %param.14), kind=kLoop, calls=%fused_computation.112 | loop fusion | bytes 1105920 | tf_op jit(solution)/shard_map/slice | solution.py:600
  3.7 6.2 %collective-permute-start = (bf16[48,2,1440]{2,1,0:T(2,128)(2,1)}, bf16[48,2,1440]{2,1,0:T(2,128)(2,1)}, u32[]{:S(2)}, u32[]{:S(2)}) collective-permute-start(bf16[48,2,1440]{2,1,0:T(2,128)(2,1)} %get-tuple-element.23), channel_id=1, source_target_pairs={{0,1},{1,2},{2,3},{3,4},{4,5},{5,6},{6,7},{7,8},{8,9},{9,10},{10,1... | collective-permute-start | bytes 829448 | tf_op jit(solution)/shard_map/ppermute | solution.py:600
  9.9 1.9 %collective-permute-start.1 = (bf16[48,2,1440]{2,1,0:T(2,128)(2,1)}, bf16[48,2,1440]{2,1,0:T(2,128)(2,1)}, u32[]{:S(2)}, u32[]{:S(2)}) collective-permute-start(bf16[48,2,1440]{2,1,0:T(2,128)(2,1)} %get-tuple-element.24), channel_id=1, source_target_pairs={{1,0},{2,1},{3,2},{4,3},{5,4},{6,5},{7,6},{8,7},{9,8},{10,9},{11,1... | collective-permute-start | bytes 829448 | tf_op jit(solution)/shard_map/ppermute | solution.py:601
  11.9 2.9 %fusion.78 = (bf16[48,2,1440]{2,1,0:T(2,128)(2,1)}, bf16[48,2,1440]{2,1,0:T(2,128)(2,1)}) fusion(bf16[48,16,1440]{2,1,0:T(8,128)(2,1)} %param.19), kind=kLoop, calls=%fused_computation.111 | loop fusion | bytes 1105920 | tf_op jit(solution)/shard_map/slice | solution.py:600
  14.8 5.1 %collective-permute-start.2 = (bf16[48,2,1440]{2,1,0:T(2,128)(2,1)}, bf16[48,2,1440]{2,1,0:T(2,128)(2,1)}, u32[]{:S(2)}, u32[]{:S(2)}) collective-permute-start(bf16[48,2,1440]{2,1,0:T(2,128)(2,1)} %get-tuple-element.21), channel_id=1, source_target_pairs={{0,1},{1,2},{2,3},{3,4},{4,5},{5,6},{6,7},{7,8},{8,9},{9,10},{10,1... | collective-permute-start | bytes 829448 | tf_op jit(solution)/shard_map/ppermute | solution.py:600
  19.9 1.9 %collective-permute-start.3 = (bf16[48,2,1440]{2,1,0:T(2,128)(2,1)}, bf16[48,2,1440]{2,1,0:T(2,128)(2,1)}, u32[]{:S(2)}, u32[]{:S(2)}) collective-permute-start(bf16[48,2,1440]{2,1,0:T(2,128)(2,1)} %get-tuple-element.22), channel_id=1, source_target_pairs={{1,0},{2,1},{3,2},{4,3},{5,4},{6,5},{7,6},{8,7},{9,8},{10,9},{11,1... | collective-permute-start | bytes 829448 | tf_op jit(solution)/shard_map/ppermute | solution.py:601
  21.9 0.0 copy-done.11
  21.9 0.0 copy-done.12
  21.9 0.1 copy.28
  22.0 0.1 copy.27
  22.1 0.0 copy-done.10
  22.1 0.1 copy.29
  22.2 0.0 copy-done.16
  22.2 0.1 dynamic_slice.6
  22.3 0.1 pad.14.clone
  22.4 0.0 copy-done.7
  22.4 2.9 %fusion.13.grad_ref = bf16[768,512]{1,0:T(8,128)(2,1)S(1)} fusion(bf16[768,1440]{1,0:T(8,128)(2,1)S(1)} %bitcast.73, bf16[1440,512]{1,0:T(8,128)(2,1)} %constant.33.clone), kind=kOutput, calls=%fused_computation.18 | convolution fusion | flops 1132855296 | bytes 4472832 | tf_op jit(solution)/shard_map/ik,kn->in/dot_general | solution.py:606
  25.3 0.0 copy-done.5
  25.3 0.0 copy-done.13
  25.3 0.0 copy-start.9
  25.3 0.0 copy-start.2
  25.3 0.0 copy-start.3
  25.4 0.0 copy-start.4
  25.4 1.4 fusion.12.source_ref
  26.7 0.0 copy-done.9
  26.8 0.0 copy-start
  26.8 0.0 copy-start.1
  26.8 0.1 add_exponential_fusion.sector_ref
  26.9 0.1 maximum_maximum_fusion.info_ref
  26.9 0.0 copy-done.2
  26.9 0.0 copy-done.3
  27.0 0.0 copy-done.4
  27.0 70.8 %shard_map.157 = (bf16[32,64,128]{2,1,0:T(8,128)(2,1)S(1)}, bf16[8,6,48,384]{3,2,1,0:T(8,128)(2,1)S(1)}, bf16[32,16,128]{2,1,0:T(8,128)(2,1)S(1)}, bf16[12,512,256]{2,1,0:T(8,128)(2,1)}) custom-call(bf16[768,512]{1,0:T(8,128)(2,1)S(1)} %fusion.12.source_ref, bf16[768,512]{1,0:T(8,128)(2,1)S(1)} %fusion.13.grad_ref, ...), custom_call_target="tpu_custom_call" | custom-call | tf_op jit(solution)/shard_map/pallas_call | solution.py:585
  97.8 0.1 copy.31
  97.9 0.1 fusion.14
  98.0 0.1 slice_bitcast_fusion.7
  98.1 0.1 slice_bitcast_fusion.8
  98.2 0.1 compare_bitcast_fusion.7
  98.3 0.0 copy-done
  98.3 0.0 copy-done.1
  98.3 7.0 %shard_map.158 = (bf16[32,64,128]{2,1,0:T(8,128)(2,1)S(1)}, bf16[8,6,48,384]{3,2,1,0:T(8,128)(2,1)S(1)}) custom-call(bf16[32,64,128]{2,1,0:T(8,128)(2,1)S(1)} %get-tuple-element.12.in_ref, bf16[8,6,48,384]{3,2,1,0:T(8,128)(2,1)S(1)} %get-tuple-element.13.weight_ref, bf16[384,512]{1,0:T(8,128)(2,1)S(1)} %copy-done.1, bf16[512,384]{1,0:T(8,128)(2,1)S(1)} %copy-done), custom_call_target="tpu_custom_call" | custom-call | tf_op jit(solution)/shard_map/pallas_call | solution.py:290
  105.3 0.0 copy-start.15
  105.3 60.4 %shard_map.159 = (bf16[8,6,48,384]{3,2,1,0:T(8,128)(2,1)S(1)}, bf16[768,512]{1,0:T(8,128)(2,1)S(1)}, bf16[768,512]{1,0:T(8,128)(2,1)S(1)}) custom-call(bf16[32,64,128]{2,1,0:T(8,128)(2,1)S(1)} %get-tuple-element.14.reply_ref, bf16[8,6,48,384]{3,2,1,0:T(8,128)(2,1)S(1)} %get-tuple-element.15.grad_ref, bf16[12,512,256]{2,1,0:T(8,128)(2,1)} %get-tuple-element.16.table_ref), custom_call_target="tpu_custom_call" | custom-call | tf_op jit(solution)/shard_map/pallas_call | solution.py:585
  165.7 0.0 copy-done.15
  165.7 0.0 copy-start.14
  165.7 1.4 fusion.80
  167.1 0.0 copy-done.14
  167.2 0.0 copy-start.6
  167.2 1.4 fusion.81
  168.6 1.0 convert_reduce_fusion
  169.6 0.0 collective-permute-done
  169.6 0.0 collective-permute-done.1
  169.6 0.0 copy-done.6
  169.6 0.0 copy-start.8
  169.6 4.4 %fusion.1 = bf16[48,16,1440]{2,1,0:T(8,128)(2,1)} fusion(f32[48,16,1440]{2,1,0:T(8,128)S(1)} %bitcast.75, bf16[48,2,1440]{2,1,0:T(2,128)(2,1)} %collective-permute-done.1, bf16[48,16,1440]{2,1,0:T(8,128)(2,1)S(1)} %copy-done.6, bf16[48,2,1440]{2,1,0:T(2,128)(2,1)} %collective-permute-done, f32[16]{0:T(128)S(1)} %get-tuple-element.37, ...), kind=kOutput, calls=%fused_computation.3 | convolution fusion | flops 54749120 | bytes 9400704 | tf_op jit(solution)/shard_map/ij,cjn->cin/dot_general | solution.py:606
  174.1 0.0 collective-permute-done.2
  174.1 0.0 collective-permute-done.3
  174.1 0.0 copy-done.8
  174.1 4.3 %fusion = bf16[48,16,1440]{2,1,0:T(8,128)(2,1)} fusion(f32[48,16,1440]{2,1,0:T(8,128)S(1)} %bitcast.74, bf16[48,2,1440]{2,1,0:T(2,128)(2,1)} %collective-permute-done.3, bf16[48,16,1440]{2,1,0:T(8,128)(2,1)S(1)} %copy-done.8, bf16[48,2,1440]{2,1,0:T(2,128)(2,1)} %collective-permute-done.2, f32[20]{0:T(128)S(1)} %get-tuple-element.30, ...), kind=kOutput, calls=%fused_computation.1 | convolution fusion | flops 54749120 | bytes 9400800 | tf_op jit(solution)/shard_map/ji,cjn->cin/dot_general | solution.py:606
  (9 shorter events, 0.0 us)
Async XLA Ops:
  0.6 21.6 %copy-start.16 = (f32[194]{0:T(256)S(1)}, f32[194]{0:T(256)}, u32[]{:S(2)}) copy-start(f32[194]{0:T(256)} %constant.12.clone) | copy-start | bytes 2332
  0.6 21.7 %copy-start.7 = (bf16[48,16,1440]{2,1,0:T(8,128)(2,1)S(1)}, bf16[48,16,1440]{2,1,0:T(8,128)(2,1)}, u32[]{:S(2)}) copy-start(bf16[48,16,1440]{2,1,0:T(8,128)(2,1)} %param.19) | copy-start | bytes 6635524
  0.7 21.2 %copy-start.11 = (s32[16]{0:T(128)S(1)}, s32[16]{0:T(128)}, u32[]{:S(2)}) copy-start(s32[16]{0:T(128)} %param.15) | copy-start | bytes 196
  0.7 21.3 %copy-start.12 = (s32[16]{0:T(128)S(1)}, s32[16]{0:T(128)}, u32[]{:S(2)}) copy-start(s32[16]{0:T(128)} %param.16) | copy-start | bytes 196
  0.7 21.5 %copy-start.10 = (bf16[16,4]{0,1:T(4,128)(2,1)S(1)}, bf16[16,4]{0,1:T(4,128)(2,1)}, u32[]{:S(2)}) copy-start(bf16[16,4]{0,1:T(4,128)(2,1)} %param.17) | copy-start | bytes 388
  3.7 165.9 %collective-permute-start = (bf16[48,2,1440]{2,1,0:T(2,128)(2,1)}, bf16[48,2,1440]{2,1,0:T(2,128)(2,1)}, u32[]{:S(2)}, u32[]{:S(2)}) collective-permute-start(bf16[48,2,1440]{2,1,0:T(2,128)(2,1)} %get-tuple-element.23), channel_id=1, source_target_pairs={{0,1},{1,2},{2,3},{3,4},{4,5},{5,6},{6,7},{7,8},{8,9},{9,10},{10,1... | collective-permute-start | bytes 829448 | tf_op jit(solution)/shard_map/ppermute | solution.py:600
  9.9 159.7 %collective-permute-start.1 = (bf16[48,2,1440]{2,1,0:T(2,128)(2,1)}, bf16[48,2,1440]{2,1,0:T(2,128)(2,1)}, u32[]{:S(2)}, u32[]{:S(2)}) collective-permute-start(bf16[48,2,1440]{2,1,0:T(2,128)(2,1)} %get-tuple-element.24), channel_id=1, source_target_pairs={{1,0},{2,1},{3,2},{4,3},{5,4},{6,5},{7,6},{8,7},{9,8},{10,9},{11,1... | collective-permute-start | bytes 829448 | tf_op jit(solution)/shard_map/ppermute | solution.py:601
  14.8 159.3 %collective-permute-start.2 = (bf16[48,2,1440]{2,1,0:T(2,128)(2,1)}, bf16[48,2,1440]{2,1,0:T(2,128)(2,1)}, u32[]{:S(2)}, u32[]{:S(2)}) collective-permute-start(bf16[48,2,1440]{2,1,0:T(2,128)(2,1)} %get-tuple-element.21), channel_id=1, source_target_pairs={{0,1},{1,2},{2,3},{3,4},{4,5},{5,6},{6,7},{7,8},{8,9},{9,10},{10,1... | collective-permute-start | bytes 829448 | tf_op jit(solution)/shard_map/ppermute | solution.py:600
  19.9 154.2 %collective-permute-start.3 = (bf16[48,2,1440]{2,1,0:T(2,128)(2,1)}, bf16[48,2,1440]{2,1,0:T(2,128)(2,1)}, u32[]{:S(2)}, u32[]{:S(2)}) collective-permute-start(bf16[48,2,1440]{2,1,0:T(2,128)(2,1)} %get-tuple-element.22), channel_id=1, source_target_pairs={{1,0},{2,1},{3,2},{4,3},{5,4},{6,5},{7,6},{8,7},{9,8},{10,9},{11,1... | collective-permute-start | bytes 829448 | tf_op jit(solution)/shard_map/ppermute | solution.py:601
  22.4 2.9 %copy-start.5 = (bf16[48,16,1440]{2,1,0:T(8,128)(2,1)S(1)}, bf16[48,16,1440]{2,1,0:T(8,128)(2,1)}, u32[]{:S(2)}) copy-start(bf16[48,16,1440]{2,1,0:T(8,128)(2,1)} %param.14) | copy-start | bytes 6635524
  22.4 2.9 %copy-start.13 = (bf16[1440,512]{1,0:T(8,128)(2,1)S(1)}, bf16[1440,512]{1,0:T(8,128)(2,1)}, u32[]{:S(2)}) copy-start(bf16[1440,512]{1,0:T(8,128)(2,1)} %constant.32.clone) | copy-start | bytes 4423684
  25.3 1.4 copy-start.9
  25.3 1.6 copy-start.2
  25.3 1.6 copy-start.3
  25.4 1.6 copy-start.4
  26.8 71.5 %copy-start = (bf16[512,384]{1,0:T(8,128)(2,1)S(1)}, bf16[512,384]{1,0:T(8,128)(2,1)}, u32[]{:S(2)}) copy-start(bf16[512,384]{1,0:T(8,128)(2,1)} %constant.17.clone.pick_t_ref) | copy-start | bytes 1179652
  26.8 71.5 %copy-start.1 = (bf16[384,512]{1,0:T(8,128)(2,1)S(1)}, bf16[384,512]{1,0:T(8,128)(2,1)}, u32[]{:S(2)}) copy-start(bf16[384,512]{1,0:T(8,128)(2,1)} %constant.16.clone.pick_ref) | copy-start | bytes 1179652
  105.3 60.4 %copy-start.15 = (bf16[1440,512]{1,0:T(8,128)(2,1)S(1)}, bf16[1440,512]{1,0:T(8,128)(2,1)}, u32[]{:S(2)}) copy-start(bf16[1440,512]{1,0:T(8,128)(2,1)} %constant.33.clone) | copy-start | bytes 4423684
  165.7 1.4 copy-start.14
  167.2 2.5 %copy-start.6 = (bf16[48,16,1440]{2,1,0:T(8,128)(2,1)S(1)}, bf16[48,16,1440]{2,1,0:T(8,128)(2,1)}, u32[]{:S(2)}) copy-start(bf16[48,16,1440]{2,1,0:T(8,128)(2,1)} %param.14) | copy-start | bytes 6635524
  169.6 4.5 %copy-start.8 = (bf16[48,16,1440]{2,1,0:T(8,128)(2,1)S(1)}, bf16[48,16,1440]{2,1,0:T(8,128)(2,1)}, u32[]{:S(2)}) copy-start(bf16[48,16,1440]{2,1,0:T(8,128)(2,1)} %param.19) | copy-start | bytes 6635524

commit v3 on v2

--- a/solution.py
+++ b/solution.py
@@ -118,7 +118,7 @@
         lax.fori_loop(0, ROWS, turn, 0)
 
     def send(step, carry):
-        d = lax.rem(link.lat + step, LAT)
+        d = wrap(link.lat + step, LAT)
         units = [
             rows[f, pl.ds(pl.multiple_of((d * 6 + m) * 16, 16), 16), :]
             for f in range(2)
@@ -314,13 +314,17 @@
     return order, jnp.asarray(cosine), sector, jnp.asarray(quadrature)
 
 
+def wrap(value, size):
+    return value - jnp.where(value >= size, size, 0)
+
+
 def lat_to(step, lat, chan):
-    other = lax.rem(lat + step, LAT)
+    other = wrap(lat + step, LAT)
     return other, chan, other, lat
 
 
 def spectral_to(step, lat, chan):
-    other = lax.rem(lat + step, LAT)
+    other = wrap(lat + step, LAT)
     group = 2 * lax.rem(lat, 4) + lax.rem(lax.div(lat, 4), 2)
     return other, group, other, chan * 4 + lax.div(lat, 8)
 
@@ -333,7 +337,7 @@
 
 
 def degree_owner(step, lat, chan):
-    other = lax.rem(lat + LAT - step, LAT)
+    other = wrap(lat + LAT - step, LAT)
     group = 2 * lax.rem(lat, 4) + lax.rem(lax.div(lat, 4), 2)
     return other, group, other, 0
 
@@ -492,28 +496,144 @@
 
 
 def whole_to(step, lat, chan):
-    other = lax.rem(lat + step, LAT)
+    other = wrap(lat + step, LAT)
     return other, chan, 0, lat
 
 
 def whole_from(step, lat, chan):
-    other = lax.rem(lat + LAT - step, LAT)
+    other = wrap(lat + LAT - step, LAT)
     return other, chan, other, lat
 
 
-class Whole(Wire):
+class Bulk(Wire):
+    def remote(self, pair, slot):
+        return pltpu.make_async_remote_copy(
+            src_ref=self.source.at[pair[2]],
+            dst_ref=self.target.at[slot],
+            send_sem=self.send_sem,
+            recv_sem=self.recv_sem,
+            device_id={"lat": pair[0], "chan": pair[1]},
+            device_id_type=MESH,
+        )
+
+    def local(self, pair):
+        return pltpu.make_async_copy(
+            self.source.at[pair[2]], self.target.at[pair[3]], self.recv_sem
+        )
+
+    def arrive(self):
+        pltpu.make_async_copy(self.target, self.target, self.recv_sem).wait()
+
+    def leave(self):
+        sent = self.target.at[pl.ds(0, LAT - 1)]
+        pltpu.make_async_copy(sent, sent, self.send_sem).wait()
+
+
+class Whole(Bulk):
     def remote(self, pair, slot):
         return pltpu.make_async_remote_copy(
             src_ref=self.source,
             dst_ref=self.target.at[slot],
-            send_sem=self.send_sem.at[pair[0]],
-            recv_sem=self.recv_sem.at[slot],
+            send_sem=self.send_sem,
+            recv_sem=self.recv_sem,
             device_id={"lat": pair[0], "chan": pair[1]},
             device_id_type=MESH,
         )
 
     def local(self, pair):
-        return pltpu.make_async_copy(self.source, self.target.at[pair[3]], self.own_sem)
+        return pltpu.make_async_copy(self.source, self.target.at[pair[3]], self.recv_sem)
+
+
+class Halo:
+    def __init__(self, source, target, send_sem, recv_sem):
+        self.lat, self.chan = lax.axis_index("lat"), lax.axis_index("chan")
+        self.source, self.target = source, target
+        self.send_sem, self.recv_sem = send_sem, recv_sem
+        self.up, self.down = self.lat < LAT - 1, self.lat > 0
+
+    def copy(self, way):
+        step = jnp.where(self.up, 1, -1) if way == 0 else jnp.where(self.down, -1, 1)
+        other = self.lat + step
+        return pltpu.make_async_remote_copy(
+            src_ref=self.source.at[way],
+            dst_ref=self.target.at[way],
+            send_sem=self.send_sem.at[way],
+            recv_sem=self.recv_sem.at[way],
+            device_id={"lat": other, "chan": self.chan},
+            device_id_type=MESH,
+        )
+
+    def start(self):
+        pl.when(self.up)(lambda: self.copy(0).start())
+        pl.when(self.down)(lambda: self.copy(1).start())
+
+    def arrive(self):
+        pl.when(self.down)(lambda: self.copy(0).wait_recv())
+        pl.when(self.up)(lambda: self.copy(1).wait_recv())
+
+    def leave(self):
+        pl.when(self.up)(lambda: self.copy(0).wait_send())
+        pl.when(self.down)(lambda: self.copy(1).wait_send())
+
+
+CHUNKS = [(k * 128, min(128, NLON - k * 128)) for k in range(12)]
+EDGES = (14, 15, 0, 1)
+
+
+def edge_rows(f, field, part, out_ref):
+    for k, (low, size) in enumerate(CHUNKS):
+        slot = k % 4
+        part[slot, :, :size] = field[:, low : low + size].astype(jnp.float32)
+        for r, i in enumerate(EDGES):
+            row = part[slot, pl.ds(i, 48, stride=16), :]
+            out_ref[r // 2, f, r % 2, :, low : low + size] = row[:, :size].astype(jnp.bfloat16)
+
+
+def band_block(info, target, source, same):
+    relative = (source - target).astype(jnp.float32) - info[:, 0:1]
+    total = jnp.zeros(relative.shape, jnp.float32)
+    for k in range(4):
+        keep = (relative == float(k)) & (info[:, 1:2] > float(k)) & same
+        total = total + jnp.where(keep, info[:, 2 + k : 3 + k], 0.0)
+    return total
+
+
+def halo_place(index):
+    edge = index // 16
+    return jnp.where(edge < 2, edge - HALO, edge + ROWS - HALO)
+
+
+def residuals(fields, edges, bands, outs):
+    lat = lax.axis_index("lat")
+    own = bands[lat].astype(jnp.float32)
+    below = bands[jnp.maximum(lat - 1, 0)].astype(jnp.float32)
+    above = bands[jnp.minimum(lat + 1, LAT - 1)].astype(jnp.float32)
+    own = jnp.concatenate([own] * 16, axis=0)
+    near = [below[14:15], below[15:16], above[0:1], above[1:2]]
+    near = jnp.concatenate([jnp.broadcast_to(x, (16, 128)) for x in near], axis=0)
+
+    row, column = iota((256, 256), 0), iota((256, 256), 1)
+    inner = band_block(own, row % 16, column % 16, row // 16 == column // 16)
+    row, column = iota((256, 64), 0), iota((256, 64), 1)
+    outer = band_block(own, row % 16, halo_place(column), row // 16 == column % 16)
+    row, column = iota((64, 256), 0), iota((64, 256), 1)
+    outer_back = band_block(near, halo_place(row), column % 16, row % 16 == column // 16)
+    left = (
+        (inner.astype(jnp.bfloat16), outer.astype(jnp.bfloat16)),
+        (inner.T.astype(jnp.bfloat16), outer_back.T.astype(jnp.bfloat16)),
+    )
+    for low, size in ((0, 512), (512, 512), (1024, 416)):
+        live = (lat > 0, lat < LAT - 1)
+        for b in range(3):
+            for f in range(2):
+                rim = [
+                    jnp.where(live[r // 2], edges[r // 2, f, r % 2, 16 * b : 16 * b + 16, low : low + size].astype(jnp.float32), 0.0)
+                    for r in range(4)
+                ]
+                rim = jnp.concatenate(rim, axis=0).astype(jnp.bfloat16)
+                rows = slice(256 * b, 256 * b + 256)
+                value = dense(left[f][0], fields[f][rows, low : low + size]) + dense(left[f][1], rim)
+                outs[f][rows, low : low + size] = value.astype(jnp.bfloat16)
 
 
 def meet(links):
@@ -525,39 +645,63 @@
 
 
 def front_kernel(
-    source_ref, grad_ref, info_ref, weight_ref, order_ref, cosine_ref, sector_ref, quad_ref,
-    out_ref, weights_ref, bands_ref, far_ref,
-    part, rows, table, near, message, landing, bands, spectral, *sems
+    source_ref, grad_ref, info_ref, weight_ref, source_hbm, grad_hbm,
+    order_ref, cosine_ref, sector_ref, quad_ref,
+    out_ref, weights_ref, ahead_ref, behind_ref, far_ref,
+    part, rows, table, near, message, landing, bands, spectral,
+    fields, sums, edges, rim, field_sem, sum_sem, edge_send, edge_recv,
+    info_send, info_recv, panel_send, panel_recv, *sems
 ):
-    panels = Wire(lat_to, lat_from, False, message, landing, sems[0:3])
-    degrees = Wire(spectral_to, spectral_from, True, spectral, out_ref, sems[3:6])
-    info = Whole(whole_to, whole_from, False, info_ref, bands, sems[6:9])
-    side = Side(False, weight_ref, weights_ref, sems[9:12])
-    meet([panels, degrees, info, side])
+    panels = Bulk(lat_to, lat_from, False, message, landing, (panel_send, panel_recv, None))
+    degrees = Wire(spectral_to, spectral_from, True, spectral, out_ref, sems[0:3])
+    info = Whole(whole_to, whole_from, False, info_ref, bands, (info_send, info_recv, None))
+    side = Side(False, weight_ref, weights_ref, sems[3:6])
+    halo = Halo(edges, rim, edge_send, edge_recv)
+    loads = [
+        pltpu.make_async_copy(ref, fields.at[f], field_sem.at[f])
+        for f, ref in ((0, source_hbm), (1, grad_hbm))
+    ]
+    stores = [
+        pltpu.make_async_copy(sums.at[f], ref, sum_sem.at[f])
+        for f, ref in ((0, ahead_ref), (1, behind_ref))
+    ]
+    for load in loads:
+        load.start()
+    meet([panels, degrees, side])
+    info.start_all()
     side.start()
-    info.start_all()
     spread_kernel(source_ref, grad_ref, message, part, rows, panels)
+    for f in range(2):
+        loads[f].wait()
+        edge_rows(f, fields.at[f], part, edges)
+    halo.start()
     recurrence(order_ref, cosine_ref, sector_ref, table)
     info.arrive()
     finish_tables(quad_ref, bands, near, far_ref, table)
-    bands_ref[...] = bands[...]
+    halo.arrive()
+    residuals([fields.at[0], fields.at[1]], rim, bands, [sums.at[0], sums.at[1]])
+    for store in stores:
+        store.start()
     panels.arrive()
     analysis_kernel(landing, near, spectral)
     degrees.start_all()
     info.leave()
     panels.leave()
+    halo.leave()
     degrees.arrive()
     degrees.leave()
     side.finish()
+    for store in stores:
+        store.wait()
 
 
 def back_kernel(
     reply_ref, grad_ref, table_ref, parts_ref, forward_ref, backward_ref,
-    answers, message, landing, part, rows, *sems
+    answers, message, landing, part, rows, panel_send, panel_recv, *sems
 ):
     degrees = Wire(spectral_from, degree_owner, True, reply_ref, answers, sems[0:3])
-    panels = Wire(lat_to, lat_from, False, message, landing, sems[3:6])
-    side = Side(True, grad_ref, parts_ref, sems[6:9])
+    panels = Bulk(lat_to, lat_from, False, message, landing, (panel_send, panel_recv, None))
+    side = Side(True, grad_ref, parts_ref, sems[3:6])
     meet([degrees, panels, side])
     degrees.start_all()
     side.start()
@@ -594,32 +738,11 @@
     )(*arrays)
 
 
-def with_halo(block):
-    forward = [(i, i + 1) for i in range(LAT - 1)]
-    backward = [(i + 1, i) for i in range(LAT - 1)]
-    low = lax.ppermute(block[:, -HALO:], "lat", forward)
-    high = lax.ppermute(block[:, :HALO], "lat", backward)
-    return jnp.concatenate([low, block, high], axis=1)
-
-
 def dot(spec, a, b):
     return jnp.einsum(spec, a, b, preferred_element_type=jnp.float32)
 
 
-def local_band(start, width, coef, low):
-    count = start.shape[0]
-    target = jnp.arange(count, dtype=jnp.int32)[:, None]
-    source = jnp.arange(ROWS + 4 if low else ROWS, dtype=jnp.int32)[None, :]
-    relative = source - target - (HALO if low else -HALO) - start[:, None]
-    matrix = jnp.zeros(relative.shape, jnp.float32)
-    for offset in range(4):
-        keep = (relative == offset) & (width[:, None] > offset)
-        matrix = matrix + jnp.where(keep, coef[:, offset : offset + 1], 0.0)
-    return matrix.astype(jnp.bfloat16)
-
-
 def per_device(source_field, band_start, band_width, band_coef, mixing_weight, output_grad):
-    lat = lax.axis_index("lat")
     channels = source_field.shape[0]
     table = fourier_table()
     lon_analysis = jnp.asarray((table / math.sqrt(NLON)).astype(jnp.bfloat16))
@@ -637,16 +760,17 @@
     )
     vmem, anywhere = pltpu.VMEM, pl.ANY
     work = [vmem((4, flat, 128), jnp.float32), vmem((2, MMAX * ROWS, 128), jnp.float32)]
-    received, weight, band_rows, far = linked(
+    received, weight, ahead, behind, far = linked(
         front_kernel,
         1,
         [
             bf16(LAT, 64, 128),
             bf16(CHAN, 6, channels, CHAN * channels),
-            bf16(LAT, ROWS, 128),
+            bf16(flat, NLON),
+            bf16(flat, NLON),
             bf16(12, NLAT, 256),
         ],
-        [anywhere, anywhere, vmem, vmem],
+        [anywhere] * 4 + [vmem],
         work
         + [
             vmem((4, 2048, 128), jnp.float32),
@@ -655,14 +779,22 @@
             vmem((LAT, 9, ROWS, 128), jnp.bfloat16),
             vmem((LAT, ROWS, 128), jnp.bfloat16),
             vmem((LAT, 64, 128), jnp.bfloat16),
+            vmem((2, flat, NLON), jnp.bfloat16),
+            vmem((2, flat, NLON), jnp.bfloat16),
+            vmem((2, 2, 2, channels, NLON), jnp.bfloat16),
+            vmem((2, 2, 2, channels, NLON), jnp.bfloat16),
         ]
-        + link_sems([LAT, LAT, LAT, CHAN]),
-        [vmem, vmem, vmem, anywhere] + [vmem] * 4,
+        + [pltpu.SemaphoreType.DMA((2,))] * 4
+        + [pltpu.SemaphoreType.DMA] * 4
+        + link_sems([LAT, CHAN]),
+        [vmem, vmem, vmem] + [anywhere] * 3 + [vmem] * 4,
         [
             dot("ik,kn->in", source_field.reshape(flat, NLON), lon_analysis).astype(jnp.bfloat16),
             dot("ik,kn->in", output_grad.reshape(flat, NLON), lon_synthesis).astype(jnp.bfloat16),
             info,
             mixing_weight,
+            source_field.reshape(flat, NLON),
+            output_grad.reshape(flat, NLON),
             *legendre_inputs(),
         ],
     )
@@ -692,25 +824,21 @@
             vmem((LAT, 9, ROWS, 128), jnp.bfloat16),
         ]
         + work
-        + link_sems([LAT, LAT, CHAN]),
+        + [pltpu.SemaphoreType.DMA] * 2
+        + link_sems([LAT, CHAN]),
         [anywhere, anywhere, vmem],
         [reply, grad, far],
     )
     grad_mixing = jnp.sum(grad_parts.astype(jnp.float32), axis=0)
 
-    rows = jnp.pad(band_rows.reshape(NLAT, 128), ((HALO, HALO), (0, 0)))
-    rows = lax.dynamic_slice(rows, (lat * ROWS, 0), (ROWS + 4, 128)).astype(jnp.float32)
-    start, width, coef = rows[:, 0].astype(jnp.int32), rows[:, 1].astype(jnp.int32), rows[:, 2:6]
-    own = slice(HALO, HALO + ROWS)
-    band_ahead = local_band(start[own], width[own], coef[own], True)
-    band_back = local_band(start, width, coef, False)
-    mixed_field = dot("ik,nk->in", forward, lon_synthesis).reshape(channels, ROWS, NLON) + dot(
-        "ij,cjn->cin", band_ahead, with_halo(source_field)
-    )
-    grad_input = dot("ik,nk->in", backward, lon_analysis).reshape(channels, ROWS, NLON) + dot(
-        "ji,cjn->cin", band_back, with_halo(output_grad)
-    )
-    return (mixed_field.astype(jnp.bfloat16), grad_input.astype(jnp.bfloat16), grad_mixing)
+    shape = (channels, ROWS, NLON)
+    mixed_field = dot("ik,nk->in", forward, lon_synthesis) + ahead.astype(jnp.float32)
+    grad_input = dot("ik,nk->in", backward, lon_analysis) + behind.astype(jnp.float32)
+    return (
+        mixed_field.astype(jnp.bfloat16).reshape(shape),
+        grad_input.astype(jnp.bfloat16).reshape(shape),
+        grad_mixing,
+    )
 
 
 def solution(mesh):

time: 180 us -> 170 us (0.944)
  the two profiles are of different devices: /device:TPU:1 before, /device:TPU:25 now
where the time goes in v3:
time: 170 us
  Pallas kernels  153 us (90%)
  matrix products  10.7 us (6%)
  other arithmetic  3.17 us (2%)
  local copies, waits for them, and re-layouts  1.86 us (1%)
    pallas_call x2, Pallas kernels, linked(): pl.pallas_call(kernel, out_shape=shapes, in_specs=[spec(space) for space...  146 us
    dot_general x4, matrix products, dot(): return jnp.einsum(spec, a, b, preferred_element_type=jnp.float32)  10.7 us
    pallas_call x1, Pallas kernels, local(): pl.pallas_call(kernel, out_shape=shapes, in_specs=[spec] * len(arrays), o...  7.04 us

profile of v3, /device:TPU:25, one launch (start us, length us, event | category | flops | bytes accessed | tf_op | source)
XLA Modules:
  0.0 169.6 jit_solution(17567532349609832759)
XLA Ops:
  0.6 0.8 dynamic_slice.3
  1.4 0.7 convert_bitcast_fusion.1
  2.1 0.7 convert_bitcast_fusion
  2.7 0.1 pad.3.clone
  2.8 0.1 copy.20
  2.9 0.1 copy.19
  3.0 0.8 copy.21
  3.8 0.1 maximum_maximum_fusion.info_ref
  3.8 0.8 add_exponential_fusion.sector_ref
  4.6 0.0 copy-start.5
  4.6 0.0 copy-start.9
  4.6 3.6 %fusion.source_ref = bf16[768,512]{1,0:T(8,128)(2,1)S(1)} fusion(bf16[768,1440]{1,0:T(8,128)(2,1)} %bitcast.20, bf16[1440,512]{1,0:T(8,128)(2,1)} %constant.30.clone), kind=kOutput, calls=%fused_computation.5 | convolution fusion | flops 1132855296 | bytes 4472832 | tf_op jit(solution)/shard_map/ik,kn->in/dot_general | solution.py:742
  8.2 0.0 copy-done.5
  8.2 0.0 copy-done.9
  8.3 0.0 copy-start.2
  8.3 0.0 copy-start.3
  8.3 0.0 copy-start.4
  8.3 1.4 fusion.1.grad_ref
  9.7 0.0 copy-done.2
  9.7 0.0 copy-done.3
  9.7 0.0 copy-done.4
  9.7 0.0 copy-start
  9.7 0.0 copy-start.1
  9.7 79.6 %shard_map.157 = (bf16[32,64,128]{2,1,0:T(8,128)(2,1)S(1)}, bf16[8,6,48,384]{3,2,1,0:T(8,128)(2,1)S(1)}, bf16[768,1440]{1,0:T(8,128)(2,1)}, bf16[768,1440]{1,0:T(8,128)(2,1)}, bf16[12,512,256]{2,1,0:T(8,128)(2,1)}) custom-call(bf16[768,512]{1,0:T(8,128)(2,1)S(1)} %fusion.source_ref, bf16[768,512]{1,0:T(8,128)(2,1)S(1)} %fusion.1.grad_ref, ...), custom_call_target="tpu_custom_call" | custom-call | tf_op jit(solution)/shard_map/pallas_call | solution.py:729
  89.3 0.0 copy-done
  89.3 0.0 copy-done.1
  89.3 7.0 %shard_map.158 = (bf16[32,64,128]{2,1,0:T(8,128)(2,1)S(1)}, bf16[8,6,48,384]{3,2,1,0:T(8,128)(2,1)S(1)}) custom-call(bf16[32,64,128]{2,1,0:T(8,128)(2,1)S(1)} %get-tuple-element.13.in_ref, bf16[8,6,48,384]{3,2,1,0:T(8,128)(2,1)S(1)} %get-tuple-element.14.weight_ref, bf16[384,512]{1,0:T(8,128)(2,1)S(1)} %copy-done.1, bf16[512,384]{1,0:T(8,128)(2,1)S(1)} %copy-done), custom_call_target="tpu_custom_call" | custom-call | tf_op jit(solution)/shard_map/pallas_call | solution.py:290
  96.4 0.0 copy-start.7
  96.4 66.5 %shard_map.159 = (bf16[8,6,48,384]{3,2,1,0:T(8,128)(2,1)S(1)}, bf16[768,512]{1,0:T(8,128)(2,1)S(1)}, bf16[768,512]{1,0:T(8,128)(2,1)S(1)}) custom-call(bf16[32,64,128]{2,1,0:T(8,128)(2,1)S(1)} %get-tuple-element.15.reply_ref, bf16[8,6,48,384]{3,2,1,0:T(8,128)(2,1)S(1)} %get-tuple-element.16.grad_ref, bf16[12,512,256]{2,1,0:T(8,128)(2,1)} %get-tuple-element.17.table_ref), custom_call_target="tpu_custom_call" | custom-call | tf_op jit(solution)/shard_map/pallas_call | solution.py:729
  162.9 0.0 copy-done.7
  162.9 0.0 copy-start.6
  162.9 0.0 copy-start.8
  162.9 2.8 %add_convert_fusion.1 = bf16[768,1440]{1,0:T(8,128)(2,1)} fusion(bf16[768,1440]{1,0:T(8,128)(2,1)S(1)} %copy-done.7, bf16[768,512]{1,0:T(8,128)(2,1)S(1)} %get-tuple-element.18, bf16[1440,512]{1,0:T(8,128)(2,1)S(1)} %copy-done.9), kind=kOutput, calls=%fused_computation.1 | convolution fusion | flops 1135779840 | bytes 6684672 | tf_op jit(solution)/shard_map/ik,nk->in/dot_general | solution.py:742
  165.7 0.0 copy-done.6
  165.7 0.0 copy-done.8
  165.7 2.9 %add_convert_fusion = bf16[768,1440]{1,0:T(8,128)(2,1)} fusion(bf16[768,1440]{1,0:T(8,128)(2,1)S(1)} %copy-done.6, bf16[768,512]{1,0:T(8,128)(2,1)S(1)} %get-tuple-element.20, bf16[1440,512]{1,0:T(8,128)(2,1)S(1)} %copy-done.8), kind=kOutput, calls=%fused_computation | convolution fusion | flops 1135779840 | bytes 6684672 | tf_op jit(solution)/shard_map/ik,nk->in/dot_general | solution.py:742
  168.6 1.0 convert_reduce_fusion
  (3 shorter events, 0.0 us)
Async XLA Ops:
  4.6 3.6 %copy-start.5 = (bf16[48,16,1440]{2,1,0:T(8,128)(2,1)S(1)}, bf16[48,16,1440]{2,1,0:T(8,128)(2,1)}, u32[]{:S(2)}) copy-start(bf16[48,16,1440]{2,1,0:T(8,128)(2,1)} %param.19) | copy-start | bytes 6635524
  4.6 3.6 %copy-start.9 = (bf16[1440,512]{1,0:T(8,128)(2,1)S(1)}, bf16[1440,512]{1,0:T(8,128)(2,1)}, u32[]{:S(2)}) copy-start(bf16[1440,512]{1,0:T(8,128)(2,1)} %constant.31.clone) | copy-start | bytes 4423684
  8.3 1.4 copy-start.2
  8.3 1.4 copy-start.3
  8.3 1.4 copy-start.4
  9.7 79.6 %copy-start = (bf16[512,384]{1,0:T(8,128)(2,1)S(1)}, bf16[512,384]{1,0:T(8,128)(2,1)}, u32[]{:S(2)}) copy-start(bf16[512,384]{1,0:T(8,128)(2,1)} %constant.37.clone.pick_t_ref) | copy-start | bytes 1179652
  9.7 79.6 %copy-start.1 = (bf16[384,512]{1,0:T(8,128)(2,1)S(1)}, bf16[384,512]{1,0:T(8,128)(2,1)}, u32[]{:S(2)}) copy-start(bf16[384,512]{1,0:T(8,128)(2,1)} %constant.36.clone.pick_ref) | copy-start | bytes 1179652
  96.4 66.5 %copy-start.7 = (bf16[768,1440]{1,0:T(8,128)(2,1)S(1)}, bf16[768,1440]{1,0:T(8,128)(2,1)}, u32[]{:S(2)}) copy-start(bf16[768,1440]{1,0:T(8,128)(2,1)} %get-tuple-element.19) | copy-start | bytes 6635524
  162.9 2.9 %copy-start.6 = (bf16[768,1440]{1,0:T(8,128)(2,1)S(1)}, bf16[768,1440]{1,0:T(8,128)(2,1)}, u32[]{:S(2)}) copy-start(bf16[768,1440]{1,0:T(8,128)(2,1)} %get-tuple-element.21) | copy-start | bytes 6635524
  162.9 2.8 %copy-start.8 = (bf16[1440,512]{1,0:T(8,128)(2,1)S(1)}, bf16[1440,512]{1,0:T(8,128)(2,1)}, u32[]{:S(2)}) copy-start(bf16[1440,512]{1,0:T(8,128)(2,1)} %constant.30.clone) | copy-start | bytes 4423684

commit v4 on v3

--- a/solution.py
+++ b/solution.py
@@ -19,7 +19,7 @@
 MODES = MMAX // LAT
 ROWS = NLAT // LAT
 MESH = pl.DeviceIdType.MESH
-VMEM_LIMIT = 48 * 1024 * 1024
+VMEM_LIMIT = 58 * 1024 * 1024
 
 
 def log_norms():
@@ -232,7 +232,18 @@
             out_ref[:, 3 * g + k] = tiles[k].reshape(LAT, ROWS, 128).astype(jnp.bfloat16)
 
 
-def mixing_kernel(in_ref, weight_ref, pick_ref, pick_t_ref, out_ref, grad_ref, before, after):
+def widen(weight_ref, pick_ref, wide):
+    def degree(l, carry):
+        rows = []
+        for e in range(CHAN):
+            rows += [weight_ref[e, l], jnp.zeros((16, 384), jnp.bfloat16)]
+        wide[l] = dense(jnp.concatenate(rows, axis=0), pick_ref[...]).astype(jnp.bfloat16)
+        return carry
+
+    lax.fori_loop(0, 6, degree, 0)
+
+
+def mixing_kernel(in_ref, wide, pick_t_ref, out_ref, grad_ref, before, after):
     lat, chan = lax.axis_index("lat"), lax.axis_index("chan")
     slot = iota((LAT, 16, 128), 0)
     other = (2 * (slot % 4) + lax.rem(chan, 2)) * 4 + lax.div(chan, 2)
@@ -256,10 +267,7 @@
                 second = jnp.where(lane < 64, pltpu.roll(a, 80, 1), pltpu.roll(b, 16, 1))
                 columns.append(jnp.concatenate([first, second], axis=0))
             left.append(jnp.concatenate(columns, axis=1).astype(jnp.bfloat16))
-        rows = []
-        for e in range(CHAN):
-            rows += [weight_ref[e, l], jnp.zeros((16, 384), jnp.bfloat16)]
-        weight = dense(jnp.concatenate(rows, axis=0), pick_ref[...]).astype(jnp.bfloat16)
+        weight = wide[l]
         mixed = dense(left[0], weight)
         back = dense(left[1], weight, ((1,), (1,)))
         dense_back = dense(left[1], pick_t_ref[...]).astype(jnp.bfloat16)
@@ -282,19 +290,6 @@
         a, b, c, d = units[4 * g : 4 * g + 4]
         packed += merge_lanes(a, pltpu.roll(b, 96, 1), pltpu.roll(c, 64, 1), pltpu.roll(d, 32, 1))
     store_rows(out_ref, merge_rows(packed))
-
-
-def local(kernel, shapes, scratch, *arrays):
-    single = not isinstance(shapes, list)
-    spec = pl.BlockSpec(memory_space=pltpu.VMEM)
-    return pl.pallas_call(
-        kernel,
-        out_shape=shapes,
-        in_specs=[spec] * len(arrays),
-        out_specs=spec if single else [spec] * len(shapes),
-        scratch_shapes=scratch,
-        compiler_params=pltpu.CompilerParams(vmem_limit_bytes=VMEM_LIMIT),
-    )(*arrays)
 
 
 def bf16(*shape):
@@ -644,18 +639,22 @@
     pl.semaphore_wait(barrier, total)
 
 
-def front_kernel(
+def block_kernel(
     source_ref, grad_ref, info_ref, weight_ref, source_hbm, grad_hbm,
-    order_ref, cosine_ref, sector_ref, quad_ref,
-    out_ref, weights_ref, ahead_ref, behind_ref, far_ref,
-    part, rows, table, near, message, landing, bands, spectral,
+    order_ref, cosine_ref, sector_ref, quad_ref, pick_ref, pick_t_ref,
+    parts_ref, ahead_ref, behind_ref, forward_ref, backward_ref,
+    part, rows, table, near, far, message, landing, bands, spectral, received,
+    weights, wide, before, after, reply, grads, answers, grids,
     fields, sums, edges, rim, field_sem, sum_sem, edge_send, edge_recv,
-    info_send, info_recv, panel_send, panel_recv, *sems
+    info_send, info_recv, panel_send, panel_recv, grid_send, grid_recv, *sems
 ):
     panels = Bulk(lat_to, lat_from, False, message, landing, (panel_send, panel_recv, None))
-    degrees = Wire(spectral_to, spectral_from, True, spectral, out_ref, sems[0:3])
+    grid_panels = Bulk(lat_to, lat_from, False, message, grids, (grid_send, grid_recv, None))
+    degrees = Wire(spectral_to, spectral_from, True, spectral, received, sems[0:3])
+    replies = Wire(spectral_from, degree_owner, True, reply, answers, sems[3:6])
     info = Whole(whole_to, whole_from, False, info_ref, bands, (info_send, info_recv, None))
-    side = Side(False, weight_ref, weights_ref, sems[3:6])
+    side = Side(False, weight_ref, weights, sems[6:9])
+    grad_side = Side(True, grads, parts_ref, sems[9:12])
     halo = Halo(edges, rim, edge_send, edge_recv)
     loads = [
         pltpu.make_async_copy(ref, fields.at[f], field_sem.at[f])
@@ -667,7 +666,7 @@
     ]
     for load in loads:
         load.start()
-    meet([panels, degrees, side])
+    meet([panels, degrees, replies, side])
     info.start_all()
     side.start()
     spread_kernel(source_ref, grad_ref, message, part, rows, panels)
@@ -677,7 +676,7 @@
     halo.start()
     recurrence(order_ref, cosine_ref, sector_ref, table)
     info.arrive()
-    finish_tables(quad_ref, bands, near, far_ref, table)
+    finish_tables(quad_ref, bands, near, far, table)
     halo.arrive()
     residuals([fields.at[0], fields.at[1]], rim, bands, [sums.at[0], sums.at[1]])
     for store in stores:
@@ -685,34 +684,26 @@
     panels.arrive()
     analysis_kernel(landing, near, spectral)
     degrees.start_all()
+    side.finish()
+    widen(weights, pick_ref, wide)
     info.leave()
     panels.leave()
     halo.leave()
     degrees.arrive()
+    mixing_kernel(received, wide, pick_t_ref, reply, grads, before, after)
+    replies.start_all()
     degrees.leave()
-    side.finish()
+    replies.arrive()
+    synthesis_kernel(answers, far, message)
+    grid_panels.start_all()
+    grad_side.start()
+    replies.leave()
+    grid_panels.arrive()
+    gather_kernel(grids, forward_ref, backward_ref, part, rows)
+    grid_panels.leave()
+    grad_side.finish()
     for store in stores:
         store.wait()
-
-
-def back_kernel(
-    reply_ref, grad_ref, table_ref, parts_ref, forward_ref, backward_ref,
-    answers, message, landing, part, rows, panel_send, panel_recv, *sems
-):
-    degrees = Wire(spectral_from, degree_owner, True, reply_ref, answers, sems[0:3])
-    panels = Bulk(lat_to, lat_from, False, message, landing, (panel_send, panel_recv, None))
-    side = Side(True, grad_ref, parts_ref, sems[3:6])
-    meet([degrees, panels, side])
-    degrees.start_all()
-    side.start()
-    degrees.arrive()
-    synthesis_kernel(answers, table_ref, message)
-    panels.start_all()
-    degrees.leave()
-    panels.arrive()
-    gather_kernel(landing, forward_ref, backward_ref, part, rows)
-    panels.leave()
-    side.finish()
 
 
 def link_sems(counts):
@@ -759,35 +750,56 @@
         axis=1,
     )
     vmem, anywhere = pltpu.VMEM, pl.ANY
-    work = [vmem((4, flat, 128), jnp.float32), vmem((2, MMAX * ROWS, 128), jnp.float32)]
-    received, weight, ahead, behind, far = linked(
-        front_kernel,
+    pick = np.zeros((CHAN, channels, CHAN, 64), np.float32)
+    for e in range(CHAN):
+        pick[e, :, e, :channels] = np.eye(channels)
+    pick = pick.reshape(CHAN * channels, 512)
+
+    def held(*shape):
+        return vmem(shape, jnp.bfloat16)
+
+    def panel(*shape):
+        return vmem(shape, jnp.float32)
+
+    grad_parts, ahead, behind, forward, backward = linked(
+        block_kernel,
         1,
         [
-            bf16(LAT, 64, 128),
             bf16(CHAN, 6, channels, CHAN * channels),
             bf16(flat, NLON),
             bf16(flat, NLON),
-            bf16(12, NLAT, 256),
+            bf16(flat, 512),
+            bf16(flat, 512),
         ],
-        [anywhere] * 4 + [vmem],
-        work
-        + [
-            vmem((4, 2048, 128), jnp.float32),
-            vmem((12, 256, NLAT), jnp.bfloat16),
-            vmem((LAT, 9, ROWS, 128), jnp.bfloat16),
-            vmem((LAT, 9, ROWS, 128), jnp.bfloat16),
-            vmem((LAT, ROWS, 128), jnp.bfloat16),
-            vmem((LAT, 64, 128), jnp.bfloat16),
-            vmem((2, flat, NLON), jnp.bfloat16),
-            vmem((2, flat, NLON), jnp.bfloat16),
-            vmem((2, 2, 2, channels, NLON), jnp.bfloat16),
-            vmem((2, 2, 2, channels, NLON), jnp.bfloat16),
+        [anywhere] * 3 + [vmem] * 2,
+        [
+            panel(4, flat, 128),
+            panel(2, MMAX * ROWS, 128),
+            panel(4, 2048, 128),
+            held(12, 256, NLAT),
+            held(12, NLAT, 256),
+            held(LAT, 9, ROWS, 128),
+            held(LAT, 9, ROWS, 128),
+            held(LAT, ROWS, 128),
+            held(LAT, 64, 128),
+            held(LAT, 64, 128),
+            held(CHAN, 6, channels, CHAN * channels),
+            held(6, 512, 512),
+            panel(2, CHAN, 192, 128),
+            panel(2, CHAN, 192, 128),
+            held(LAT, 64, 128),
+            held(CHAN, 6, channels, CHAN * channels),
+            held(LAT, 64, 128),
+            held(LAT, 9, ROWS, 128),
+            held(2, flat, NLON),
+            held(2, flat, NLON),
+            held(2, 2, 2, channels, NLON),
+            held(2, 2, 2, channels, NLON),
         ]
         + [pltpu.SemaphoreType.DMA((2,))] * 4
-        + [pltpu.SemaphoreType.DMA] * 4
-        + link_sems([LAT, CHAN]),
-        [vmem, vmem, vmem] + [anywhere] * 3 + [vmem] * 4,
+        + [pltpu.SemaphoreType.DMA] * 6
+        + link_sems([LAT, LAT, CHAN, CHAN]),
+        [vmem, vmem, vmem] + [anywhere] * 3 + [vmem] * 6,
         [
             dot("ik,kn->in", source_field.reshape(flat, NLON), lon_analysis).astype(jnp.bfloat16),
             dot("ik,kn->in", output_grad.reshape(flat, NLON), lon_synthesis).astype(jnp.bfloat16),
@@ -796,38 +808,9 @@
             source_field.reshape(flat, NLON),
             output_grad.reshape(flat, NLON),
             *legendre_inputs(),
+            jnp.asarray(pick.astype(jnp.bfloat16)),
+            jnp.asarray(pick.T.astype(jnp.bfloat16)),
         ],
-    )
-
-    pick = np.zeros((CHAN, channels, CHAN, 64), np.float32)
-    for e in range(CHAN):
-        pick[e, :, e, :channels] = np.eye(channels)
-    pick = pick.reshape(CHAN * channels, 512)
-    panel = pltpu.VMEM((2, CHAN, 192, 128), jnp.float32)
-    reply, grad = local(
-        mixing_kernel,
-        [bf16(LAT, 64, 128), bf16(CHAN, 6, channels, CHAN * channels)],
-        [panel, panel],
-        received,
-        weight,
-        jnp.asarray(pick.astype(jnp.bfloat16)),
-        jnp.asarray(pick.T.astype(jnp.bfloat16)),
-    )
-    grad_parts, forward, backward = linked(
-        back_kernel,
-        2,
-        [bf16(CHAN, 6, channels, CHAN * channels), bf16(flat, 512), bf16(flat, 512)],
-        [anywhere, vmem, vmem],
-        [
-            vmem((LAT, 64, 128), jnp.bfloat16),
-            vmem((LAT, 9, ROWS, 128), jnp.bfloat16),
-            vmem((LAT, 9, ROWS, 128), jnp.bfloat16),
-        ]
-        + work
-        + [pltpu.SemaphoreType.DMA] * 2
-        + link_sems([LAT, CHAN]),
-        [anywhere, anywhere, vmem],
-        [reply, grad, far],
     )
     grad_mixing = jnp.sum(grad_parts.astype(jnp.float32), axis=0)
 

time: 170 us -> 169 us (level)
  the two profiles are of different devices: /device:TPU:25 before, /device:TPU:9 now
where the time goes in v4:
time: 169 us
  Pallas kernels  147 us (87%)
  matrix products  14.5 us (9%)
  other arithmetic  4.97 us (3%)
  local copies, waits for them, and re-layouts  1.83 us (1%)
    pallas_call x1, Pallas kernels, linked(): pl.pallas_call(kernel, out_shape=shapes, in_specs=[spec(space) for space...  147 us
    dot_general x4, matrix products, dot(): return jnp.einsum(spec, a, b, preferred_element_type=jnp.float32)  14.5 us

profile of v4, /device:TPU:9, one launch (start us, length us, event | category | flops | bytes accessed | tf_op | source)
XLA Modules:
  0.0 168.9 jit_solution(17619236296792520843)
XLA Ops:
  0.6 0.8 dynamic_slice.3
  1.4 0.7 convert_bitcast_fusion.1
  2.1 0.7 convert_bitcast_fusion
  2.7 0.1 pad.3.clone
  2.8 0.6 add_convert_fusion.2.order_ref
  3.4 0.1 copy.20
  3.5 0.1 copy.19
  3.6 0.8 copy.21
  4.4 0.7 maximum_maximum_fusion.info_ref
  5.0 1.4 add_exponential_fusion.sector_ref
  6.4 0.0 copy-start
  6.4 0.0 copy-start.5
  6.4 4.5 %fusion.source_ref = bf16[768,512]{1,0:T(8,128)(2,1)} fusion(bf16[768,1440]{1,0:T(8,128)(2,1)} %bitcast.20, bf16[1440,512]{1,0:T(8,128)(2,1)} %constant.30.clone), kind=kOutput, calls=%fused_computation.5 | convolution fusion | flops 1132855296 | bytes 4472832 | tf_op jit(solution)/shard_map/ik,kn->in/dot_general | solution.py:733
  10.9 0.0 copy-done
  10.9 0.0 copy-done.5
  10.9 2.3 %fusion.1.grad_ref = bf16[768,512]{1,0:T(8,128)(2,1)} fusion(bf16[768,1440]{1,0:T(8,128)(2,1)S(1)} %bitcast.23, bf16[1440,512]{1,0:T(8,128)(2,1)S(1)} %copy-done.5), kind=kOutput, calls=%fused_computation.6 | convolution fusion | flops 1132855296 | bytes 4472832 | tf_op jit(solution)/shard_map/ik,kn->in/dot_general | solution.py:733
  13.2 147.0 %shard_map.157 = (bf16[8,6,48,384]{3,2,1,0:T(8,128)(2,1)}, bf16[768,1440]{1,0:T(8,128)(2,1)}, bf16[768,1440]{1,0:T(8,128)(2,1)}, bf16[768,512]{1,0:T(8,128)(2,1)}, bf16[768,512]{1,0:T(8,128)(2,1)}) custom-call(bf16[768,512]{1,0:T(8,128)(2,1)} %fusion.source_ref, bf16[768,512]{1,0:T(8,128)(2,1)} %fusion.1.grad_ref, ...), custom_call_target="tpu_custom_call" | custom-call | tf_op jit(solution)/shard_map/pallas_call | solution.py:720
  160.1 0.0 copy-start.1
  160.2 0.0 copy-start.2
  160.2 0.0 copy-start.3
  160.2 0.0 copy-start.4
  160.2 4.9 %add_convert_fusion.1 = bf16[768,1440]{1,0:T(8,128)(2,1)} fusion(bf16[768,1440]{1,0:T(8,128)(2,1)} %get-tuple-element.9, bf16[768,512]{1,0:T(8,128)(2,1)} %get-tuple-element.8, bf16[1440,512]{1,0:T(8,128)(2,1)S(1)} %copy-done.5), kind=kOutput, calls=%fused_computation.1 | convolution fusion | flops 1135779840 | bytes 6684672 | tf_op jit(solution)/shard_map/ik,nk->in/dot_general | solution.py:733
  165.1 0.0 copy-done.1
  165.1 1.0 convert_reduce_fusion
  166.1 0.0 copy-done.2
  166.1 0.0 copy-done.3
  166.1 0.0 copy-done.4
  166.1 2.8 %add_convert_fusion = bf16[768,1440]{1,0:T(8,128)(2,1)} fusion(bf16[768,1440]{1,0:T(8,128)(2,1)S(1)} %copy-done.2, bf16[768,512]{1,0:T(8,128)(2,1)S(1)} %copy-done.3, bf16[1440,512]{1,0:T(8,128)(2,1)S(1)} %copy-done.4), kind=kOutput, calls=%fused_computation | convolution fusion | flops 1135779840 | bytes 6684672 | tf_op jit(solution)/shard_map/ik,nk->in/dot_general | solution.py:733
  (2 shorter events, 0.0 us)
Async XLA Ops:
  6.4 4.5 %copy-start = (bf16[48,16,1440]{2,1,0:T(8,128)(2,1)S(1)}, bf16[48,16,1440]{2,1,0:T(8,128)(2,1)}, u32[]{:S(2)}) copy-start(bf16[48,16,1440]{2,1,0:T(8,128)(2,1)} %param.19) | copy-start | bytes 6635524
  6.4 4.5 %copy-start.5 = (bf16[1440,512]{1,0:T(8,128)(2,1)S(1)}, bf16[1440,512]{1,0:T(8,128)(2,1)}, u32[]{:S(2)}) copy-start(bf16[1440,512]{1,0:T(8,128)(2,1)} %constant.31.clone) | copy-start | bytes 4423684
  160.1 4.9 %copy-start.1 = (bf16[8,6,48,384]{3,2,1,0:T(8,128)(2,1)S(1)}, bf16[8,6,48,384]{3,2,1,0:T(8,128)(2,1)}, u32[]{:S(2)}) copy-start(bf16[8,6,48,384]{3,2,1,0:T(8,128)(2,1)} %get-tuple-element.12) | copy-start | bytes 5308420
  160.2 5.9 %copy-start.2 = (bf16[768,1440]{1,0:T(8,128)(2,1)S(1)}, bf16[768,1440]{1,0:T(8,128)(2,1)}, u32[]{:S(2)}) copy-start(bf16[768,1440]{1,0:T(8,128)(2,1)} %get-tuple-element.11) | copy-start | bytes 6635524
  160.2 5.9 %copy-start.3 = (bf16[768,512]{1,0:T(8,128)(2,1)S(1)}, bf16[768,512]{1,0:T(8,128)(2,1)}, u32[]{:S(2)}) copy-start(bf16[768,512]{1,0:T(8,128)(2,1)} %get-tuple-element.10) | copy-start | bytes 2359300
  160.2 5.9 %copy-start.4 = (bf16[1440,512]{1,0:T(8,128)(2,1)S(1)}, bf16[1440,512]{1,0:T(8,128)(2,1)}, u32[]{:S(2)}) copy-start(bf16[1440,512]{1,0:T(8,128)(2,1)} %constant.30.clone) | copy-start | bytes 4423684

commit v5 on v4

--- a/solution.py
+++ b/solution.py
@@ -38,11 +38,12 @@
     )
 
 
-def fourier_table():
+def fourier_table(shift):
     phase = 2.0 * math.pi / NLON * (np.outer(np.arange(NLON), np.arange(MMAX)) % NLON)
     table = np.zeros((NLON, 2, 256))
-    table[:, 0, :MMAX] = np.cos(phase)
-    table[:, 1, :MMAX] = -np.sin(phase)
+    places = np.concatenate([np.arange(128), np.arange(128, MMAX) + shift])
+    table[:, 0, places] = np.cos(phase)
+    table[:, 1, places] = -np.sin(phase)
     return table.reshape(NLON, 512)
 
 
@@ -102,20 +103,35 @@
     return tiles
 
 
-def spread_kernel(source_ref, grad_ref, out_ref, part, rows, link):
-    for f, ref in ((0, source_ref), (1, grad_ref)):
-        for k in range(4):
-            part[k] = ref[:, 128 * k : 128 * k + 128].astype(jnp.float32)
-
-        def turn(i, carry):
-            for half, count in ((0, 128), (1, 64)):
-                a = part[half, pl.ds(i, 48, stride=16), :]
-                b = part[2 + half, pl.ds(i, 48, stride=16), :]
-                block = jnp.concatenate([a, b, a[:32]], axis=0).T
-                rows[f, pl.ds(half * 2048 + i, count, stride=16), :] = block[:count]
+def spread_kernel(fields, tables, loads, out_ref, part, rows, link):
+    for f in range(2):
+        loads[f].wait()
+
+        def transform(b, carry):
+            block = pl.ds(pl.multiple_of(b * 256, 256), 256)
+            panel = dense(fields[f, block, :], tables[f][...])
+            part[2 * f, block, :] = panel[:, :128]
+            part[2 * f + 1, block, :] = panel[:, 256:384]
+            for r in range(2):
+                half = panel[:, 256 * r + 128 : 256 * r + 256]
+                part[4 + r, block, :] = half if f == 0 else part[4 + r, block, :] + half
             return carry
 
-        lax.fori_loop(0, ROWS, turn, 0)
+        lax.fori_loop(0, 3, transform, 0)
+
+    def turn(i, carry):
+        for k in range(3):
+            a = part[2 * k, pl.ds(i, 48, stride=16), :]
+            b = part[2 * k + 1, pl.ds(i, 48, stride=16), :]
+            block = jnp.concatenate([a, b, a[:32]], axis=0).T
+            if k < 2:
+                rows[k, pl.ds(i, 128, stride=16), :] = block
+            else:
+                rows[0, pl.ds(2048 + i, 64, stride=16), :] = block[:64]
+                rows[1, pl.ds(2048 + i, 64, stride=16), :] = block[64:]
+        return carry
+
+    lax.fori_loop(0, ROWS, turn, 0)
 
     def send(step, carry):
         d = wrap(link.lat + step, LAT)
@@ -146,26 +162,33 @@
         return carry
 
     lax.fori_loop(0, LAT, receive, 0)
-    for f, ref in ((0, source_ref), (1, grad_ref)):
-
-        def turn(i, carry):
-            block = rows[f, pl.ds(i, MMAX, stride=16), :]
-            halves = (block[:128], jnp.concatenate([block[128:], jnp.zeros((64, 128), jnp.float32)], axis=0))
-            for half in range(2):
-                flat = halves[half].T
-                part[half, pl.ds(i, 48, stride=16), :] = flat[:48]
-                part[2 + half, pl.ds(i, 48, stride=16), :] = flat[48:96]
-            return carry
-
-        lax.fori_loop(0, ROWS, turn, 0)
-        for k in range(4):
-            ref[:, 128 * k : 128 * k + 128] = part[k].astype(jnp.bfloat16)
-
-
-def recurrence(order_ref, cosine_ref, sector_ref, table):
-    order = jnp.broadcast_to(order_ref[...], (8, NLAT))
+
+    def turn(i, carry):
+        first = rows[0, pl.ds(i, MMAX, stride=16), :]
+        second = rows[1, pl.ds(i, MMAX, stride=16), :]
+        blocks = (
+            first[:128], second[:128], jnp.concatenate([first[128:], second[128:]], axis=0)
+        )
+        for k in range(3):
+            flat = blocks[k].T
+            part[2 * k, pl.ds(i, 48, stride=16), :] = flat[:48]
+            part[2 * k + 1, pl.ds(i, 48, stride=16), :] = flat[48:96]
+        return carry
+
+    lax.fori_loop(0, ROWS, turn, 0)
+    for r in range(2):
+        low = 256 * r
+        half = part[4 + r, :768, :].astype(jnp.bfloat16)
+        for f, ref in ((0, source_ref), (1, grad_ref)):
+            ref[:, low : low + 128] = part[2 * f + r, :768, :].astype(jnp.bfloat16)
+            ref[:, low + 128 : low + 256] = half
+
+
+def recurrence(norm_ref, cosine_ref, log_sine_ref, table):
+    lat = lax.axis_index("lat")
+    order = (iota((8, NLAT), 0) + lat * MODES).astype(jnp.float32)
     cosine = jnp.broadcast_to(cosine_ref[...], (8, NLAT))
-    sector = sector_ref[...]
+    sector = jnp.exp(norm_ref[lat][:, 0:1] + order * jnp.broadcast_to(log_sine_ref[...], (8, NLAT)))
     order_sq = order * order
     table[...] = jnp.zeros_like(table)
 
@@ -298,15 +321,22 @@
 
 def legendre_inputs():
     theta = math.pi * (np.arange(NLAT, dtype=np.float64) + 0.5) / NLAT
-    cosine = np.cos(theta).astype(np.float32)[None, :]
     sine = np.sin(theta)
-    orders = lax.axis_index("lat") * MODES + jnp.arange(8, dtype=jnp.int32)
-    norm = jnp.asarray(np.concatenate([log_norms(), np.zeros(2, np.float32)]))
-    order = orders.astype(jnp.float32)[:, None]
-    own = lax.dynamic_slice(norm, (lax.axis_index("lat") * MODES,), (8,))
-    sector = jnp.exp(own[:, None] + order * jnp.asarray(np.log(sine).astype(np.float32))[None, :])
-    quadrature = (math.sqrt(NLAT) * math.pi / NLAT * sine).astype(np.float32)[None, :]
-    return order, jnp.asarray(cosine), sector, jnp.asarray(quadrature)
+    norm = np.zeros((LAT, 8, 128), np.float32)
+    norm[:, :MODES] = log_norms().reshape(LAT, MODES, 1)
+    quadrature = math.sqrt(NLAT) * math.pi / NLAT * sine
+    flat = [np.cos(theta), np.log(sine), quadrature]
+    return [jnp.asarray(norm)] + [jnp.asarray(x.astype(np.float32)[None, :]) for x in flat]
+
+
+def band_info(start_ref, width_ref, coef_ref, out_ref):
+    row, lane = iota((ROWS, 128), 0), iota((ROWS, 128), 1)
+    coef = coef_ref[...].astype(jnp.float32)
+    total = pltpu.roll(jnp.concatenate([coef, jnp.zeros((ROWS, 124), jnp.float32)], axis=1), 2, 1)
+    for i in range(ROWS):
+        total = jnp.where((row == i) & (lane == 0), start_ref[i].astype(jnp.float32), total)
+        total = jnp.where((row == i) & (lane == 1), width_ref[i].astype(jnp.float32), total)
+    out_ref[...] = total.astype(jnp.bfloat16)
 
 
 def wrap(value, size):
@@ -578,7 +608,7 @@
 def edge_rows(f, field, part, out_ref):
     for k, (low, size) in enumerate(CHUNKS):
         slot = k % 4
-        part[slot, :, :size] = field[:, low : low + size].astype(jnp.float32)
+        part[slot, :768, :size] = field[:, low : low + size].astype(jnp.float32)
         for r, i in enumerate(EDGES):
             row = part[slot, pl.ds(i, 48, stride=16), :]
             out_ref[r // 2, f, r % 2, :, low : low + size] = row[:, :size].astype(jnp.bfloat16)
@@ -640,10 +670,10 @@
 
 
 def block_kernel(
-    source_ref, grad_ref, info_ref, weight_ref, source_hbm, grad_hbm,
-    order_ref, cosine_ref, sector_ref, quad_ref, pick_ref, pick_t_ref,
+    start_ref, width_ref, coef_ref, weight_ref, source_hbm, grad_hbm, lon_first, lon_second,
+    norm_ref, cosine_ref, log_sine_ref, quad_ref, pick_ref, pick_t_ref,
     parts_ref, ahead_ref, behind_ref, forward_ref, backward_ref,
-    part, rows, table, near, far, message, landing, bands, spectral, received,
+    part, rows, table, near, far, message, landing, info_ref, bands, spectral, received,
     weights, wide, before, after, reply, grads, answers, grids,
     fields, sums, edges, rim, field_sem, sum_sem, edge_send, edge_recv,
     info_send, info_recv, panel_send, panel_recv, grid_send, grid_recv, *sems
@@ -666,15 +696,15 @@
     ]
     for load in loads:
         load.start()
+    band_info(start_ref, width_ref, coef_ref, info_ref)
     meet([panels, degrees, replies, side])
     info.start_all()
     side.start()
-    spread_kernel(source_ref, grad_ref, message, part, rows, panels)
+    spread_kernel(fields, (lon_first, lon_second), loads, message, part, rows, panels)
     for f in range(2):
-        loads[f].wait()
         edge_rows(f, fields.at[f], part, edges)
     halo.start()
-    recurrence(order_ref, cosine_ref, sector_ref, table)
+    recurrence(norm_ref, cosine_ref, log_sine_ref, table)
     info.arrive()
     finish_tables(quad_ref, bands, near, far, table)
     halo.arrive()
@@ -735,20 +765,12 @@
 
 def per_device(source_field, band_start, band_width, band_coef, mixing_weight, output_grad):
     channels = source_field.shape[0]
-    table = fourier_table()
-    lon_analysis = jnp.asarray((table / math.sqrt(NLON)).astype(jnp.bfloat16))
-    lon_synthesis = jnp.asarray((table / math.sqrt(MMAX)).astype(jnp.bfloat16))
+    plain, moved = fourier_table(0), fourier_table(64)
+    scales = (1.0 / math.sqrt(NLON), 1.0 / math.sqrt(MMAX))
+    analysis, moved_analysis = [jnp.asarray((x * scales[0]).astype(jnp.bfloat16)) for x in (plain, moved)]
+    synthesis, moved_synthesis = [jnp.asarray((x * scales[1]).astype(jnp.bfloat16)) for x in (plain, moved)]
     flat = channels * ROWS
 
-    info = jnp.concatenate(
-        [
-            band_start.astype(jnp.bfloat16)[:, None],
-            band_width.astype(jnp.bfloat16)[:, None],
-            band_coef,
-            jnp.zeros((ROWS, 122), jnp.bfloat16),
-        ],
-        axis=1,
-    )
     vmem, anywhere = pltpu.VMEM, pl.ANY
     pick = np.zeros((CHAN, channels, CHAN, 64), np.float32)
     for e in range(CHAN):
@@ -773,20 +795,21 @@
         ],
         [anywhere] * 3 + [vmem] * 2,
         [
-            panel(4, flat, 128),
-            panel(2, MMAX * ROWS, 128),
-            panel(4, 2048, 128),
+            panel(6, flat + 16, 128),
+            panel(2, MMAX * ROWS + 16, 128),
+            panel(4, 2048 + 256, 128),
             held(12, 256, NLAT),
             held(12, NLAT, 256),
             held(LAT, 9, ROWS, 128),
             held(LAT, 9, ROWS, 128),
+            held(ROWS, 128),
             held(LAT, ROWS, 128),
             held(LAT, 64, 128),
             held(LAT, 64, 128),
             held(CHAN, 6, channels, CHAN * channels),
             held(6, 512, 512),
-            panel(2, CHAN, 192, 128),
-            panel(2, CHAN, 192, 128),
+            panel(2, CHAN, 192 + 8, 128),
+            panel(2, CHAN, 192 + 8, 128),
             held(LAT, 64, 128),
             held(CHAN, 6, channels, CHAN * channels),
             held(LAT, 64, 128),
@@ -799,14 +822,16 @@
         + [pltpu.SemaphoreType.DMA((2,))] * 4
         + [pltpu.SemaphoreType.DMA] * 6
         + link_sems([LAT, LAT, CHAN, CHAN]),
-        [vmem, vmem, vmem] + [anywhere] * 3 + [vmem] * 6,
+        [pltpu.SMEM] * 2 + [vmem] + [anywhere] * 3 + [vmem] * 8,
         [
-            dot("ik,kn->in", source_field.reshape(flat, NLON), lon_analysis).astype(jnp.bfloat16),
-            dot("ik,kn->in", output_grad.reshape(flat, NLON), lon_synthesis).astype(jnp.bfloat16),
-            info,
+            band_start,
+            band_width,
+            band_coef,
             mixing_weight,
             source_field.reshape(flat, NLON),
             output_grad.reshape(flat, NLON),
+            analysis,
+            moved_synthesis,
             *legendre_inputs(),
             jnp.asarray(pick.astype(jnp.bfloat16)),
             jnp.asarray(pick.T.astype(jnp.bfloat16)),
@@ -815,8 +840,8 @@
     grad_mixing = jnp.sum(grad_parts.astype(jnp.float32), axis=0)
 
     shape = (channels, ROWS, NLON)
-    mixed_field = dot("ik,nk->in", forward, lon_synthesis) + ahead.astype(jnp.float32)
-    grad_input = dot("ik,nk->in", backward, lon_analysis) + behind.astype(jnp.float32)
+    mixed_field = dot("ik,nk->in", forward, synthesis) + ahead.astype(jnp.float32)
+    grad_input = dot("ik,nk->in", backward, moved_analysis) + behind.astype(jnp.float32)
     return (
         mixed_field.astype(jnp.bfloat16).reshape(shape),
         grad_input.astype(jnp.bfloat16).reshape(shape),

time: 169 us -> 154 us (0.911)
  matrix products: 14.5 us -> 7.71 us
  Pallas kernels: 147 us -> 143 us
  other arithmetic: 4.97 us -> 1 us
    dot_general x4 -> x2, matrix products: 14.5 us -> 7.71 us  [dot(): return jnp.einsum(spec, a, b, preferred_element_type=jnp.float32)]
    pallas_call x1, Pallas kernels: 147 us -> 143 us  [linked(): pl.pallas_call(kernel, out_shape=shapes, in_specs=[spec(space) for space...]
where the time goes in v5:
time: 154 us; the launch traced here: 153 us
  Pallas kernels  143 us (93%)
  matrix products  7.71 us (5%)
    pallas_call x1, Pallas kernels, linked(): pl.pallas_call(kernel, out_shape=shapes, in_specs=[spec(space) for space...  143 us
    dot_general x2, matrix products, dot(): return jnp.einsum(spec, a, b, preferred_element_type=jnp.float32)  7.71 us

profile of v5, /device:TPU:9, one launch (start us, length us, event | category | flops | bytes accessed | tf_op | source)
XLA Modules:
  0.0 153.4 jit_solution(8750978468203812500)
XLA Ops:
  0.6 1.4 copy.19.coef_ref
  2.0 0.0 copy-start.4
  2.0 142.7 %shard_map.175 = (bf16[8,6,48,384]{3,2,1,0:T(8,128)(2,1)}, bf16[768,1440]{1,0:T(8,128)(2,1)}, bf16[768,1440]{1,0:T(8,128)(2,1)}, bf16[768,512]{1,0:T(8,128)(2,1)}, bf16[768,512]{1,0:T(8,128)(2,1)}) custom-call(s32[16]{0:T(128)} %start_ref.1, s32[16]{0:T(128)} %width_ref.1, bf16[16,4]{1,0:T(8,128)(2,1)} %copy.19.coef_ref, bf16[6,48,384]{2,1,0:T(8,128)(2,1)} %weight_ref.1, ...), custom_call_target="tpu_custom_call" | custom-call | tf_op jit(solution)/shard_map/pallas_call | solution.py:750
  144.7 0.0 copy-done.4
  144.7 0.0 copy-start
  144.7 0.0 copy-start.1
  144.7 0.0 copy-start.2
  144.7 0.0 copy-start.3
  144.7 4.9 %add_convert_fusion.1 = bf16[768,1440]{1,0:T(8,128)(2,1)} fusion(bf16[768,1440]{1,0:T(8,128)(2,1)} %get-tuple-element.9, bf16[768,512]{1,0:T(8,128)(2,1)} %get-tuple-element.8, bf16[1440,512]{1,0:T(8,128)(2,1)S(1)} %copy-done.4), kind=kOutput, calls=%fused_computation.1 | convolution fusion | flops 1135779840 | bytes 6684672 | tf_op jit(solution)/shard_map/ik,nk->in/dot_general | solution.py:763
  149.6 0.0 copy-done
  149.6 1.0 convert_reduce_fusion
  150.6 0.0 copy-done.1
  150.6 0.0 copy-done.2
  150.6 0.0 copy-done.3
  150.6 2.8 %add_convert_fusion = bf16[768,1440]{1,0:T(8,128)(2,1)} fusion(bf16[768,1440]{1,0:T(8,128)(2,1)S(1)} %copy-done.1, bf16[768,512]{1,0:T(8,128)(2,1)S(1)} %copy-done.2, bf16[1440,512]{1,0:T(8,128)(2,1)S(1)} %copy-done.3), kind=kOutput, calls=%fused_computation | convolution fusion | flops 1135779840 | bytes 6684672 | tf_op jit(solution)/shard_map/ik,nk->in/dot_general | solution.py:763
Async XLA Ops:
  2.0 142.7 %copy-start.4 = (bf16[1440,512]{1,0:T(8,128)(2,1)S(1)}, bf16[1440,512]{1,0:T(8,128)(2,1)}, u32[]{:S(2)}) copy-start(bf16[1440,512]{1,0:T(8,128)(2,1)} %constant.24.clone) | copy-start | bytes 4423684
  144.7 4.9 %copy-start = (bf16[8,6,48,384]{3,2,1,0:T(8,128)(2,1)S(1)}, bf16[8,6,48,384]{3,2,1,0:T(8,128)(2,1)}, u32[]{:S(2)}) copy-start(bf16[8,6,48,384]{3,2,1,0:T(8,128)(2,1)} %get-tuple-element.12) | copy-start | bytes 5308420
  144.7 5.9 %copy-start.1 = (bf16[768,1440]{1,0:T(8,128)(2,1)S(1)}, bf16[768,1440]{1,0:T(8,128)(2,1)}, u32[]{:S(2)}) copy-start(bf16[768,1440]{1,0:T(8,128)(2,1)} %get-tuple-element.11) | copy-start | bytes 6635524
  144.7 5.9 %copy-start.2 = (bf16[768,512]{1,0:T(8,128)(2,1)S(1)}, bf16[768,512]{1,0:T(8,128)(2,1)}, u32[]{:S(2)}) copy-start(bf16[768,512]{1,0:T(8,128)(2,1)} %get-tuple-element.10) | copy-start | bytes 2359300
  144.7 5.9 %copy-start.3 = (bf16[1440,512]{1,0:T(8,128)(2,1)S(1)}, bf16[1440,512]{1,0:T(8,128)(2,1)}, u32[]{:S(2)}) copy-start(bf16[1440,512]{1,0:T(8,128)(2,1)} %constant.23.clone) | copy-start | bytes 4423684

commit v6 on v5

--- a/solution.py
+++ b/solution.py
@@ -103,7 +103,7 @@
     return tiles
 
 
-def spread_kernel(fields, tables, loads, out_ref, part, rows, link):
+def transform_kernel(fields, tables, loads, part):
     for f in range(2):
         loads[f].wait()
 
@@ -119,6 +119,8 @@
 
         lax.fori_loop(0, 3, transform, 0)
 
+
+def spread_kernel(out_ref, part, rows, link):
     def turn(i, carry):
         for k in range(3):
             a = part[2 * k, pl.ds(i, 48, stride=16), :]
@@ -151,8 +153,9 @@
     lax.fori_loop(0, LAT, send, 0)
 
 
-def gather_kernel(in_ref, source_ref, grad_ref, part, rows):
-    def receive(d, carry):
+def gather_kernel(in_ref, source_ref, grad_ref, part, rows, link):
+    def receive(step, carry):
+        d = link.arrive_one(step)
         tiles = [in_ref[d, k].astype(jnp.float32) for k in range(9)]
         units = split_lanes(tiles)
         for u in range(12):
@@ -315,6 +318,19 @@
     store_rows(out_ref, merge_rows(packed))
 
 
+def tail_kernel(
+    forward_ref, backward_ref, ahead_ref, behind_ref, first_ref, second_ref, parts_ref,
+    mixed_ref, input_ref, grad_ref
+):
+    for panel, table, extra, out in (
+        (forward_ref, first_ref, ahead_ref, mixed_ref),
+        (backward_ref, second_ref, behind_ref, input_ref),
+    ):
+        value = dense(panel[...], table[...]) + extra[...].astype(jnp.float32)
+        out[...] = value.astype(jnp.bfloat16).reshape(out.shape)
+    grad_ref[0] = jnp.sum(parts_ref[:, 0].astype(jnp.float32), axis=0)
+
+
 def bf16(*shape):
     return jax.ShapeDtypeStruct(shape, jnp.bfloat16)
 
@@ -433,19 +449,23 @@
 
         lax.fori_loop(0, LAT, step_fn, 0)
 
+    def arrive_one(self, step):
+        target = self.sends(step, self.lat, self.chan)
+        source = self.receives(step, self.lat, self.chan)
+
+        @pl.when(self.own(target))
+        def _():
+            self.local(target).wait()
+
+        @pl.when(self.far(source))
+        def _():
+            self.remote(source, source[2]).wait_recv()
+
+        return source[2]
+
     def arrive(self):
         def step_fn(step, carry):
-            target = self.sends(step, self.lat, self.chan)
-            source = self.receives(step, self.lat, self.chan)
-
-            @pl.when(self.own(target))
-            def _():
-                self.local(target).wait()
-
-            @pl.when(self.far(source))
-            def _():
-                self.remote(source, source[2]).wait_recv()
-
+            self.arrive_one(step)
             return carry
 
         lax.fori_loop(0, LAT, step_fn, 0)
@@ -666,7 +686,7 @@
     total = jnp.int32(0)
     for link in links:
         total = link.greet(barrier, total)
-    pl.semaphore_wait(barrier, total)
+    return lambda: pl.semaphore_wait(barrier, total)
 
 
 def block_kernel(
@@ -676,10 +696,10 @@
     part, rows, table, near, far, message, landing, info_ref, bands, spectral, received,
     weights, wide, before, after, reply, grads, answers, grids,
     fields, sums, edges, rim, field_sem, sum_sem, edge_send, edge_recv,
-    info_send, info_recv, panel_send, panel_recv, grid_send, grid_recv, *sems
+    info_send, info_recv, panel_send, panel_recv, *sems
 ):
     panels = Bulk(lat_to, lat_from, False, message, landing, (panel_send, panel_recv, None))
-    grid_panels = Bulk(lat_to, lat_from, False, message, grids, (grid_send, grid_recv, None))
+    grid_panels = Wire(lat_to, lat_from, False, message, grids, sems[12:15])
     degrees = Wire(spectral_to, spectral_from, True, spectral, received, sems[0:3])
     replies = Wire(spectral_from, degree_owner, True, reply, answers, sems[3:6])
     info = Whole(whole_to, whole_from, False, info_ref, bands, (info_send, info_recv, None))
@@ -697,20 +717,18 @@
     for load in loads:
         load.start()
     band_info(start_ref, width_ref, coef_ref, info_ref)
-    meet([panels, degrees, replies, side])
+    met = meet([panels, degrees, replies, side])
+    transform_kernel(fields, (lon_first, lon_second), loads, part)
+    met()
     info.start_all()
     side.start()
-    spread_kernel(fields, (lon_first, lon_second), loads, message, part, rows, panels)
+    spread_kernel(message, part, rows, panels)
     for f in range(2):
         edge_rows(f, fields.at[f], part, edges)
     halo.start()
     recurrence(norm_ref, cosine_ref, log_sine_ref, table)
     info.arrive()
     finish_tables(quad_ref, bands, near, far, table)
-    halo.arrive()
-    residuals([fields.at[0], fields.at[1]], rim, bands, [sums.at[0], sums.at[1]])
-    for store in stores:
-        store.start()
     panels.arrive()
     analysis_kernel(landing, near, spectral)
     degrees.start_all()
@@ -727,9 +745,12 @@
     synthesis_kernel(answers, far, message)
     grid_panels.start_all()
     grad_side.start()
+    halo.arrive()
+    residuals([fields.at[0], fields.at[1]], rim, bands, [sums.at[0], sums.at[1]])
+    for store in stores:
+        store.start()
     replies.leave()
-    grid_panels.arrive()
-    gather_kernel(grids, forward_ref, backward_ref, part, rows)
+    gather_kernel(grids, forward_ref, backward_ref, part, rows, grid_panels)
     grid_panels.leave()
     grad_side.finish()
     for store in stores:
@@ -767,8 +788,12 @@
     channels = source_field.shape[0]
     plain, moved = fourier_table(0), fourier_table(64)
     scales = (1.0 / math.sqrt(NLON), 1.0 / math.sqrt(MMAX))
-    analysis, moved_analysis = [jnp.asarray((x * scales[0]).astype(jnp.bfloat16)) for x in (plain, moved)]
-    synthesis, moved_synthesis = [jnp.asarray((x * scales[1]).astype(jnp.bfloat16)) for x in (plain, moved)]
+    analysis, moved_analysis, synthesis, moved_synthesis = [
+        jnp.asarray((x * scale).astype(jnp.bfloat16))
+        for x, scale in (
+            (plain, scales[0]), (moved.T, scales[0]), (plain.T, scales[1]), (moved, scales[1])
+        )
+    ]
     flat = channels * ROWS
 
     vmem, anywhere = pltpu.VMEM, pl.ANY
@@ -820,8 +845,8 @@
             held(2, 2, 2, channels, NLON),
         ]
         + [pltpu.SemaphoreType.DMA((2,))] * 4
-        + [pltpu.SemaphoreType.DMA] * 6
-        + link_sems([LAT, LAT, CHAN, CHAN]),
+        + [pltpu.SemaphoreType.DMA] * 4
+        + link_sems([LAT, LAT, CHAN, CHAN, LAT]),
         [pltpu.SMEM] * 2 + [vmem] + [anywhere] * 3 + [vmem] * 8,
         [
             band_start,
@@ -837,16 +862,28 @@
             jnp.asarray(pick.T.astype(jnp.bfloat16)),
         ],
     )
-    grad_mixing = jnp.sum(grad_parts.astype(jnp.float32), axis=0)
-
-    shape = (channels, ROWS, NLON)
-    mixed_field = dot("ik,nk->in", forward, synthesis) + ahead.astype(jnp.float32)
-    grad_input = dot("ik,nk->in", backward, moved_analysis) + behind.astype(jnp.float32)
-    return (
-        mixed_field.astype(jnp.bfloat16).reshape(shape),
-        grad_input.astype(jnp.bfloat16).reshape(shape),
-        grad_mixing,
-    )
+    def rowwise(*block):
+        return pl.BlockSpec(block, lambda i: (i,) + (0,) * (len(block) - 1))
+
+    def fixed(*block):
+        return pl.BlockSpec(block, lambda i: (0, 0))
+
+    return pl.pallas_call(
+        tail_kernel,
+        grid=(6,),
+        out_shape=[
+            bf16(channels, ROWS, NLON),
+            bf16(channels, ROWS, NLON),
+            jax.ShapeDtypeStruct((6, channels, CHAN * channels), jnp.float32),
+        ],
+        in_specs=[rowwise(flat // 6, 512)] * 2
+        + [rowwise(flat // 6, NLON)] * 2
+        + [fixed(512, NLON)] * 2
+        + [pl.BlockSpec((CHAN, 1, channels, CHAN * channels), lambda i: (0, i, 0, 0))],
+        out_specs=[rowwise(channels // 6, ROWS, NLON)] * 2
+        + [rowwise(1, channels, CHAN * channels)],
+        compiler_params=pltpu.CompilerParams(vmem_limit_bytes=VMEM_LIMIT),
+    )(forward, backward, ahead, behind, synthesis, moved_analysis, grad_parts)
 
 
 def solution(mesh):

time: 154 us -> 142 us (0.922)
  the two profiles are of different devices: /device:TPU:9 before, /device:TPU:1 now
where the time goes in v6:
time: 142 us
  Pallas kernels  140 us (99%)
    pallas_call x1, Pallas kernels, linked(): pl.pallas_call(kernel, out_shape=shapes, in_specs=[spec(space) for space...  130 us
    pallas_call x1, Pallas kernels, per_device(): pl.pallas_call(tail_kernel, grid=(6,), out_shape=[bf16(channels, ROWS, NL...  9.18 us

profile of v6, /device:TPU:1, one launch (start us, length us, event | category | flops | bytes accessed | tf_op | source)
XLA Modules:
  0.0 141.6 jit_solution(5900813433909758706)
XLA Ops:
  0.6 1.4 copy.19.coef_ref
  2.0 130.4 %shard_map.175 = (bf16[8,6,48,384]{3,2,1,0:T(8,128)(2,1)}, bf16[768,1440]{1,0:T(8,128)(2,1)}, bf16[768,1440]{1,0:T(8,128)(2,1)}, bf16[768,512]{1,0:T(8,128)(2,1)}, bf16[768,512]{1,0:T(8,128)(2,1)}) custom-call(s32[16]{0:T(128)} %start_ref.1, s32[16]{0:T(128)} %width_ref.1, bf16[16,4]{1,0:T(8,128)(2,1)} %copy.19.coef_ref, bf16[6,48,384]{2,1,0:T(8,128)(2,1)} %weight_ref.1, ...), custom_call_target="tpu_custom_call" | custom-call | tf_op jit(solution)/shard_map/pallas_call | solution.py:771
  132.4 9.2 %shard_map.176 = (bf16[48,16,1440]{2,1,0:T(8,128)(2,1)}, bf16[48,16,1440]{2,1,0:T(8,128)(2,1)}, f32[6,48,384]{2,1,0:T(8,128)}) custom-call(bf16[768,512]{1,0:T(8,128)(2,1)} %get-tuple-element.8.forward_ref, bf16[768,512]{1,0:T(8,128)(2,1)} %get-tuple-element.9.backward_ref, bf16[768,1440]{1,0:T(8,128)(2,1)} %get-tuple-element.10.ahead_ref, ...), custom_call_target="tpu_custom_call" | custom-call | tf_op jit(solution)/shard_map/pallas_call | solution.py:871

commit v7 on v6

--- a/solution.py
+++ b/solution.py
@@ -328,7 +328,7 @@
     ):
         value = dense(panel[...], table[...]) + extra[...].astype(jnp.float32)
         out[...] = value.astype(jnp.bfloat16).reshape(out.shape)
-    grad_ref[0] = jnp.sum(parts_ref[:, 0].astype(jnp.float32), axis=0)
+    grad_ref[...] = jnp.sum(parts_ref[...].astype(jnp.float32), axis=0)
 
 
 def bf16(*shape):
@@ -364,23 +364,27 @@
     return other, chan, other, lat
 
 
-def spectral_to(step, lat, chan):
-    other = wrap(lat + step, LAT)
-    group = 2 * lax.rem(lat, 4) + lax.rem(lax.div(lat, 4), 2)
-    return other, group, other, chan * 4 + lax.div(lat, 8)
-
-
-def spectral_from(step, lat, chan):
-    part = lax.rem(step + lat, 4)
-    group = lax.rem(lax.div(step, 4) + chan, CHAN)
-    other = (2 * part + lax.rem(chan, 2)) * 4 + lax.div(chan, 2)
-    return other, group, group * 4 + part, lat
-
-
-def degree_owner(step, lat, chan):
-    other = wrap(lat + LAT - step, LAT)
-    group = 2 * lax.rem(lat, 4) + lax.rem(lax.div(lat, 4), 2)
-    return other, group, other, 0
+def spectral_maps():
+    lat, chan = lax.axis_index("lat"), lax.axis_index("chan")
+    low = lax.rem(lat, 4)
+    group = 2 * low + lax.rem(lax.div(lat, 4), 2)
+    slot = chan * 4 + lax.div(lat, 8)
+    base = lax.rem(chan, 2) * 4 + lax.div(chan, 2)
+
+    def spectral_to(step, lat, chan):
+        other = wrap(lat + step[0] * 4 + step[1], LAT)
+        return other, group, other, slot
+
+    def spectral_from(step, lat, chan):
+        part = wrap(low + step[1], 4)
+        near = wrap(chan + step[0], CHAN)
+        return part * 8 + base, near, near * 4 + part, lat
+
+    def degree_owner(step, lat, chan):
+        other = wrap(lat + LAT - step[0] * 4 - step[1], LAT)
+        return other, group, other, 0
+
+    return spectral_to, spectral_from, degree_owner
 
 
 class Wire:
@@ -390,6 +394,17 @@
         self.source, self.target = source, target
         self.send_sem, self.recv_sem, self.own_sem = sems
 
+    def each(self, body, carry):
+        if not self.skip:
+            return lax.fori_loop(0, LAT, body, carry)
+
+        def four(outer, carry):
+            for inner in range(4):
+                carry = body((outer, inner), carry)
+            return carry
+
+        return lax.fori_loop(0, LAT // 4, four, carry)
+
     def live(self, pair):
         if self.skip:
             return self.lat + pair[0] < LAT
@@ -414,7 +429,7 @@
 
             return count + jnp.where(self.far(self.sends(step, self.lat, self.chan)), 1, 0)
 
-        return lax.fori_loop(0, LAT, step_fn, total)
+        return self.each(step_fn, total)
 
     def remote(self, pair, slot):
         return pltpu.make_async_remote_copy(
@@ -447,7 +462,7 @@
             self.start(step)
             return carry
 
-        lax.fori_loop(0, LAT, step_fn, 0)
+        self.each(step_fn, 0)
 
     def arrive_one(self, step):
         target = self.sends(step, self.lat, self.chan)
@@ -468,7 +483,7 @@
             self.arrive_one(step)
             return carry
 
-        lax.fori_loop(0, LAT, step_fn, 0)
+        self.each(step_fn, 0)
 
     def leave(self):
         def step_fn(step, carry):
@@ -480,7 +495,7 @@
 
             return carry
 
-        lax.fori_loop(0, LAT, step_fn, 0)
+        self.each(step_fn, 0)
 
 
 class Side:
@@ -700,6 +715,7 @@
 ):
     panels = Bulk(lat_to, lat_from, False, message, landing, (panel_send, panel_recv, None))
     grid_panels = Wire(lat_to, lat_from, False, message, grids, sems[12:15])
+    spectral_to, spectral_from, degree_owner = spectral_maps()
     degrees = Wire(spectral_to, spectral_from, True, spectral, received, sems[0:3])
     replies = Wire(spectral_from, degree_owner, True, reply, answers, sems[3:6])
     info = Whole(whole_to, whole_from, False, info_ref, bands, (info_send, info_recv, None))
@@ -870,18 +886,18 @@
 
     return pl.pallas_call(
         tail_kernel,
-        grid=(6,),
+        grid=(3,),
         out_shape=[
             bf16(channels, ROWS, NLON),
             bf16(channels, ROWS, NLON),
             jax.ShapeDtypeStruct((6, channels, CHAN * channels), jnp.float32),
         ],
-        in_specs=[rowwise(flat // 6, 512)] * 2
-        + [rowwise(flat // 6, NLON)] * 2
+        in_specs=[rowwise(flat // 3, 512)] * 2
+        + [rowwise(flat // 3, NLON)] * 2
         + [fixed(512, NLON)] * 2
-        + [pl.BlockSpec((CHAN, 1, channels, CHAN * channels), lambda i: (0, i, 0, 0))],
-        out_specs=[rowwise(channels // 6, ROWS, NLON)] * 2
-        + [rowwise(1, channels, CHAN * channels)],
+        + [pl.BlockSpec((CHAN, 2, channels, CHAN * channels), lambda i: (0, i, 0, 0))],
+        out_specs=[rowwise(channels // 3, ROWS, NLON)] * 2
+        + [rowwise(2, channels, CHAN * channels)],
         compiler_params=pltpu.CompilerParams(vmem_limit_bytes=VMEM_LIMIT),
     )(forward, backward, ahead, behind, synthesis, moved_analysis, grad_parts)
 

time: 142 us -> 140 us (0.986)
  Pallas kernels: 140 us -> 138 us
where the time goes in v7:
time: 140 us
  Pallas kernels  138 us (99%)
    pallas_call x1, Pallas kernels, linked(): pl.pallas_call(kernel, out_shape=shapes, in_specs=[spec(space) for space...  130 us
    pallas_call x1, Pallas kernels, per_device(): pl.pallas_call(tail_kernel, grid=(3,), out_shape=[bf16(channels, ROWS, NL...  8.35 us

profile of v7, /device:TPU:1, one launch (start us, length us, event | category | flops | bytes accessed | tf_op | source)
XLA Modules:
  0.0 140.3 jit_solution(18274178156026511081)
XLA Ops:
  0.6 1.4 copy.19.coef_ref
  2.0 129.9 %shard_map.175 = (bf16[8,6,48,384]{3,2,1,0:T(8,128)(2,1)}, bf16[768,1440]{1,0:T(8,128)(2,1)}, bf16[768,1440]{1,0:T(8,128)(2,1)}, bf16[768,512]{1,0:T(8,128)(2,1)}, bf16[768,512]{1,0:T(8,128)(2,1)}) custom-call(s32[16]{0:T(128)} %start_ref.1, s32[16]{0:T(128)} %width_ref.1, bf16[16,4]{1,0:T(8,128)(2,1)} %copy.19.coef_ref, bf16[6,48,384]{2,1,0:T(8,128)(2,1)} %weight_ref.1, ...), custom_call_target="tpu_custom_call" | custom-call | tf_op jit(solution)/shard_map/pallas_call | solution.py:787
  131.9 8.4 %shard_map.176 = (bf16[48,16,1440]{2,1,0:T(8,128)(2,1)}, bf16[48,16,1440]{2,1,0:T(8,128)(2,1)}, f32[6,48,384]{2,1,0:T(8,128)}) custom-call(bf16[768,512]{1,0:T(8,128)(2,1)} %get-tuple-element.8.forward_ref, bf16[768,512]{1,0:T(8,128)(2,1)} %get-tuple-element.9.backward_ref, bf16[768,1440]{1,0:T(8,128)(2,1)} %get-tuple-element.10.ahead_ref, ...), custom_call_target="tpu_custom_call" | custom-call | tf_op jit(solution)/shard_map/pallas_call | solution.py:887

commit v8 on v7

--- a/solution.py
+++ b/solution.py
@@ -737,8 +737,8 @@
     transform_kernel(fields, (lon_first, lon_second), loads, part)
     met()
     info.start_all()
+    spread_kernel(message, part, rows, panels)
     side.start()
-    spread_kernel(message, part, rows, panels)
     for f in range(2):
         edge_rows(f, fields.at[f], part, edges)
     halo.start()

time: 140 us -> 142 us (1.014)
  no operation moved by 1% of the time
where the time goes in v8:
time: 142 us; the launch traced here: 141 us
  Pallas kernels  139 us (98%)
    pallas_call x1, Pallas kernels, linked(): pl.pallas_call(kernel, out_shape=shapes, in_specs=[spec(space) for space...  131 us
    pallas_call x1, Pallas kernels, per_device(): pl.pallas_call(tail_kernel, grid=(3,), out_shape=[bf16(channels, ROWS, NL...  8.35 us

profile of v8, /device:TPU:1, one launch (start us, length us, event | category | flops | bytes accessed | tf_op | source)
XLA Modules:
  0.0 141.5 jit_solution(4270935162417738071)
XLA Ops:
  0.6 1.4 copy.19.coef_ref
  2.0 131.1 %shard_map.175 = (bf16[8,6,48,384]{3,2,1,0:T(8,128)(2,1)}, bf16[768,1440]{1,0:T(8,128)(2,1)}, bf16[768,1440]{1,0:T(8,128)(2,1)}, bf16[768,512]{1,0:T(8,128)(2,1)}, bf16[768,512]{1,0:T(8,128)(2,1)}) custom-call(s32[16]{0:T(128)} %start_ref.1, s32[16]{0:T(128)} %width_ref.1, bf16[16,4]{1,0:T(8,128)(2,1)} %copy.19.coef_ref, bf16[6,48,384]{2,1,0:T(8,128)(2,1)} %weight_ref.1, ...), custom_call_target="tpu_custom_call" | custom-call | tf_op jit(solution)/shard_map/pallas_call | solution.py:787
  133.1 8.4 %shard_map.176 = (bf16[48,16,1440]{2,1,0:T(8,128)(2,1)}, bf16[48,16,1440]{2,1,0:T(8,128)(2,1)}, f32[6,48,384]{2,1,0:T(8,128)}) custom-call(bf16[768,512]{1,0:T(8,128)(2,1)} %get-tuple-element.8.forward_ref, bf16[768,512]{1,0:T(8,128)(2,1)} %get-tuple-element.9.backward_ref, bf16[768,1440]{1,0:T(8,128)(2,1)} %get-tuple-element.10.ahead_ref, ...), custom_call_target="tpu_custom_call" | custom-call | tf_op jit(solution)/shard_map/pallas_call | solution.py:887
